TPU v7x, 32 devices: a whole 2x2x4 slice. The times are simulated.
32 devices in a mesh: dp: 8 (over y, x, core), fsdp: 4 (over z).
Axes of the slice: x: 2, y: 2, z: 4, core: 2. Of those that a mesh axis runs over, the one named last changes fastest.
Arguments:
- fields: bfloat16 [8, 6, 48, 48, 48, 128], P('dp', None, 'fsdp'), may hold values from -6 to 6
- targets: bfloat16 [8, 6, 48, 2304], P('dp', None, 'fsdp'), may hold values from -6 to 6
- lists: int32 [8, 6], P('dp'), may hold values from 0 to 5, each once within a row
- counts: int32 [8], replicated, may hold values from 1 to 6, as said below
- spectral_w: bfloat16 [32, 2, 128, 128], P('fsdp'), may hold values from -0.375 to 0.375
- local_w: bfloat16 [128, 128], replicated, may hold values from -0.5 to 0.5
- proj: float32 [128], replicated, may hold values from -0.5 to 0.5
Outputs:
- grad_spectral: float32 [32, 2, 128, 128], P('fsdp')
- grad_local: float32 [128, 128], replicated
Inputs may be any that keep to these rules, and one draw needn't show every extreme that they name: Each row of lists names every slot of its lane once; the first counts[l] entries of row l are lane l's live grids. `counts`: exactly one lane has 6 live grids; every other lane has 1 or 2.
All inputs are finite; a program needn't handle non-finite values.
Results may differ from a plain program's by a relative error of at most 0.0036.
The roundings to bfloat16 on the way count: a program that leaves them out, or rounds other values in their place, can miss the bound.
Values may be sent and summed in bfloat16 or wider, within the bound.
No kernel may reach another device: no remote copies, remote signals or barrier semaphores. Data moves between devices by JAX's collectives and lax.ppermute only.
A program may use at most 128 MiB of HBM per device.

v0:
```python
import math

import jax
import jax.numpy as jnp
from jax import lax
from jax.sharding import PartitionSpec as P

MX = 4
MY = 4
MZ = 2


highest = lax.Precision.HIGHEST
root_half = 0.7071067811865476
inv_root_two_pi = 0.3989422804014327


def phase_table(mode_ids, cell_ids, length, direction):
    product = mode_ids[:, None] * cell_ids[None, :] % length
    angle = product.astype(jnp.float32) * (2.0 * math.pi / length)
    return (jnp.cos(angle), direction * jnp.sin(angle))


def mode_lists():
    kx_ids = jnp.arange(MX, dtype=jnp.int32) - MX // 2
    ky_ids = jnp.arange(MY, dtype=jnp.int32) - MY // 2
    kz_ids = jnp.arange(MZ, dtype=jnp.int32)
    return (kx_ids, ky_ids, kz_ids)


def complex_contract(real_part, imag_part, cos_t, sin_t, form):

    def product(left, right):
        return jnp.einsum(form, left, right, precision=highest)

    return (
        product(real_part, cos_t) - product(imag_part, sin_t),
        product(real_part, sin_t) + product(imag_part, cos_t),
    )


def forward_modes(grid_field, x_cells, scale):
    grid_len = grid_field.shape[1]
    kx_ids, ky_ids, kz_ids = mode_lists()
    cells = jnp.arange(grid_len, dtype=jnp.int32)
    cos_z, sin_z = phase_table(kz_ids, cells, grid_len, -1.0)
    part_re = jnp.einsum(
        "abzc,kz->abkc", grid_field, cos_z.astype(jnp.bfloat16), preferred_element_type=jnp.float32
    )
    part_im = jnp.einsum(
        "abzc,kz->abkc", grid_field, sin_z.astype(jnp.bfloat16), preferred_element_type=jnp.float32
    )
    cos_y, sin_y = phase_table(ky_ids, cells, grid_len, -1.0)
    next_re, next_im = complex_contract(part_re, part_im, cos_y, sin_y, "abkc,jb->ajkc")
    cos_x, sin_x = phase_table(kx_ids, x_cells, grid_len, -1.0)
    last_re, last_im = complex_contract(next_re, next_im, cos_x, sin_x, "ajkc,ia->ijkc")
    stacked = jnp.stack([last_re, last_im], axis=3) * scale
    return stacked.reshape(MX * MY * MZ, 2, stacked.shape[-1])


def inverse_modes(spectrum, x_cells, grid_len):
    kx_ids, ky_ids, kz_ids = mode_lists()
    cells = jnp.arange(grid_len, dtype=jnp.int32)
    values = spectrum.astype(jnp.float32).reshape(MX, MY, MZ, 2, spectrum.shape[-1])
    cos_x, sin_x = phase_table(kx_ids, x_cells, grid_len, 1.0)
    first_re, first_im = complex_contract(
        values[:, :, :, 0], values[:, :, :, 1], cos_x, sin_x, "ijkc,ia->ajkc"
    )
    cos_y, sin_y = phase_table(ky_ids, cells, grid_len, 1.0)
    second_re, second_im = complex_contract(first_re, first_im, cos_y, sin_y, "ajkc,jb->abkc")
    cos_z, sin_z = phase_table(kz_ids, cells, grid_len, 1.0)
    real_out = jnp.einsum("abkc,kz->abzc", second_re, cos_z, precision=highest)
    real_out = real_out - jnp.einsum("abkc,kz->abzc", second_im, sin_z, precision=highest)
    return real_out * float(MX * MY * MZ) ** (-0.5)


def mix_modes(coeff_b, weights):
    signs = jnp.array([1.0, -1.0], jnp.bfloat16).reshape(1, 2, 1, 1)
    spec_re = jnp.einsum(
        "gmri,mrio->gmo", coeff_b, weights * signs, preferred_element_type=jnp.float32
    )
    spec_im = jnp.einsum(
        "gmri,mrio->gmo", coeff_b[:, :, ::-1], weights, preferred_element_type=jnp.float32
    )
    return jnp.stack([spec_re, spec_im], axis=2)


def weight_grad(coeff_b, back_stack):
    coeff_f = coeff_b.astype(jnp.float32)
    rotated = jnp.stack([-coeff_f[:, :, 1], coeff_f[:, :, 0]], axis=2)
    grad_re = jnp.einsum("gmri,gmro->mio", coeff_f, back_stack, precision=highest)
    grad_im = jnp.einsum("gmri,gmro->mio", rotated, back_stack, precision=highest)
    return jnp.stack([grad_re, grad_im], axis=1)


def point_part(grid_field, branch, local_w, proj, grid_target, scale):
    width = grid_field.shape[-1]
    flat_field = grid_field.reshape(-1, width)
    pre = branch.reshape(-1, width) + jnp.dot(
        flat_field, local_w, preferred_element_type=jnp.float32
    )
    erf_part = lax.erf(pre * root_half)
    active = 0.5 * pre * (1.0 + erf_part)
    pred = jnp.dot(active, proj, precision=highest)
    resid = (pred - grid_target.reshape(-1).astype(jnp.float32)) * scale
    slope = 0.5 * (1.0 + erf_part) + pre * jnp.exp(-0.5 * pre * pre) * inv_root_two_pi
    d_pre = (resid[:, None] * proj[None, :] * slope).astype(jnp.bfloat16)
    local_grad = lax.dot_general(
        flat_field, d_pre, (((0,), (0,)), ((), ())), preferred_element_type=jnp.float32
    )
    return (d_pre.reshape(grid_field.shape), local_grad)


def body(fields, targets, lists, counts, spectral_w, local_w, proj):
    grid_store = fields[0]
    target_store = targets[0]
    slot_order = lists[0]
    slot_count = grid_store.shape[0]
    plane_count = grid_store.shape[1]
    grid_len = grid_store.shape[2]
    width = grid_store.shape[-1]
    lane_index = lax.axis_index("dp")
    x_cells = lax.axis_index("fsdp") * plane_count + jnp.arange(plane_count, dtype=jnp.int32)
    scale = 1.0 / jnp.sum(counts).astype(jnp.float32)
    mode_scale = float(MX * MY * MZ) ** (-0.5)
    live_count = counts[lane_index]
    coeff_init = jnp.zeros((slot_count, MX * MY * MZ, 2, width), jnp.float32)

    def forward_pass(position, coeff_stack):
        slot_index = slot_order[position]
        grid_field = lax.dynamic_index_in_dim(grid_store, slot_index, 0, keepdims=False)
        grid_coeff = forward_modes(grid_field, x_cells, float(grid_len) ** (-1.5))
        return lax.dynamic_update_index_in_dim(coeff_stack, grid_coeff, position, 0)

    coeff_stack = lax.fori_loop(0, live_count, forward_pass, coeff_init)
    coeff_part = lax.psum_scatter(coeff_stack, "fsdp", scatter_dimension=1, tiled=True)
    coeff_b = coeff_part.astype(jnp.bfloat16)
    own_spectrum = mix_modes(coeff_b, spectral_w).astype(jnp.bfloat16)
    spectrum = lax.all_gather(own_spectrum, "fsdp", axis=1, tiled=True)

    def backward_pass(position, carry):
        back_stack, local_total = carry
        slot_index = slot_order[position]
        grid_field = lax.dynamic_index_in_dim(grid_store, slot_index, 0, keepdims=False)
        grid_target = lax.dynamic_index_in_dim(target_store, slot_index, 0, keepdims=False)
        grid_spectrum = lax.dynamic_index_in_dim(spectrum, position, 0, keepdims=False)
        branch = inverse_modes(grid_spectrum, x_cells, grid_len)
        d_pre, local_grad = point_part(grid_field, branch, local_w, proj, grid_target, scale)
        grid_back = forward_modes(d_pre, x_cells, mode_scale)
        return (
            lax.dynamic_update_index_in_dim(back_stack, grid_back, position, 0),
            local_total + local_grad,
        )

    back_init = (jnp.zeros_like(coeff_init), jnp.zeros((width, width), jnp.float32))
    back_stack, local_total = lax.fori_loop(0, live_count, backward_pass, back_init)
    back_part = lax.psum_scatter(back_stack, "fsdp", scatter_dimension=1, tiled=True)
    grad_part = weight_grad(coeff_b, back_part)
    grad_spectral = lax.psum(grad_part, "dp")
    grad_local = lax.psum(local_total, ("dp", "fsdp"))
    return (grad_spectral, grad_local)


def solution(mesh):
    return jax.shard_map(
        body,
        mesh=mesh,
        in_specs=(
            P("dp", None, "fsdp", None, None, None),
            P("dp", None, "fsdp", None),
            P("dp", None),
            P(),
            P("fsdp", None, None, None),
            P(),
            P(),
        ),
        out_specs=(P("fsdp", None, None, None), P()),
        check_vma=False,
    )
```

profile of v0, /device:TPU:0, one launch (start us, length us, event | category | flops | bytes accessed | tf_op | source)
XLA Modules:
  0.0 909.9 jit_solution(849343060945326253)
XLA Ops:
  7.2 1.3 dynamic_slice.42
  8.6 16.0 %while.28 = (s32[]{:T(128)}, f32[6,32,2,128]{3,0,2,1:T(8,128)S(1)}, s32[]{:T(128)}, s32[6]{0:T(128)}, bf16[6,12,48,48,128]{4,3,2,1,0:T(8,128)(2,1)}, /*index=5*/s32[]{:T(128)}, s32[]{:T(128)}, s32[]{:T(128)}, s32[]{:T(128)}) while((s32[]{:T(128)}, f32[6,32,2,128]{3,0,2,1:T(8,128)S(1)}, s32[]{:T(128)}, s32[6]{0:T(128)}, ...), condition=%wide.region_1.2_spmd.clone, body=%wide.region_0.0_spmd.clone.sunk | while | flops 59042712 | bytes 18547260 | solution.py:135
  9.3 1.2 dynamic_slice.73
  12.5 4.1 fusion.405
  16.6 0.5 fusion.406
  17.0 4.1 fusion.407
  21.1 0.5 fusion.408
  21.6 0.3 fusion.412
  21.9 0.5 fusion.410
  22.4 0.5 fusion.411
  22.8 0.3 convolution_subtract_fusion.8
  23.2 0.3 fusion.409
  23.4 0.3 convolution_add_fusion.12
  23.8 0.1 dynamic_update_slice.18
  24.6 0.7 copy-done.2
  25.3 0.0 reduce-scatter.5.cloned.1.call-start
  25.4 0.6 reduce_sum.9
  26.7 97.2 %reduce-scatter.3.cloned.1.call-done = f32[6,8,2,128]{3,0,2,1:T(8,128)} async-done(((f32[6,32,2,128]{3,0,2,1:T(8,128)}), f32[6,8,2,128]{3,0,2,1:T(8,128)}) %reduce-scatter.3.cloned.1.call-update) | async-done | bytes 49168 | tf_op jit(solution)/shard_map/reduce_scatter | solution.py:136
  123.9 1.5 fusion.282
  125.4 0.2 fusion.272
  125.6 0.2 fusion.273
  125.9 13.4 %all_gather.3 = bf16[6,32,2,128]{3,0,1,2:T(8,128)(2,1)S(1)} all-gather(bf16[6,8,2,128]{3,0,1,2:T(8,128)(2,1)S(1)} %pad_maximum_fusion.1), channel_id=1, replica_groups=mesh['dp'=8,'fsdp'=4] {'fsdp'}, dimensions={1}, use_global_device_ids=true | all-gather | bytes 122880 | tf_op jit(solution)/shard_map/all_gather | solution.py:139
  139.4 112.8 %while.29 = (s32[]{:T(128)}, f32[6,32,2,128]{3,1,2,0:T(8,128)S(1)}, f32[128,128]{1,0:T(8,128)S(1)}, s32[]{:T(128)}, bf16[6,32,2,128]{3,1,2,0:T(8,128)(2,1)S(1)},...) while((s32[]{:T(128)}, f32[6,32,2,128]{3,1,2,0:T(8,128)S(1)}, ...), condition=%wide.region_5.6_spmd.clone, body=%wide.region_4.5_spmd.clone.sunk | while | flops 2178119680 | bytes 216721648 | solution.py:156
  161.2 0.3 fusion.458
  161.5 0.4 convolution_subtract_fusion.9
  161.9 0.8 fusion.459
  162.7 0.3 fusion.456
  163.0 0.4 convolution_add_fusion.13
  163.4 0.8 fusion.457
  164.2 11.7 %fusion.460 = f32[48,12,48,128]{3,0,2,1:T(8,128)S(1)} fusion(f32[48,12,2,128]{3,0,2,1:T(8,128)S(1)} %fusion.457, f32[48,12,2,128]{3,0,2,1:T(8,128)S(1)} %fusion.459), kind=kOutput, calls=%fused_computation.130.clone.1 | convolution fusion | flops 85082976 | bytes 15335424 | tf_op jit(solution)/shard_map/while/body/abkc,kz->abzc/dot_general | solution.py:72
  175.9 0.8 fusion.462
  176.7 0.8 fusion.461
  177.6 15.1 %subtract_multiply_fusion.4 = f32[48,12,48,128]{3,0,2,1:T(8,128)} fusion(f32[48,12,48,128]{3,0,2,1:T(8,128)S(1)} %fusion.460, f32[48,12,2,128]{3,0,2,1:T(8,128)S(1)} %fusion.461, f32[48,12,2,128]{3,0,2,1:T(8,128)S(1)} %fusion.462), kind=kOutput, calls=%fused_computation.116.clone.1 | convolution fusion | flops 92160864 | bytes 29491200 | tf_op jit(solution)/shard_map/while/body/abkc,kz->abzc/dot_general | solution.py:73
  192.7 0.6 dynamic_slice.77
  195.2 4.2 constant_dynamic-slice_fusion.5
  199.5 11.8 %convolution_add_fusion.14 = f32[27648,128]{1,0:T(8,128)} fusion(f32[27648,128]{1,0:T(8,128)} %bitcast.341, bf16[27648,128]{1,0:T(8,128)(2,1)S(1)} %bitcast.337, bf16[128,128]{1,0:T(8,128)(2,1)S(1)} %get-tuple-element.534), kind=kOutput, calls=%fused_computation.104.clone.1 | convolution fusion | flops 909508608 | bytes 35422208 | tf_op jit(solution)/shard_map/while/body/dot_general | solution.py:99
  211.2 16.9 %fusion.463 = f32[1,27648]{1,0:T(1,128)S(1)} fusion(f32[27648,128]{1,0:T(8,128)} %convolution_add_fusion.14, f32[128]{0:T(128)S(1)} %get-tuple-element.535), kind=kOutput, calls=%fused_computation.112.clone.1 | convolution fusion | flops 56623104 | bytes 14266880 | tf_op jit(solution)/shard_map/while/body/dot_general | solution.py:104
  228.2 1.1 dynamic-slice_convert_fusion.2
  229.3 14.7 %fusion.464 = bf16[27648,128]{1,0:T(8,128)(2,1)S(1)} fusion(f32[27648,128]{1,0:T(8,128)} %convolution_add_fusion.14, f32[128]{0:T(128)} %get-tuple-element.576, f32[27648]{0:T(1024)S(1)} %subtract_multiply_fusion.5), kind=kLoop, calls=%fused_computation.111.clone.1 | loop fusion | flops 38928384 | bytes 21344768 | tf_op jit(solution)/shard_map/while/body/convert_element_type | solution.py:107
  244.0 2.0 convolution_add_fusion.16
  246.1 1.1 convolution_bitcast_fusion.8
  247.2 0.5 fusion.468
  247.7 1.1 convolution_bitcast_fusion.9
  248.7 0.5 fusion.469
  249.2 0.5 fusion.465
  249.7 0.5 fusion.466
  250.2 0.3 fusion.470
  250.4 0.3 convolution_subtract_fusion.10
  250.8 0.3 fusion.467
  251.0 0.3 convolution_add_fusion.15
  252.2 0.7 copy-done.4
  252.9 0.0 all-reduce.3.cloned.1.call-start
  253.0 0.7 slice.19
  253.7 0.8 slice_negate_fusion
  254.5 465.9 %reduce-scatter.5.cloned.1.call-done = f32[6,8,2,128]{3,1,2,0:T(8,128)} async-done(((f32[6,32,2,128]{3,1,2,0:T(8,128)}), f32[6,8,2,128]{3,1,2,0:T(8,128)}) %reduce-scatter.5.cloned.1.call-update) | async-done | bytes 49168 | tf_op jit(solution)/shard_map/reduce_scatter | solution.py:157
  720.4 1.2 convolution_bitcast_fusion.2
  721.7 1.8 convolution_bitcast_fusion.3
  723.5 1.1 pad_maximum_fusion
  724.6 0.0 all-reduce.5.cloned.1.call-start
  724.6 0.5 all-reduce.5.cloned.1.call-update
  725.1 54.3 %all-reduce.3.cloned.1.call-done = f32[8,2,128,128]{3,2,0,1:T(8,128)} async-done(((f32[8,2,128,128]{3,2,0,1:T(8,128)}), f32[8,2,128,128]{3,2,0,1:T(8,128)}) %all-reduce.3.cloned.1.call-update) | async-done | bytes 1048592 | tf_op jit(solution)/shard_map/psum | solution.py:159
  779.5 2.3 copy.57
  781.8 119.8 %all-reduce.5.cloned.1.call-done = f32[128,128]{1,0:T(8,128)} async-done(((f32[128,128]{1,0:T(8,128)}), f32[128,128]{1,0:T(8,128)}) %all-reduce.5.cloned.1.call-update) | async-done | bytes 65552 | tf_op jit(solution)/shard_map/psum | solution.py:160
  901.5 1.5 copy.239
  (56 shorter events, 0.4 us)
Async XLA Ops:
  7.2 116.7 %reduce-scatter.3.cloned.1.call-start = ((), (), s32[]{:S(2)}) async-start(), calls=%async_computation.2 | async-start | bytes 327680 | tf_op jit(solution)/shard_map/reduce_scatter | solution.py:136
  8.5 16.8 %copy-start.11 = (s32[8]{0:T(128)S(1)}, s32[8]{0:T(128)}, u32[]{:S(2)}) copy-start(s32[8]{0:T(128)} %param.15) | copy-start | bytes 100
  8.5 116.9 %copy-start.6 = (bf16[8,2,128,128]{3,2,1,0:T(8,128)(2,1)S(1)}, bf16[8,2,128,128]{3,2,1,0:T(8,128)(2,1)}, u32[]{:S(2)}) copy-start(bf16[8,2,128,128]{3,2,1,0:T(8,128)(2,1)} %param.16) | copy-start | bytes 1572868
  8.6 117.0 %copy-start.13 = (bf16[2]{0:T(256)(128)(2,1)S(1)}, bf16[2]{0:T(256)(128)(2,1)}, u32[]{:S(2)}) copy-start(bf16[2]{0:T(256)(128)(2,1)} %constant.202.clone) | copy-start | bytes 16
  8.6 130.8 %copy-start.3 = (bf16[128,128]{1,0:T(8,128)(2,1)S(1)}, bf16[128,128]{1,0:T(8,128)(2,1)}, u32[]{:S(2)}) copy-start(bf16[128,128]{1,0:T(8,128)(2,1)} %param.17) | copy-start | bytes 98308
  8.6 130.8 %copy-start.9 = (f32[128]{0:T(128)S(1)}, f32[128]{0:T(128)}, u32[]{:S(2)}) copy-start(f32[128]{0:T(128)} %param.18) | copy-start | bytes 1540
  24.6 0.7 copy-start.2
  25.3 695.1 %reduce-scatter.5.cloned.1.call-start = ((), (), s32[]{:S(2)}) async-start(), calls=%async_computation.3 | async-start | bytes 245760 | tf_op jit(solution)/shard_map/reduce_scatter | solution.py:157
  125.4 14.0 %copy-start.5 = (bf16[6,8,2,128]{3,0,2,1:T(8,128)(2,1)}, bf16[6,8,2,128]{3,0,2,1:T(8,128)(2,1)S(1)}, u32[]{:S(2)}) copy-start(bf16[6,8,2,128]{3,0,2,1:T(8,128)(2,1)S(1)} %get-tuple-element.351) | copy-start | bytes 73732
  161.1 14.8 %copy-start.7 = (bf16[6,32,2,128]{3,1,2,0:T(8,128)(2,1)}, bf16[6,32,2,128]{3,1,2,0:T(8,128)(2,1)S(1)}, u32[]{:S(2)}) copy-start(bf16[6,32,2,128]{3,1,2,0:T(8,128)(2,1)S(1)} %get-tuple-element.531) | copy-start | bytes 294916 | tf_op jit(solution)/shard_map/while
  177.6 15.1 %copy-start.12 = (s32[6]{0:T(128)S(1)}, s32[6]{0:T(128)}, u32[]{:S(2)}) copy-start(s32[6]{0:T(128)} %get-tuple-element.532) | copy-start | bytes 76 | tf_op jit(solution)/shard_map/while
  199.5 11.8 %copy-start = (bf16[1,12,48,48,128]{4,3,2,1,0:T(8,128)(2,1)}, bf16[1,12,48,48,128]{4,3,2,1,0:T(8,128)(2,1)S(1)}, u32[]{:S(2)}) copy-start(bf16[1,12,48,48,128]{4,3,2,1,0:T(8,128)(2,1)S(1)} %constant_dynamic-slice_fusion.5) | copy-start | bytes 21233668 | tf_op jit(solution)/shard_map/while
  228.1 15.9 %slice-start = ((s8[7077888]{0:T(1024)(128)(4,1)}), s8[2883584]{0:T(1024)(128)(4,1)S(1)}, s32[]{:S(2)}) async-start(s8[7077888]{0:T(1024)(128)(4,1)} %bitcast.338), calls=%async_computation.6 | async-start | bytes 5767168 | tf_op jit(solution)/shard_map/while
  229.3 14.8 %slice-start.1 = ((s8[7077888]{0:T(1024)(128)(4,1)}), s8[4194304]{0:T(1024)(128)(4,1)S(1)}, s32[]{:S(2)}) async-start(s8[7077888]{0:T(1024)(128)(4,1)} %bitcast.338), calls=%async_computation.7 | async-start | bytes 8388608 | tf_op jit(solution)/shard_map/while
  246.1 5.3 copy-start.8
  246.1 5.3 copy-start.10
  252.2 0.7 copy-start.4
  252.2 472.4 %copy-start.1 = (f32[128,128]{1,0:T(8,128)}, f32[128,128]{1,0:T(8,128)S(1)}, u32[]{:S(2)}) copy-start(f32[128,128]{1,0:T(8,128)S(1)} %get-tuple-element.563) | copy-start | bytes 196612
  252.9 526.6 %all-reduce.3.cloned.1.call-start = ((), (), s32[]{:S(2)}) async-start(), calls=%async_computation.4 | async-start | bytes 2097152 | tf_op jit(solution)/shard_map/psum | solution.py:159
  724.6 177.0 %all-reduce.5.cloned.1.call-start = ((), (), s32[]{:S(2)}) async-start(), calls=%async_computation.5 | async-start | bytes 131072 | tf_op jit(solution)/shard_map/psum | solution.py:160
Sparse Core Ops, SparseCore 0:
  25.4 98.4 reduce-scatter.2
  253.1 467.3 reduce-scatter.4
  724.7 54.7 all-reduce.2
  784.9 116.5 all-reduce.4
where the time goes:
time: 919 us; the launch traced here: 910 us
  waiting for transfers between devices  738 us (80%)
  matrix products  82 us (9%)
  loops' own time  28.1 us (3%)
  other arithmetic  19.8 us (2%)
  between operations  15 us (2%)
  local copies, waits for them, and re-layouts  13.7 us (1%)
  blocking collectives  13.4 us (1%)
    reduce_scatter x1, waiting for transfers between devices, body(): lax.psum_scatter(back_stack, 'fsdp', scatter_dimension=1, tiled=True)  466 us
    psum x1, waiting for transfers between devices, body(): grad_local = lax.psum(local_total, ('dp', 'fsdp'))  120 us
    reduce_scatter x1, waiting for transfers between devices, body(): lax.psum_scatter(coeff_stack, 'fsdp', scatter_dimension=1, tiled=True)  97.2 us
    psum x1, waiting for transfers between devices, body(): grad_spectral = lax.psum(grad_part, 'dp')  54.3 us
    another operation x1, loops' own time, body(): lax.fori_loop(0, live_count, backward_pass, back_init)  24.7 us
  transfers between devices with their start and end apart: 4, of which 4 were waited for; matrix products, arithmetic and copies ran while one was open for 0% of the time, Pallas kernels for 0%

commit v1 on v0

v1 whole, which is shorter than its diff:
```python
import functools
import math

import jax
import jax.numpy as jnp
import ml_dtypes
import numpy as np
from jax import lax
from jax.experimental import pallas as pl
from jax.experimental.pallas import tpu as pltpu
from jax.sharding import PartitionSpec as P

MX = 4
MY = 4
MZ = 2
MODES = MX * MY * MZ
VMEM_BYTES = 40 * 1024 * 1024
f32 = jnp.float32
bf16 = jnp.bfloat16
inv_root_two_pi = 0.3989422804014327
half_log2e = 0.7213475204444817
erf_p = 0.3275911 * 0.7071067811865476
erf_a = tuple(0.5 * a for a in (0.254829592, -0.284496736, 1.421413741, -1.453152027, 1.061405429))


def split_bf16(values):
    high = values.astype(ml_dtypes.bfloat16)
    low = (values - high.astype(np.float64)).astype(ml_dtypes.bfloat16)
    return high, low


def angles(mode_ids, length):
    product = np.outer(mode_ids, np.arange(length)) % length
    return product * (2.0 * math.pi / length)


def phase_constants(length):
    y_angle = angles(np.arange(MY) - MY // 2, length)
    z_angle = angles(np.arange(MZ), length)
    rounded = lambda v: v.astype(np.float32).astype(ml_dtypes.bfloat16).astype(np.float64)
    cz, sz = rounded(np.cos(z_angle)), rounded(-np.sin(z_angle))
    cy, sy = np.cos(y_angle), -np.sin(y_angle)
    both = lambda a, b: (a[:, None, :, None] * b[None, :, None, :]).reshape(MY * MZ, length * length)
    fwd = np.concatenate([both(cy, cz) - both(sy, sz), both(sy, cz) + both(cy, sz)], axis=0)
    fwd = np.concatenate(split_bf16(fwd), axis=0)
    cz, sz = np.cos(z_angle), np.sin(z_angle)
    cy, sy = np.cos(y_angle), np.sin(y_angle)
    inv = np.concatenate([both(cy, cz) - both(sy, sz), -(both(sy, cz) + both(cy, sz))], axis=0).T
    high, low = split_bf16(inv)
    pad = np.zeros((length * length, 128 - 4 * high.shape[1]), ml_dtypes.bfloat16)
    inv = np.concatenate([high, low, high, low, pad], axis=1)
    x_angle = angles(np.arange(MX) - MX // 2, length).T
    xtab = np.stack([np.cos(x_angle), np.sin(x_angle)], axis=2).astype(np.float32)
    return fwd, inv, xtab.reshape(-1)


def scalar_places(slots):
    return dict(count=slots, total=slots + 1, shard=slots + 2, first=slots + 3)


def combine_planes(q_ref, xtab_ref, cell0, shard, planes, scale, store):
    for d in range(MX):
        i = lax.rem(shard + d, MX)
        re = jnp.zeros((8, 128), f32)
        im = jnp.zeros((8, 128), f32)
        for a in range(planes):
            at = ((cell0 + a) * MX + i) * 2
            c = xtab_ref[at]
            s = xtab_ref[at + 1]
            q_re = q_ref[a, 0:8, :]
            q_im = q_ref[a, 8:16, :]
            re = re + (q_re * c + q_im * s)
            im = im + (q_im * c - q_re * s)
        store(d, re * scale, im * scale)


def forward_kernel(
    slots, planes, step_planes, scale, meta_ref, xtab_ref, f_ref, basis_ref, *rest
):
    outs, q_ref = rest[:MX], rest[MX]
    place = scalar_places(slots)
    g, blk = pl.program_id(0), pl.program_id(1)
    live = g < meta_ref[place["count"]]
    row = pl.multiple_of(g * 16, 16)

    @pl.when(live)
    def _():
        cells = f_ref.shape[3] * f_ref.shape[4]
        for p in range(step_planes):
            field = f_ref[0, 0, p].reshape(cells, 128)
            part = jnp.dot(basis_ref[...], field, preferred_element_type=f32)
            q_ref[blk * step_planes + p] = part[0:16] + part[16:32]

        @pl.when(blk == planes // step_planes - 1)
        def _():
            def store(d, re, im):
                outs[d][pl.ds(row, 8), :] = re
                outs[d][pl.ds(row + 8, 8), :] = im

            combine_planes(
                q_ref, xtab_ref, meta_ref[place["first"]], meta_ref[place["shard"]], planes, scale, store
            )

    @pl.when(jnp.logical_not(live) & (blk == 0))
    def _():
        for out in outs:
            out[pl.ds(row, 16), :] = jnp.zeros((16, 128), f32)


def gelu_parts(pre):
    bell = jnp.exp2(pre * pre * (-half_log2e))
    t = pl.reciprocal(1.0 + erf_p * jnp.abs(pre), approx=True)
    poly = erf_a[4]
    for a in (erf_a[3], erf_a[2], erf_a[1], erf_a[0]):
        poly = poly * t + a
    tail = poly * t * bell
    cdf = jnp.where(pre >= 0.0, 1.0 - tail, tail)
    return cdf, bell


def backward_kernel(
    slots, planes, step_planes, rows_step, scale, meta_ref, xtab_ref, f_ref, t_ref, *rest
):
    specs = rest[:MX]
    w_ref, proj_ref, inv_ref, basis_ref, eye_ref, ones_ref = rest[MX : MX + 6]
    outs = rest[MX + 6 : 2 * MX + 6]
    rhs_ref, d_ref, total_ref, q_ref, t16_ref, spec_ref = rest[2 * MX + 6 :]
    place = scalar_places(slots)
    g, blk = pl.program_id(0), pl.program_id(1)
    blocks = planes // step_planes
    live = g < meta_ref[place["count"]]
    row = pl.multiple_of(g * 16, 16)
    shard = meta_ref[place["shard"]]
    cell0 = meta_ref[place["first"]]
    cells = f_ref.shape[3] * f_ref.shape[4]
    third = cells // 3
    steps = third // rows_step
    subs = rows_step // 128

    @pl.when((g == 0) & (blk == 0))
    def _():
        total_ref[...] = jnp.zeros_like(total_ref)
        rhs_ref[0:128, :] = w_ref[...]
        rhs_ref[128:256, :] = jnp.zeros((128, 128), bf16)

    @pl.when(live)
    def _():
        @pl.when(blk == 0)
        def _():
            lines = t_ref[0, 0].astype(f32)
            for a in range(planes):
                line = jnp.broadcast_to(lines[a : a + 1, :], (16, cells))
                t16_ref[a] = line.astype(bf16)
            for d in range(MX):
                spec_ref[d] = specs[d][pl.ds(row, 16), :].astype(f32)

        count = meta_ref[place["total"]].astype(f32)
        proj = proj_ref[...]
        proj_scaled = proj / jnp.full((1, 128), count, f32)

        def plane(p, carry):
            a = blk * step_planes + p
            re = jnp.zeros((8, 128), f32)
            im = jnp.zeros((8, 128), f32)
            for d in range(MX):
                i = lax.rem(shard - d + MX, MX)
                at = ((cell0 + a) * MX + i) * 2
                c = xtab_ref[at]
                s = xtab_ref[at + 1]
                s_re = spec_ref[d, 0:8, :]
                s_im = spec_ref[d, 8:16, :]
                re = re + (s_re * c - s_im * s)
                im = im + (s_re * s + s_im * c)
            first = jnp.concatenate([re, im], axis=0) * scale
            high = first.astype(bf16)
            low = (first - high.astype(f32)).astype(bf16)
            rhs_ref[128:144, :] = high
            rhs_ref[144:160, :] = high
            rhs_ref[160:176, :] = low
            rhs_ref[176:192, :] = low
            field = f_ref[0, 0, p].reshape(cells, 128)

            def stage_one(r0):
                part = slice(r0, r0 + rows_step)
                lhs = jnp.concatenate([field[part], inv_ref[part, :]], axis=1)
                pre = jnp.dot(lhs, rhs_ref[...], preferred_element_type=f32)
                cdf, bell = gelu_parts(pre)
                slope = (cdf + pre * bell * inv_root_two_pi) * proj_scaled
                active = (pre * cdf * proj).astype(bf16)
                wanted = []
                for j in range(subs):
                    at = r0 + j * 128
                    line = t16_ref[a, :, at : at + 128]
                    wanted.extend(line * eye_ref[n : n + 16, :] for n in range(0, 128, 16))
                wanted = jnp.concatenate(wanted, axis=0)
                return jnp.concatenate([active, wanted], axis=1), slope

            def stage_two(r0, both, slope):
                resid = jnp.dot(both, ones_ref[...], preferred_element_type=f32)
                d_ref[r0 : r0 + rows_step, :] = (resid * slope).astype(bf16)

            q = jnp.zeros((32, 128), f32)
            for k in range(3):
                waiting = None
                for s in range(steps):
                    r0 = k * third + s * rows_step
                    made = stage_one(r0)
                    if waiting is not None:
                        stage_two(*waiting)
                    waiting = (r0,) + made
                stage_two(*waiting)
                part = slice(k * third, (k + 1) * third)
                lhs = jnp.concatenate([field[part].T, basis_ref[:, part]], axis=0)
                sums = jnp.dot(lhs, d_ref[part, :], preferred_element_type=f32)
                total_ref[...] += sums[0:128]
                q = q + sums[128:160]
            q_ref[a] = q[0:16] + q[16:32]
            return carry

        lax.fori_loop(0, step_planes, plane, 0)

        @pl.when(blk == blocks - 1)
        def _():
            def store(d, re, im):
                outs[d][pl.ds(row, 8), :] = re
                outs[d][pl.ds(row + 8, 8), :] = im

            combine_planes(q_ref, xtab_ref, cell0, shard, planes, scale, store)

    @pl.when(jnp.logical_not(live) & (blk == 0))
    def _():
        for out in outs:
            out[pl.ds(row, 16), :] = jnp.zeros((16, 128), f32)

    @pl.when((g == slots - 1) & (blk == blocks - 1))
    def _():
        part = 128 // MX
        for d in range(MX):
            i = lax.rem(shard + d, MX)
            at = pl.multiple_of(i * part, part)
            outs[d][slots * 16 : slots * 16 + part, :] = total_ref[pl.ds(at, part), :]


def mix_kernel(slots, per, shards, *refs):
    parts = refs[:shards]
    w_ref, coeff_out, spec_out, c_ref, s_ref = refs[shards:]
    total = parts[0][...]
    for part in parts[1:]:
        total = total + part[...]
    coeff = total.astype(bf16)
    coeff_out[...] = coeff
    c_ref[...] = coeff.astype(f32)
    for m in range(per):
        re_rows = pl.ds(m, slots, stride=2 * per)
        im_rows = pl.ds(per + m, slots, stride=2 * per)
        re = c_ref[re_rows, :].astype(bf16)
        im = c_ref[im_rows, :].astype(bf16)
        weight = w_ref[m].reshape(256, 128)
        s_ref[re_rows, :] = jnp.dot(
            jnp.concatenate([re, -im], axis=1), weight, preferred_element_type=f32
        )
        s_ref[im_rows, :] = jnp.dot(
            jnp.concatenate([im, re], axis=1), weight, preferred_element_type=f32
        )
    spec_out[...] = s_ref[...].astype(bf16)


def sum_kernel(count, *refs):
    total = refs[0][...]
    for part in refs[1:count]:
        total = total + part[...]
    refs[count][...] = total


def local_sum_kernel(count, rows, *refs):
    size = refs[count].shape[0]
    total = refs[0][rows : rows + size, :]
    for part in refs[1:count]:
        total = total + part[rows : rows + size, :]
    refs[count][...] = total


def weight_kernel(lanes, slots, per, *refs):
    coeffs, backs = refs[:lanes], refs[lanes : 2 * lanes]
    out_ref, c_ref, b_ref = refs[2 * lanes :]
    rows = slots * 2 * per
    for n in range(lanes):
        c_ref[n * rows : (n + 1) * rows, :] = coeffs[n][...].astype(f32)
        b_ref[n * rows : (n + 1) * rows, :] = backs[n][0:rows, :]
    for m in range(per):
        re_rows = pl.ds(m, lanes * slots, stride=2 * per)
        im_rows = pl.ds(per + m, lanes * slots, stride=2 * per)
        c_re = c_ref[re_rows, :].astype(bf16)
        c_im = c_ref[im_rows, :].astype(bf16)
        b_re = b_ref[re_rows, :]
        b_im = b_ref[im_rows, :]
        left = jnp.concatenate([c_re, c_im], axis=0)
        right = jnp.concatenate(
            [jnp.concatenate([b_re, b_im], axis=1), jnp.concatenate([b_im, -b_re], axis=1)], axis=0
        )
        high = right.astype(bf16)
        low = (right - high.astype(f32)).astype(bf16)
        left = jnp.concatenate([left, left], axis=0)
        right = jnp.concatenate([high, low], axis=0)
        grad = lax.dot_general(
            left, right, (((0,), (0,)), ((), ())), preferred_element_type=f32
        )
        out_ref[m, 0] = grad[:, 0:128]
        out_ref[m, 1] = grad[:, 128:256]


def place_kernel(shards, meta_ref, *refs):
    out_ref = refs[shards]
    size = refs[0].shape[0]
    for d in range(shards):
        i = lax.rem(meta_ref[0] - d + shards, shards)
        out_ref[pl.ds(pl.multiple_of(i * size, size), size), :] = refs[d][...]


def whole_vmem(count):
    return [pl.BlockSpec(memory_space=pltpu.VMEM)] * count


def params():
    return pltpu.CompilerParams(vmem_limit_bytes=VMEM_BYTES)


def rotations(value_of, axis, size):
    got = [value_of(0)]
    for d in range(1, size):
        perm = [(s, (s + d) % size) for s in range(size)]
        got.append(lax.ppermute(value_of(d), axis, perm))
    return got


def body(lanes, shards, fields, targets, lists, counts, spectral_w, local_w, proj):
    _, slots, planes, grid_len, _, width = fields.shape
    per = MODES // shards
    split = shards // MX
    cells = grid_len * grid_len
    step_planes = max(n for n in (1, 2, 3, 4) if planes % n == 0)
    blocks = planes // step_planes
    basis, inverse, xtab = phase_constants(grid_len)
    lane = lax.axis_index("dp")
    shard = lax.axis_index("fsdp").astype(jnp.int32)
    turn = shard if split == 1 else jnp.int32(0)
    meta = jnp.concatenate(
        [
            lists[0],
            counts[lane][None],
            jnp.sum(counts)[None],
            turn[None],
            (shard * planes)[None],
        ]
    ).astype(jnp.int32)
    place = scalar_places(slots)

    def field_block(g, blk, meta_ref, xtab_ref):
        count = meta_ref[place["count"]]
        slot = meta_ref[jnp.minimum(g, count - 1)]
        return (0, slot, jnp.where(g < count, blk, blocks - 1), 0, 0, 0)

    def target_block(g, blk, meta_ref, xtab_ref):
        count = meta_ref[place["count"]]
        return (0, meta_ref[jnp.minimum(g, count - 1)], 0, 0)

    def fixed(*shape):
        return pl.BlockSpec(shape, lambda g, blk, meta_ref, xtab_ref: (0,) * len(shape))

    field_spec = pl.BlockSpec((1, 1, step_planes, grid_len, grid_len, width), field_block)
    part_rows = slots * 16
    parts = pl.pallas_call(
        functools.partial(forward_kernel, slots, planes, step_planes, float(grid_len) ** (-1.5)),
        grid_spec=pltpu.PrefetchScalarGridSpec(
            num_scalar_prefetch=2,
            grid=(slots, blocks),
            in_specs=[field_spec, fixed(*basis.shape)],
            out_specs=[fixed(part_rows, width)] * MX,
            scratch_shapes=[pltpu.VMEM((planes, 16, width), f32)],
        ),
        out_shape=[jax.ShapeDtypeStruct((part_rows, width), f32)] * MX,
        compiler_params=params(),
        name="forward_modes",
    )(meta, xtab, fields, basis)

    def shard_parts(pieces, count):
        if split == 1:
            return lambda d: pieces[d]
        stacked = jnp.stack(pieces).reshape(MX, count, 2, split, per, width)
        stacked = jnp.moveaxis(stacked, 3, 1).reshape(shards, count * 2 * per, width)
        return lambda d: lax.dynamic_index_in_dim(stacked, (shard + d) % shards, 0, keepdims=False)

    def mode_parts(pieces, count):
        if split == 1:
            return pieces
        stacked = jnp.stack(pieces)[(shard - jnp.arange(shards)) % shards]
        stacked = stacked.reshape(MX, split, count, 2, per, width)
        stacked = jnp.moveaxis(stacked, 1, 3).reshape(MX, count * 16, width)
        return [stacked[(-d) % MX] for d in range(MX)]

    came = rotations(shard_parts(parts, slots), "fsdp", shards)
    own_rows = slots * 2 * per
    coeff, own_spectrum = pl.pallas_call(
        functools.partial(mix_kernel, slots, per, shards),
        in_specs=whole_vmem(shards + 1),
        out_specs=whole_vmem(2),
        out_shape=[jax.ShapeDtypeStruct((own_rows, width), bf16)] * 2,
        scratch_shapes=[pltpu.VMEM((own_rows, width), f32)] * 2,
        compiler_params=params(),
        name="mix_modes",
    )(*came, spectral_w)
    spectrum = mode_parts(rotations(lambda d: own_spectrum, "fsdp", shards), slots)
    coeffs = rotations(lambda d: coeff, "dp", lanes)

    local_rows = width // MX
    eye = np.eye(128, dtype=ml_dtypes.bfloat16)
    ones = np.ones((128, 128), ml_dtypes.bfloat16)
    ones = np.concatenate([ones, -ones], axis=0)
    results = pl.pallas_call(
        functools.partial(backward_kernel, slots, planes, step_planes, 256, float(MODES) ** (-0.5)),
        grid_spec=pltpu.PrefetchScalarGridSpec(
            num_scalar_prefetch=2,
            grid=(slots, blocks),
            in_specs=[field_spec, pl.BlockSpec((1, 1, planes, cells), target_block)]
            + [fixed(part_rows, width)] * MX
            + [
                fixed(width, width),
                fixed(1, width),
                fixed(*inverse.shape),
                fixed(*basis.shape),
                fixed(*eye.shape),
                fixed(*ones.shape),
            ],
            out_specs=[fixed(part_rows + local_rows, width)] * MX,
            scratch_shapes=[
                pltpu.VMEM((256, width), bf16),
                pltpu.VMEM((cells, width), bf16),
                pltpu.VMEM((width, width), f32),
                pltpu.VMEM((planes, 16, width), f32),
                pltpu.VMEM((planes, 16, cells), bf16),
                pltpu.VMEM((MX, 16, width), f32),
            ],
        ),
        out_shape=[jax.ShapeDtypeStruct((part_rows + local_rows, width), f32)] * MX,
        compiler_params=params(),
        cost_estimate=pl.CostEstimate(
            flops=4 * slots * planes * cells * 256 * 256,
            bytes_accessed=slots * planes * cells * width * 2,
            transcendentals=0,
        ),
        name="backward_modes",
    )(
        meta, xtab, fields, targets, *spectrum, local_w, proj.reshape(1, width), inverse, basis, eye, ones
    )

    if split == 1:
        chunk = lambda d: results[d]
    else:
        backs = shard_parts([r[:part_rows] for r in results], slots)
        local = jnp.concatenate([r[part_rows:] for r in results], axis=0)
        rows = width // shards
        chunk = lambda d: jnp.concatenate(
            [backs(d), lax.dynamic_slice_in_dim(local, (shard + d) % shards * rows, rows, 0)], axis=0
        )
    came = rotations(chunk, "fsdp", shards)
    own_sum = pl.pallas_call(
        functools.partial(sum_kernel, shards),
        in_specs=whole_vmem(shards),
        out_specs=pl.BlockSpec(memory_space=pltpu.VMEM),
        out_shape=jax.ShapeDtypeStruct(came[0].shape, f32),
        compiler_params=params(),
        name="sum_shards",
    )(*came)
    sums = rotations(lambda d: own_sum, "dp", lanes)
    own_local = pl.pallas_call(
        functools.partial(local_sum_kernel, lanes, own_rows),
        in_specs=whole_vmem(lanes),
        out_specs=pl.BlockSpec(memory_space=pltpu.VMEM),
        out_shape=jax.ShapeDtypeStruct((width // shards, width), f32),
        compiler_params=params(),
        name="sum_local",
    )(*sums)
    locals_ = rotations(lambda d: own_local, "fsdp", shards)
    grad_spectral = pl.pallas_call(
        functools.partial(weight_kernel, lanes, slots, per),
        in_specs=whole_vmem(2 * lanes),
        out_specs=pl.BlockSpec(memory_space=pltpu.VMEM),
        out_shape=jax.ShapeDtypeStruct((per, 2, width, width), f32),
        scratch_shapes=[pltpu.VMEM((lanes * own_rows, width), f32)] * 2,
        compiler_params=params(),
        cost_estimate=pl.CostEstimate(
            flops=2 * per * 192 * 128 * 256, bytes_accessed=2 * per * 2 * width * width * 4, transcendentals=0
        ),
        name="weight_grad",
    )(*coeffs, *sums)
    grad_local = pl.pallas_call(
        functools.partial(place_kernel, shards),
        in_specs=[pl.BlockSpec(memory_space=pltpu.SMEM)] + whole_vmem(shards),
        out_specs=pl.BlockSpec(memory_space=pltpu.VMEM),
        out_shape=jax.ShapeDtypeStruct((width, width), f32),
        compiler_params=params(),
        name="place_local",
    )(shard[None], *locals_)
    return (grad_spectral, grad_local)


def solution(mesh):
    return jax.shard_map(
        functools.partial(body, mesh.shape["dp"], mesh.shape["fsdp"]),
        mesh=mesh,
        in_specs=(
            P("dp", None, "fsdp", None, None, None),
            P("dp", None, "fsdp", None),
            P("dp", None),
            P(),
            P("fsdp", None, None, None),
            P(),
            P(),
        ),
        out_specs=(P("fsdp", None, None, None), P()),
        check_vma=False,
    )
```

time: 919 us -> 232 us (0.25)
  waiting for transfers between devices: 738 us -> 12.4 us
  starting transfers between devices: 0.16 us -> 174 us
  matrix products: 82 us -> 0 us
  Pallas kernels: 0 us -> 37.6 us
  loops' own time: 28.1 us -> 0 us
  other arithmetic: 19.8 us -> 1.35 us
  between operations: 15 us -> 0.78 us
  blocking collectives: 13.4 us -> 0 us
    reduce_scatter x2 -> x0, waiting for transfers between devices: 563 us -> none  [the longest x1 466 us: body(): lax.psum_scatter(back_stack, 'fsdp', scatter_dimension=1, tiled=True)]
    psum x2 -> x0, waiting for transfers between devices: 174 us -> none  [the longest x1 120 us: body(): grad_local = lax.psum(local_total, ('dp', 'fsdp'))]
    ppermute x0 -> x26, starting transfers between devices: none -> 174 us  [rotations(): got.append(lax.ppermute(value_of(d), axis, perm))]
    dot_general x37 -> x0, matrix products: 82 us -> none  [the longest x1 16.9 us: point_part(): pred = jnp.dot(active, proj, precision=highest)]
    pallas_call x0 -> x7, Pallas kernels: none -> 37.6 us  [the longest x1 29.4 us: body(): pl.pallas_call(functools.partial(backward_kernel, slots, planes, step_pla...]
    another operation x2 -> x0, loops' own time: 28.1 us -> none  [the longest x1 24.7 us: body(): lax.fori_loop(0, live_count, backward_pass, back_init)]
    convert_element_type x3 -> x0, other arithmetic: 17.2 us -> none  [the longest x1 14.7 us: point_part(): d_pre = (resid[:, None] * proj[None, :] * slope).astype(jnp.bfloat16)]
    all_gather x1 -> x0, blocking collectives: 13.4 us -> none  [body(): spectrum = lax.all_gather(own_spectrum, 'fsdp', axis=1, tiled=True)]
  transfers between devices with their start and end apart: 4 -> 26, of which waited for: 4 -> 11; matrix products, arithmetic and copies ran while one was open for 0% -> 0% of each run, Pallas kernels for 0% -> 1%
where the time goes in v1:
time: 232 us; the launch traced here: 231 us
  starting transfers between devices  174 us (75%)
  Pallas kernels  37.6 us (16%)
  waiting for transfers between devices  12.4 us (5%)
  local copies, waits for them, and re-layouts  4.9 us (2%)
    ppermute x26, starting transfers between devices, rotations(): got.append(lax.ppermute(value_of(d), axis, perm))  174 us
    pallas_call x1, Pallas kernels, body(): pl.pallas_call(functools.partial(backward_kernel, slots, planes, step_pla...  29.4 us
    ppermute x26, waiting for transfers between devices, rotations(): got.append(lax.ppermute(value_of(d), axis, perm))  12.4 us
    pallas_call x1, Pallas kernels, body(): pl.pallas_call(functools.partial(forward_kernel, slots, planes, step_plan...  5.86 us
  transfers between devices with their start and end apart: 26, of which 11 were waited for; matrix products, arithmetic and copies ran while one was open for 0% of the time, Pallas kernels for 1%

profile of v1, /device:TPU:0, one launch (start us, length us, event | category | flops | bytes accessed | tf_op | source)
XLA Modules:
  0.0 231.1 jit_solution(7967511837727540215)
XLA Ops:
  0.6 0.0 copy-start.4
  0.7 1.4 reduce_sum.9
  2.0 1.2 dynamic_slice.3
  3.2 2.0 concatenate.3.meta_ref
  5.3 0.9 copy-done.1
  6.2 0.7 copy-done.3
  6.9 0.0 copy-start.8
  6.9 0.0 copy-start.9
  6.9 0.0 copy-start.10
  6.9 5.9 %forward_modes.1 = (f32[96,128]{1,0:T(8,128)S(1)}, f32[96,128]{1,0:T(8,128)S(1)}, f32[96,128]{1,0:T(8,128)S(1)}, f32[96,128]{1,0:T(8,128)S(1)}) custom-call(s32[10]{0:T(128)S(1)} %concatenate.3.meta_ref, f32[384]{0:T(512)S(1)} %copy-done.3, bf16[1,6,12,48,48,128]{5,4,3,2,1,0:T(8,128)(2,1)} %f_ref.3, bf16[32,2304]{1,0:T(8,128)(2,1)S(1)} %copy-done.1), custom_call_target="tpu_custom_call" | custom-call | tf_op jit(solution)/shard_map/forward_modes/pallas_call | solution.py:372
  12.8 3.1 %collective-permute-start = (f32[96,128]{1,0:T(8,128)S(1)}, f32[96,128]{1,0:T(8,128)S(1)}, u32[]{:S(2)}, u32[]{:S(2)}) collective-permute-start(f32[96,128]{1,0:T(8,128)S(1)} %get-tuple-element.13), channel_id=1, source_target_pairs={{0,1},{1,2},{2,3},{3,0},{4,5},{5,6},{6,7},{7,4},{8,9},{9,10},{10,1... | collective-permute-start | bytes 147464 | tf_op jit(solution)/shard_map/ppermute | solution.py:332
  15.8 2.6 %collective-permute-start.1 = (f32[96,128]{1,0:T(8,128)S(1)}, f32[96,128]{1,0:T(8,128)S(1)}, u32[]{:S(2)}, u32[]{:S(2)}) collective-permute-start(f32[96,128]{1,0:T(8,128)S(1)} %get-tuple-element.14), channel_id=1, source_target_pairs={{0,2},{1,3},{2,0},{3,1},{4,6},{5,7},{6,4},{7,5},{8,10},{9,11},{10,... | collective-permute-start | bytes 147464 | tf_op jit(solution)/shard_map/ppermute | solution.py:332
  18.4 1.3 collective-permute-start.2
  19.8 0.2 collective-permute-done.refs_1_
  19.9 0.9 collective-permute-done.1.refs_2_
  20.8 2.3 collective-permute-done.2.refs_3_
  23.1 0.3 mix_modes.1
  23.4 1.4 collective-permute-start.10
  24.8 2.0 collective-permute-start.11
  26.8 0.5 collective-permute-start.12
  27.3 2.1 collective-permute-done.10.rest_1_
  29.3 0.7 collective-permute-done.11.rest_2_
  30.1 0.6 collective-permute-done.12.rest_3_
  30.7 29.4 %backward_modes.1 = (f32[128,128]{1,0:T(8,128)S(1)}, f32[128,128]{1,0:T(8,128)S(1)}, f32[128,128]{1,0:T(8,128)S(1)}, f32[128,128]{1,0:T(8,128)S(1)}) custom-call(s32[10]{0:T(128)S(1)} %concatenate.3.meta_ref, f32[384]{0:T(512)S(1)} %copy-done.4, bf16[1,6,12,48,48,128]{5,4,3,2,1,0:T(8,128)(2,1)} %f_ref.3, bf16[1,6,12,2304]{3,2,1,0:T(8,128)(2,1)S(1)} %copy-done.5, ...), custom_call_target="tpu_custom_call" | custom-call | flops 43486543872 | bytes 42467328 | tf_op jit(solution)/shard_map/backward_modes/pallas_call | solution.py:419
  60.1 1.1 collective-permute-start.13
  61.2 2.0 collective-permute-start.14
  63.1 1.1 collective-permute-start.15
  64.2 2.1 collective-permute-done.13.refs_1_
  66.3 1.4 collective-permute-done.14.refs_2_
  67.7 0.3 collective-permute-done.15.refs_3_
  68.0 23.6 %collective-permute-start.16 = (f32[128,128]{1,0:T(8,128)S(1)}, f32[128,128]{1,0:T(8,128)S(1)}, u32[]{:S(2)}, u32[]{:S(2)}) collective-permute-start(f32[128,128]{1,0:T(8,128)S(1)} %sum_shards.1.refs_8_.refs_0_), channel_id=1, source_target_pairs={{0,4},{4,8},{8,12},{12,16},{16,20},{20,24},{24,28},{28,0},{1,5},{5... | collective-permute-start | bytes 196616 | tf_op jit(solution)/shard_map/ppermute | solution.py:332
  91.6 1.5 collective-permute-start.17
  93.1 0.0 collective-permute-start.3
  93.1 118.6 %collective-permute-start.4 = (bf16[96,128]{1,0:T(8,128)(2,1)S(1)}, bf16[96,128]{1,0:T(8,128)(2,1)S(1)}, u32[]{:S(2)}, u32[]{:S(2)}) collective-permute-start(bf16[96,128]{1,0:T(8,128)(2,1)S(1)} %get-tuple-element.16.refs_0_), channel_id=1, source_target_pairs={{0,8},{4,12},{8,16},{12,20},{16,24},{20,28},{24,0},{28,4},{1,9},{5... | collective-permute-start | bytes 73736 | tf_op jit(solution)/shard_map/ppermute | solution.py:332
  211.7 0.0 collective-permute-start.18
  211.7 0.0 collective-permute-done.3.refs_1_
  211.7 3.1 %collective-permute-start.19 = (f32[128,128]{1,0:T(8,128)S(1)}, f32[128,128]{1,0:T(8,128)S(1)}, u32[]{:S(2)}, u32[]{:S(2)}) collective-permute-start(f32[128,128]{1,0:T(8,128)S(1)} %sum_shards.1.refs_8_.refs_0_), channel_id=1, source_target_pairs={{0,16},{4,20},{8,24},{12,28},{16,0},{20,4},{24,8},{28,12},{1,17},{... | collective-permute-start | bytes 196616 | tf_op jit(solution)/shard_map/ppermute | solution.py:332
  214.8 0.0 collective-permute-done.4.refs_2_
  214.8 0.2 collective-permute-start.20
  215.1 0.0 collective-permute-done.16.refs_9_.refs_1_
  215.1 1.4 collective-permute-start.21
  216.4 0.0 collective-permute-done.17.refs_10_.refs_2_
  216.4 1.6 collective-permute-start.22
  218.1 0.0 collective-permute-done.18.refs_11_.refs_3_
  218.1 0.0 collective-permute-start.5
  218.1 0.0 collective-permute-done.19.refs_12_.refs_4_
  218.1 1.3 collective-permute-start.6
  219.4 0.0 collective-permute-done.20.refs_13_.refs_5_
  219.4 1.4 collective-permute-start.7
  220.8 0.0 collective-permute-done.21.refs_14_.refs_6_
  220.8 2.1 collective-permute-start.8
  222.9 0.0 collective-permute-done.22.refs_15_.refs_7_
  222.9 0.0 collective-permute-start.9
  222.9 0.0 collective-permute-done.5.refs_3_
  222.9 1.3 collective-permute-start.23
  224.3 0.0 collective-permute-done.6.refs_4_
  224.3 2.4 %collective-permute-start.24 = (f32[32,128]{1,0:T(8,128)S(1)}, f32[32,128]{1,0:T(8,128)S(1)}, u32[]{:S(2)}, u32[]{:S(2)}) collective-permute-start(f32[32,128]{1,0:T(8,128)S(1)} %sum_local.1.refs_0_), channel_id=1, source_target_pairs={{0,2},{1,3},{2,0},{3,1},{4,6},{5,7},{6,4},{7,5},{8,10},{9,11},{10,... | collective-permute-start | bytes 49160 | tf_op jit(solution)/shard_map/ppermute | solution.py:332
  226.7 0.0 collective-permute-done.7.refs_5_
  226.7 0.3 collective-permute-start.25
  227.0 1.5 weight_grad.1
  228.5 0.0 collective-permute-done.23.refs_1_
  228.5 0.4 collective-permute-done.24.refs_2_
  228.9 1.5 collective-permute-done.25.refs_3_
  230.4 0.6 place_local.1
  (20 shorter events, 0.1 us)
Async XLA Ops:
  0.6 30.0 %copy-start.4 = (f32[384]{0:T(512)S(1)}, f32[384]{0:T(512)}, u32[]{:S(2)}) copy-start(f32[384]{0:T(512)} %constant.25.clone.xtab_ref) | copy-start | bytes 4612
  0.6 22.5 %copy-start = (bf16[8,2,128,128]{3,2,1,0:T(8,128)(2,1)S(1)}, bf16[8,2,128,128]{3,2,1,0:T(8,128)(2,1)}, u32[]{:S(2)}) copy-start(bf16[8,2,128,128]{3,2,1,0:T(8,128)(2,1)} %refs_4_.1) | copy-start | bytes 1572868
  5.3 0.9 copy-start.1
  6.2 0.7 copy-start.3
  6.9 23.8 %copy-start.2 = (bf16[32,2304]{1,0:T(8,128)(2,1)S(1)}, bf16[32,2304]{1,0:T(8,128)(2,1)}, u32[]{:S(2)}) copy-start(bf16[32,2304]{1,0:T(8,128)(2,1)} %constant.26.clone.basis_ref.rest_7_) | copy-start | bytes 442372
  6.9 23.8 %copy-start.5 = (bf16[1,6,12,2304]{3,2,1,0:T(8,128)(2,1)S(1)}, bf16[1,6,12,2304]{3,2,1,0:T(8,128)(2,1)}, u32[]{:S(2)}) copy-start(bf16[1,6,12,2304]{3,2,1,0:T(8,128)(2,1)} %t_ref.1) | copy-start | bytes 995332
  6.9 23.8 %copy-start.6 = (bf16[128,128]{1,0:T(8,128)(2,1)S(1)}, bf16[128,128]{1,0:T(8,128)(2,1)}, u32[]{:S(2)}) copy-start(bf16[128,128]{1,0:T(8,128)(2,1)} %rest_4_.1) | copy-start | bytes 98308
  6.9 23.8 %copy-start.7 = (f32[128]{0:T(128)S(1)}, f32[128]{0:T(128)}, u32[]{:S(2)}) copy-start(f32[128]{0:T(128)} %param.18) | copy-start | bytes 1540
  6.9 23.8 %copy-start.8 = (bf16[2304,128]{1,0:T(8,128)(2,1)S(1)}, bf16[2304,128]{1,0:T(8,128)(2,1)}, u32[]{:S(2)}) copy-start(bf16[2304,128]{1,0:T(8,128)(2,1)} %constant.27.clone.rest_6_) | copy-start | bytes 1769476
  6.9 23.8 %copy-start.9 = (bf16[256,128]{1,0:T(8,128)(2,1)S(1)}, bf16[256,128]{1,0:T(8,128)(2,1)}, u32[]{:S(2)}) copy-start(bf16[256,128]{1,0:T(8,128)(2,1)} %constant.29.clone.rest_9_) | copy-start | bytes 196612
  6.9 23.8 %copy-start.10 = (bf16[128,128]{1,0:T(8,128)(2,1)S(1)}, bf16[128,128]{1,0:T(8,128)(2,1)}, u32[]{:S(2)}) copy-start(bf16[128,128]{1,0:T(8,128)(2,1)} %constant.28.clone.rest_8_) | copy-start | bytes 98308
  12.8 7.2 %collective-permute-start = (f32[96,128]{1,0:T(8,128)S(1)}, f32[96,128]{1,0:T(8,128)S(1)}, u32[]{:S(2)}, u32[]{:S(2)}) collective-permute-start(f32[96,128]{1,0:T(8,128)S(1)} %get-tuple-element.13), channel_id=1, source_target_pairs={{0,1},{1,2},{2,3},{3,0},{4,5},{5,6},{6,7},{7,4},{8,9},{9,10},{10,1... | collective-permute-start | bytes 147464 | tf_op jit(solution)/shard_map/ppermute | solution.py:332
  15.8 5.0 %collective-permute-start.1 = (f32[96,128]{1,0:T(8,128)S(1)}, f32[96,128]{1,0:T(8,128)S(1)}, u32[]{:S(2)}, u32[]{:S(2)}) collective-permute-start(f32[96,128]{1,0:T(8,128)S(1)} %get-tuple-element.14), channel_id=1, source_target_pairs={{0,2},{1,3},{2,0},{3,1},{4,6},{5,7},{6,4},{7,5},{8,10},{9,11},{10,... | collective-permute-start | bytes 147464 | tf_op jit(solution)/shard_map/ppermute | solution.py:332
  18.4 4.7 %collective-permute-start.2 = (f32[96,128]{1,0:T(8,128)S(1)}, f32[96,128]{1,0:T(8,128)S(1)}, u32[]{:S(2)}, u32[]{:S(2)}) collective-permute-start(f32[96,128]{1,0:T(8,128)S(1)} %get-tuple-element.15), channel_id=1, source_target_pairs={{0,3},{1,0},{2,1},{3,2},{4,7},{5,4},{6,5},{7,6},{8,11},{9,8},{10,9... | collective-permute-start | bytes 147464 | tf_op jit(solution)/shard_map/ppermute | solution.py:332
  23.4 5.9 %collective-permute-start.10 = (bf16[96,128]{1,0:T(8,128)(2,1)S(1)}, bf16[96,128]{1,0:T(8,128)(2,1)S(1)}, u32[]{:S(2)}, u32[]{:S(2)}) collective-permute-start(bf16[96,128]{1,0:T(8,128)(2,1)S(1)} %get-tuple-element.17.rest_0_), channel_id=1, source_target_pairs={{0,1},{1,2},{2,3},{3,0},{4,5},{5,6},{6,7},{7,4},{8,9},{9,10},{10,1... | collective-permute-start | bytes 73736 | tf_op jit(solution)/shard_map/ppermute | solution.py:332
  24.8 5.3 %collective-permute-start.11 = (bf16[96,128]{1,0:T(8,128)(2,1)S(1)}, bf16[96,128]{1,0:T(8,128)(2,1)S(1)}, u32[]{:S(2)}, u32[]{:S(2)}) collective-permute-start(bf16[96,128]{1,0:T(8,128)(2,1)S(1)} %get-tuple-element.17.rest_0_), channel_id=1, source_target_pairs={{0,2},{1,3},{2,0},{3,1},{4,6},{5,7},{6,4},{7,5},{8,10},{9,11},{10,... | collective-permute-start | bytes 73736 | tf_op jit(solution)/shard_map/ppermute | solution.py:332
  26.8 3.8 %collective-permute-start.12 = (bf16[96,128]{1,0:T(8,128)(2,1)S(1)}, bf16[96,128]{1,0:T(8,128)(2,1)S(1)}, u32[]{:S(2)}, u32[]{:S(2)}) collective-permute-start(bf16[96,128]{1,0:T(8,128)(2,1)S(1)} %get-tuple-element.17.rest_0_), channel_id=1, source_target_pairs={{0,3},{1,0},{2,1},{3,2},{4,7},{5,4},{6,5},{7,6},{8,11},{9,8},{10,9... | collective-permute-start | bytes 73736 | tf_op jit(solution)/shard_map/ppermute | solution.py:332
  60.1 6.2 %collective-permute-start.13 = (f32[128,128]{1,0:T(8,128)S(1)}, f32[128,128]{1,0:T(8,128)S(1)}, u32[]{:S(2)}, u32[]{:S(2)}) collective-permute-start(f32[128,128]{1,0:T(8,128)S(1)} %get-tuple-element.19), channel_id=1, source_target_pairs={{0,1},{1,2},{2,3},{3,0},{4,5},{5,6},{6,7},{7,4},{8,9},{9,10},{10,1... | collective-permute-start | bytes 196616 | tf_op jit(solution)/shard_map/ppermute | solution.py:332
  61.2 6.5 %collective-permute-start.14 = (f32[128,128]{1,0:T(8,128)S(1)}, f32[128,128]{1,0:T(8,128)S(1)}, u32[]{:S(2)}, u32[]{:S(2)}) collective-permute-start(f32[128,128]{1,0:T(8,128)S(1)} %get-tuple-element.20), channel_id=1, source_target_pairs={{0,2},{1,3},{2,0},{3,1},{4,6},{5,7},{6,4},{7,5},{8,10},{9,11},{10,... | collective-permute-start | bytes 196616 | tf_op jit(solution)/shard_map/ppermute | solution.py:332
  63.1 4.9 %collective-permute-start.15 = (f32[128,128]{1,0:T(8,128)S(1)}, f32[128,128]{1,0:T(8,128)S(1)}, u32[]{:S(2)}, u32[]{:S(2)}) collective-permute-start(f32[128,128]{1,0:T(8,128)S(1)} %get-tuple-element.21), channel_id=1, source_target_pairs={{0,3},{1,0},{2,1},{3,2},{4,7},{5,4},{6,5},{7,6},{8,11},{9,8},{10,9... | collective-permute-start | bytes 196616 | tf_op jit(solution)/shard_map/ppermute | solution.py:332
  68.0 147.0 %collective-permute-start.16 = (f32[128,128]{1,0:T(8,128)S(1)}, f32[128,128]{1,0:T(8,128)S(1)}, u32[]{:S(2)}, u32[]{:S(2)}) collective-permute-start(f32[128,128]{1,0:T(8,128)S(1)} %sum_shards.1.refs_8_.refs_0_), channel_id=1, source_target_pairs={{0,4},{4,8},{8,12},{12,16},{16,20},{20,24},{24,28},{28,0},{1,5},{5... | collective-permute-start | bytes 196616 | tf_op jit(solution)/shard_map/ppermute | solution.py:332
  91.6 124.9 %collective-permute-start.17 = (f32[128,128]{1,0:T(8,128)S(1)}, f32[128,128]{1,0:T(8,128)S(1)}, u32[]{:S(2)}, u32[]{:S(2)}) collective-permute-start(f32[128,128]{1,0:T(8,128)S(1)} %sum_shards.1.refs_8_.refs_0_), channel_id=1, source_target_pairs={{0,8},{4,12},{8,16},{12,20},{16,24},{20,28},{24,0},{28,4},{1,9},{5... | collective-permute-start | bytes 196616 | tf_op jit(solution)/shard_map/ppermute | solution.py:332
  93.1 118.6 %collective-permute-start.3 = (bf16[96,128]{1,0:T(8,128)(2,1)S(1)}, bf16[96,128]{1,0:T(8,128)(2,1)S(1)}, u32[]{:S(2)}, u32[]{:S(2)}) collective-permute-start(bf16[96,128]{1,0:T(8,128)(2,1)S(1)} %get-tuple-element.16.refs_0_), channel_id=1, source_target_pairs={{0,4},{4,8},{8,12},{12,16},{16,20},{20,24},{24,28},{28,0},{1,5},{5... | collective-permute-start | bytes 73736 | tf_op jit(solution)/shard_map/ppermute | solution.py:332
  93.1 121.7 %collective-permute-start.4 = (bf16[96,128]{1,0:T(8,128)(2,1)S(1)}, bf16[96,128]{1,0:T(8,128)(2,1)S(1)}, u32[]{:S(2)}, u32[]{:S(2)}) collective-permute-start(bf16[96,128]{1,0:T(8,128)(2,1)S(1)} %get-tuple-element.16.refs_0_), channel_id=1, source_target_pairs={{0,8},{4,12},{8,16},{12,20},{16,24},{20,28},{24,0},{28,4},{1,9},{5... | collective-permute-start | bytes 73736 | tf_op jit(solution)/shard_map/ppermute | solution.py:332
  211.7 6.4 %collective-permute-start.18 = (f32[128,128]{1,0:T(8,128)S(1)}, f32[128,128]{1,0:T(8,128)S(1)}, u32[]{:S(2)}, u32[]{:S(2)}) collective-permute-start(f32[128,128]{1,0:T(8,128)S(1)} %sum_shards.1.refs_8_.refs_0_), channel_id=1, source_target_pairs={{0,12},{4,16},{8,20},{12,24},{16,28},{20,0},{24,4},{28,8},{1,13},{... | collective-permute-start | bytes 196616 | tf_op jit(solution)/shard_map/ppermute | solution.py:332
  211.7 6.4 %collective-permute-start.19 = (f32[128,128]{1,0:T(8,128)S(1)}, f32[128,128]{1,0:T(8,128)S(1)}, u32[]{:S(2)}, u32[]{:S(2)}) collective-permute-start(f32[128,128]{1,0:T(8,128)S(1)} %sum_shards.1.refs_8_.refs_0_), channel_id=1, source_target_pairs={{0,16},{4,20},{8,24},{12,28},{16,0},{20,4},{24,8},{28,12},{1,17},{... | collective-permute-start | bytes 196616 | tf_op jit(solution)/shard_map/ppermute | solution.py:332
  214.8 4.6 %collective-permute-start.20 = (f32[128,128]{1,0:T(8,128)S(1)}, f32[128,128]{1,0:T(8,128)S(1)}, u32[]{:S(2)}, u32[]{:S(2)}) collective-permute-start(f32[128,128]{1,0:T(8,128)S(1)} %sum_shards.1.refs_8_.refs_0_), channel_id=1, source_target_pairs={{0,20},{4,24},{8,28},{12,0},{16,4},{20,8},{24,12},{28,16},{1,21},{... | collective-permute-start | bytes 196616 | tf_op jit(solution)/shard_map/ppermute | solution.py:332
  215.1 5.7 %collective-permute-start.21 = (f32[128,128]{1,0:T(8,128)S(1)}, f32[128,128]{1,0:T(8,128)S(1)}, u32[]{:S(2)}, u32[]{:S(2)}) collective-permute-start(f32[128,128]{1,0:T(8,128)S(1)} %sum_shards.1.refs_8_.refs_0_), channel_id=1, source_target_pairs={{0,24},{4,28},{8,0},{12,4},{16,8},{20,12},{24,16},{28,20},{1,25},{... | collective-permute-start | bytes 196616 | tf_op jit(solution)/shard_map/ppermute | solution.py:332
  216.4 6.4 %collective-permute-start.22 = (f32[128,128]{1,0:T(8,128)S(1)}, f32[128,128]{1,0:T(8,128)S(1)}, u32[]{:S(2)}, u32[]{:S(2)}) collective-permute-start(f32[128,128]{1,0:T(8,128)S(1)} %sum_shards.1.refs_8_.refs_0_), channel_id=1, source_target_pairs={{0,28},{4,0},{8,4},{12,8},{16,12},{20,16},{24,20},{28,24},{1,29},{... | collective-permute-start | bytes 196616 | tf_op jit(solution)/shard_map/ppermute | solution.py:332
  218.1 4.8 %collective-permute-start.5 = (bf16[96,128]{1,0:T(8,128)(2,1)S(1)}, bf16[96,128]{1,0:T(8,128)(2,1)S(1)}, u32[]{:S(2)}, u32[]{:S(2)}) collective-permute-start(bf16[96,128]{1,0:T(8,128)(2,1)S(1)} %get-tuple-element.16.refs_0_), channel_id=1, source_target_pairs={{0,12},{4,16},{8,20},{12,24},{16,28},{20,0},{24,4},{28,8},{1,13},{... | collective-permute-start | bytes 73736 | tf_op jit(solution)/shard_map/ppermute | solution.py:332
  218.1 6.2 %collective-permute-start.6 = (bf16[96,128]{1,0:T(8,128)(2,1)S(1)}, bf16[96,128]{1,0:T(8,128)(2,1)S(1)}, u32[]{:S(2)}, u32[]{:S(2)}) collective-permute-start(bf16[96,128]{1,0:T(8,128)(2,1)S(1)} %get-tuple-element.16.refs_0_), channel_id=1, source_target_pairs={{0,16},{4,20},{8,24},{12,28},{16,0},{20,4},{24,8},{28,12},{1,17},{... | collective-permute-start | bytes 73736 | tf_op jit(solution)/shard_map/ppermute | solution.py:332
  219.4 7.3 %collective-permute-start.7 = (bf16[96,128]{1,0:T(8,128)(2,1)S(1)}, bf16[96,128]{1,0:T(8,128)(2,1)S(1)}, u32[]{:S(2)}, u32[]{:S(2)}) collective-permute-start(bf16[96,128]{1,0:T(8,128)(2,1)S(1)} %get-tuple-element.16.refs_0_), channel_id=1, source_target_pairs={{0,20},{4,24},{8,28},{12,0},{16,4},{20,8},{24,12},{28,16},{1,21},{... | collective-permute-start | bytes 73736 | tf_op jit(solution)/shard_map/ppermute | solution.py:332
  220.8 6.2 %collective-permute-start.8 = (bf16[96,128]{1,0:T(8,128)(2,1)S(1)}, bf16[96,128]{1,0:T(8,128)(2,1)S(1)}, u32[]{:S(2)}, u32[]{:S(2)}) collective-permute-start(bf16[96,128]{1,0:T(8,128)(2,1)S(1)} %get-tuple-element.16.refs_0_), channel_id=1, source_target_pairs={{0,24},{4,28},{8,0},{12,4},{16,8},{20,12},{24,16},{28,20},{1,25},{... | collective-permute-start | bytes 73736 | tf_op jit(solution)/shard_map/ppermute | solution.py:332
  222.9 4.1 %collective-permute-start.9 = (bf16[96,128]{1,0:T(8,128)(2,1)S(1)}, bf16[96,128]{1,0:T(8,128)(2,1)S(1)}, u32[]{:S(2)}, u32[]{:S(2)}) collective-permute-start(bf16[96,128]{1,0:T(8,128)(2,1)S(1)} %get-tuple-element.16.refs_0_), channel_id=1, source_target_pairs={{0,28},{4,0},{8,4},{12,8},{16,12},{20,16},{24,20},{28,24},{1,29},{... | collective-permute-start | bytes 73736 | tf_op jit(solution)/shard_map/ppermute | solution.py:332
  222.9 5.6 %collective-permute-start.23 = (f32[32,128]{1,0:T(8,128)S(1)}, f32[32,128]{1,0:T(8,128)S(1)}, u32[]{:S(2)}, u32[]{:S(2)}) collective-permute-start(f32[32,128]{1,0:T(8,128)S(1)} %sum_local.1.refs_0_), channel_id=1, source_target_pairs={{0,1},{1,2},{2,3},{3,0},{4,5},{5,6},{6,7},{7,4},{8,9},{9,10},{10,1... | collective-permute-start | bytes 49160 | tf_op jit(solution)/shard_map/ppermute | solution.py:332
  224.3 4.7 %collective-permute-start.24 = (f32[32,128]{1,0:T(8,128)S(1)}, f32[32,128]{1,0:T(8,128)S(1)}, u32[]{:S(2)}, u32[]{:S(2)}) collective-permute-start(f32[32,128]{1,0:T(8,128)S(1)} %sum_local.1.refs_0_), channel_id=1, source_target_pairs={{0,2},{1,3},{2,0},{3,1},{4,6},{5,7},{6,4},{7,5},{8,10},{9,11},{10,... | collective-permute-start | bytes 49160 | tf_op jit(solution)/shard_map/ppermute | solution.py:332
  226.7 3.7 %collective-permute-start.25 = (f32[32,128]{1,0:T(8,128)S(1)}, f32[32,128]{1,0:T(8,128)S(1)}, u32[]{:S(2)}, u32[]{:S(2)}) collective-permute-start(f32[32,128]{1,0:T(8,128)S(1)} %sum_local.1.refs_0_), channel_id=1, source_target_pairs={{0,3},{1,0},{2,1},{3,2},{4,7},{5,4},{6,5},{7,6},{8,11},{9,8},{10,9... | collective-permute-start | bytes 49160 | tf_op jit(solution)/shard_map/ppermute | solution.py:332

commit v2 on v1

--- a/solution.py
+++ b/solution.py
@@ -124,7 +124,7 @@
     specs = rest[:MX]
     w_ref, proj_ref, inv_ref, basis_ref, eye_ref, ones_ref = rest[MX : MX + 6]
     outs = rest[MX + 6 : 2 * MX + 6]
-    rhs_ref, d_ref, total_ref, q_ref, t16_ref, spec_ref = rest[2 * MX + 6 :]
+    rhs_ref, pre_ref, slope_ref, both_ref, d_ref, total_ref, q_ref, t16_ref, spec_ref = rest[2 * MX + 6 :]
     place = scalar_places(slots)
     g, blk = pl.program_id(0), pl.program_id(1)
     blocks = planes // step_planes
@@ -134,14 +134,14 @@
     cell0 = meta_ref[place["first"]]
     cells = f_ref.shape[3] * f_ref.shape[4]
     third = cells // 3
-    steps = third // rows_step
-    subs = rows_step // 128
+    unroll = 2 if step_planes % 2 == 0 else 1
 
     @pl.when((g == 0) & (blk == 0))
     def _():
         total_ref[...] = jnp.zeros_like(total_ref)
-        rhs_ref[0:128, :] = w_ref[...]
-        rhs_ref[128:256, :] = jnp.zeros((128, 128), bf16)
+        for n in range(2):
+            rhs_ref[n, 0:128, :] = w_ref[...]
+            rhs_ref[n, 128:256, :] = jnp.zeros((128, 128), bf16)
 
     @pl.when(live)
     def _():
@@ -158,8 +158,7 @@
         proj = proj_ref[...]
         proj_scaled = proj / jnp.full((1, 128), count, f32)
 
-        def plane(p, carry):
-            a = blk * step_planes + p
+        def first_rows(a, rhs):
             re = jnp.zeros((8, 128), f32)
             im = jnp.zeros((8, 128), f32)
             for d in range(MX):
@@ -174,50 +173,69 @@
             first = jnp.concatenate([re, im], axis=0) * scale
             high = first.astype(bf16)
             low = (first - high.astype(f32)).astype(bf16)
-            rhs_ref[128:144, :] = high
-            rhs_ref[144:160, :] = high
-            rhs_ref[160:176, :] = low
-            rhs_ref[176:192, :] = low
-            field = f_ref[0, 0, p].reshape(cells, 128)
-
-            def stage_one(r0):
-                part = slice(r0, r0 + rows_step)
+            rhs[128:144, :] = high
+            rhs[144:160, :] = high
+            rhs[160:176, :] = low
+            rhs[176:192, :] = low
+
+        def planes_together(n, carry):
+            units = [(u, k) for u in range(unroll) for k in range(3)]
+            q = [jnp.zeros((32, 128), f32) for _ in range(unroll)]
+
+            def before(s):
+                u, k = units[s]
+                rhs = rhs_ref.at[u % 2]
+                if k == 0:
+                    first_rows(blk * step_planes + n * unroll + u, rhs)
+                field = f_ref[0, 0, n * unroll + u].reshape(cells, 128)
+                part = slice(k * third, (k + 1) * third)
                 lhs = jnp.concatenate([field[part], inv_ref[part, :]], axis=1)
-                pre = jnp.dot(lhs, rhs_ref[...], preferred_element_type=f32)
-                cdf, bell = gelu_parts(pre)
-                slope = (cdf + pre * bell * inv_root_two_pi) * proj_scaled
-                active = (pre * cdf * proj).astype(bf16)
-                wanted = []
-                for j in range(subs):
-                    at = r0 + j * 128
-                    line = t16_ref[a, :, at : at + 128]
-                    wanted.extend(line * eye_ref[n : n + 16, :] for n in range(0, 128, 16))
-                wanted = jnp.concatenate(wanted, axis=0)
-                return jnp.concatenate([active, wanted], axis=1), slope
-
-            def stage_two(r0, both, slope):
-                resid = jnp.dot(both, ones_ref[...], preferred_element_type=f32)
-                d_ref[r0 : r0 + rows_step, :] = (resid * slope).astype(bf16)
-
-            q = jnp.zeros((32, 128), f32)
-            for k in range(3):
-                waiting = None
-                for s in range(steps):
-                    r0 = k * third + s * rows_step
-                    made = stage_one(r0)
-                    if waiting is not None:
-                        stage_two(*waiting)
-                    waiting = (r0,) + made
-                stage_two(*waiting)
+                pre_ref[s % 2] = jnp.dot(lhs, rhs[...], preferred_element_type=f32)
+
+            def elementwise(s):
+                u, k = units[s]
+                a = blk * step_planes + n * unroll + u
+                for r0 in range(0, third, rows_step):
+                    rows = slice(r0, r0 + rows_step)
+                    pre = pre_ref[s % 2, rows, :]
+                    cdf, bell = gelu_parts(pre)
+                    slope_ref[s % 2, rows, :] = (cdf + pre * bell * inv_root_two_pi) * proj_scaled
+                    both_ref[s % 2, rows, 0:128] = (pre * cdf * proj).astype(bf16)
+                    for r1 in range(r0, r0 + rows_step, 16):
+                        n1 = r1 % 128
+                        at = k * third + r1 - n1
+                        line = t16_ref[a, :, at : at + 128]
+                        both_ref[s % 2, r1 : r1 + 16, 128:256] = line * eye_ref[n1 : n1 + 16, :]
+
+            def after(s):
+                resid = jnp.dot(both_ref[s % 2], ones_ref[...], preferred_element_type=f32)
+                for r0 in range(0, third, rows_step):
+                    rows = slice(r0, r0 + rows_step)
+                    d_ref[s % 2, rows, :] = (resid[rows] * slope_ref[s % 2, rows, :]).astype(bf16)
+
+            def last(s):
+                u, k = units[s]
+                field = f_ref[0, 0, n * unroll + u].reshape(cells, 128)
                 part = slice(k * third, (k + 1) * third)
                 lhs = jnp.concatenate([field[part].T, basis_ref[:, part]], axis=0)
-                sums = jnp.dot(lhs, d_ref[part, :], preferred_element_type=f32)
+                sums = jnp.dot(lhs, d_ref[s % 2], preferred_element_type=f32)
                 total_ref[...] += sums[0:128]
-                q = q + sums[128:160]
-            q_ref[a] = q[0:16] + q[16:32]
+                q[u] = q[u] + sums[128:160]
+                if k == 2:
+                    q_ref[blk * step_planes + n * unroll + u] = q[u][0:16] + q[u][16:32]
+
+            for s in range(len(units) + 3):
+                if s >= 3:
+                    last(s - 3)
+                if 0 <= s - 2 < len(units):
+                    after(s - 2)
+                if 0 <= s - 1 < len(units):
+                    elementwise(s - 1)
+                if s < len(units):
+                    before(s)
             return carry
 
-        lax.fori_loop(0, step_planes, plane, 0)
+        lax.fori_loop(0, step_planes // unroll, planes_together, 0)
 
         @pl.when(blk == blocks - 1)
         def _():
@@ -417,7 +435,7 @@
     ones = np.ones((128, 128), ml_dtypes.bfloat16)
     ones = np.concatenate([ones, -ones], axis=0)
     results = pl.pallas_call(
-        functools.partial(backward_kernel, slots, planes, step_planes, 256, float(MODES) ** (-0.5)),
+        functools.partial(backward_kernel, slots, planes, step_planes, 64, float(MODES) ** (-0.5)),
         grid_spec=pltpu.PrefetchScalarGridSpec(
             num_scalar_prefetch=2,
             grid=(slots, blocks),
@@ -433,8 +451,11 @@
             ],
             out_specs=[fixed(part_rows + local_rows, width)] * MX,
             scratch_shapes=[
-                pltpu.VMEM((256, width), bf16),
-                pltpu.VMEM((cells, width), bf16),
+                pltpu.VMEM((2, 256, width), bf16),
+                pltpu.VMEM((2, cells // 3, width), f32),
+                pltpu.VMEM((2, cells // 3, width), f32),
+                pltpu.VMEM((2, cells // 3, 2 * width), bf16),
+                pltpu.VMEM((2, cells // 3, width), bf16),
                 pltpu.VMEM((width, width), f32),
                 pltpu.VMEM((planes, 16, width), f32),
                 pltpu.VMEM((planes, 16, cells), bf16),

time: 232 us -> 213 us (0.918); the launches traced: 231 us -> 215 us
  starting transfers between devices: 174 us -> 31 us
  Pallas kernels: 37.6 us -> 162 us
  waiting for transfers between devices: 12.4 us -> 14.9 us
    ppermute x26, starting transfers between devices: 174 us -> 31 us  [rotations(): got.append(lax.ppermute(value_of(d), axis, perm))]
    pallas_call x1, Pallas kernels: 29.4 us -> 137 us  [body(): pl.pallas_call(functools.partial(backward_kernel, slots, planes, step_pla...]
    pallas_call x1, Pallas kernels: 5.86 us -> 22.6 us  [body(): pl.pallas_call(functools.partial(forward_kernel, slots, planes, step_plan...]
    ppermute x26, waiting for transfers between devices: 12.4 us -> 14.9 us  [rotations(): got.append(lax.ppermute(value_of(d), axis, perm))]
  transfers between devices with their start and end apart: 26 -> 26, of which waited for: 11 -> 13; matrix products, arithmetic and copies ran while one was open for 0% -> 0% of each run, Pallas kernels for 1% -> 1%
where the time goes in v2:
time: 213 us; the launch traced here: 215 us
  Pallas kernels  162 us (76%)
  starting transfers between devices  31 us (15%)
  waiting for transfers between devices  14.9 us (7%)
  local copies, waits for them, and re-layouts  4.9 us (2%)
    pallas_call x1, Pallas kernels, body(): pl.pallas_call(functools.partial(backward_kernel, slots, planes, step_pla...  137 us
    ppermute x26, starting transfers between devices, rotations(): got.append(lax.ppermute(value_of(d), axis, perm))  31 us
    pallas_call x1, Pallas kernels, body(): pl.pallas_call(functools.partial(forward_kernel, slots, planes, step_plan...  22.6 us
    ppermute x26, waiting for transfers between devices, rotations(): got.append(lax.ppermute(value_of(d), axis, perm))  14.9 us
  transfers between devices with their start and end apart: 26, of which 13 were waited for; matrix products, arithmetic and copies ran while one was open for 0% of the time, Pallas kernels for 1%

profile of v2, /device:TPU:0, one launch (start us, length us, event | category | flops | bytes accessed | tf_op | source)
XLA Modules:
  0.0 215.2 jit_solution(15231610723699093511)
XLA Ops:
  0.6 0.0 copy-start.4
  0.7 1.4 reduce_sum.9
  2.0 1.2 dynamic_slice.3
  3.2 2.0 concatenate.3.meta_ref
  5.3 0.9 copy-done.1
  6.2 0.7 copy-done.3
  6.9 0.0 copy-start.8
  6.9 0.0 copy-start.9
  6.9 0.0 copy-start.10
  6.9 22.6 %forward_modes.1 = (f32[96,128]{1,0:T(8,128)S(1)}, f32[96,128]{1,0:T(8,128)S(1)}, f32[96,128]{1,0:T(8,128)S(1)}, f32[96,128]{1,0:T(8,128)S(1)}) custom-call(s32[10]{0:T(128)S(1)} %concatenate.3.meta_ref, f32[384]{0:T(512)S(1)} %copy-done.3, bf16[1,6,12,48,48,128]{5,4,3,2,1,0:T(8,128)(2,1)} %f_ref.3, bf16[32,2304]{1,0:T(8,128)(2,1)S(1)} %copy-done.1), custom_call_target="tpu_custom_call" | custom-call | tf_op jit(solution)/shard_map/forward_modes/pallas_call | solution.py:390
  29.5 3.1 %collective-permute-start = (f32[96,128]{1,0:T(8,128)S(1)}, f32[96,128]{1,0:T(8,128)S(1)}, u32[]{:S(2)}, u32[]{:S(2)}) collective-permute-start(f32[96,128]{1,0:T(8,128)S(1)} %get-tuple-element.13), channel_id=1, source_target_pairs={{0,1},{1,2},{2,3},{3,0},{4,5},{5,6},{6,7},{7,4},{8,9},{9,10},{10,1... | collective-permute-start | bytes 147464 | tf_op jit(solution)/shard_map/ppermute | solution.py:350
  32.6 2.6 %collective-permute-start.1 = (f32[96,128]{1,0:T(8,128)S(1)}, f32[96,128]{1,0:T(8,128)S(1)}, u32[]{:S(2)}, u32[]{:S(2)}) collective-permute-start(f32[96,128]{1,0:T(8,128)S(1)} %get-tuple-element.14), channel_id=1, source_target_pairs={{0,2},{1,3},{2,0},{3,1},{4,6},{5,7},{6,4},{7,5},{8,10},{9,11},{10,... | collective-permute-start | bytes 147464 | tf_op jit(solution)/shard_map/ppermute | solution.py:350
  35.2 1.3 collective-permute-start.2
  36.5 0.2 collective-permute-done.refs_1_
  36.7 0.9 collective-permute-done.1.refs_2_
  37.6 1.7 collective-permute-done.2.refs_3_
  39.3 0.3 mix_modes.1
  39.5 0.5 collective-permute-start.10
  40.0 3.3 %collective-permute-start.11 = (bf16[96,128]{1,0:T(8,128)(2,1)S(1)}, bf16[96,128]{1,0:T(8,128)(2,1)S(1)}, u32[]{:S(2)}, u32[]{:S(2)}) collective-permute-start(bf16[96,128]{1,0:T(8,128)(2,1)S(1)} %get-tuple-element.17.rest_0_), channel_id=1, source_target_pairs={{0,2},{1,3},{2,0},{3,1},{4,6},{5,7},{6,4},{7,5},{8,10},{9,11},{10,... | collective-permute-start | bytes 73736 | tf_op jit(solution)/shard_map/ppermute | solution.py:350
  43.3 0.1 collective-permute-start.12
  43.4 1.9 collective-permute-done.10.rest_1_
  45.3 0.3 collective-permute-done.11.rest_2_
  45.6 1.5 collective-permute-done.12.rest_3_
  47.2 137.2 %backward_modes.1 = (f32[128,128]{1,0:T(8,128)S(1)}, f32[128,128]{1,0:T(8,128)S(1)}, f32[128,128]{1,0:T(8,128)S(1)}, f32[128,128]{1,0:T(8,128)S(1)}) custom-call(s32[10]{0:T(128)S(1)} %concatenate.3.meta_ref, f32[384]{0:T(512)S(1)} %copy-done.4, bf16[1,6,12,48,48,128]{5,4,3,2,1,0:T(8,128)(2,1)} %f_ref.3, bf16[1,6,12,2304]{3,2,1,0:T(8,128)(2,1)S(1)} %copy-done.5, ...), custom_call_target="tpu_custom_call" | custom-call | flops 43486543872 | bytes 42467328 | tf_op jit(solution)/shard_map/backward_modes/pallas_call | solution.py:437
  184.4 0.7 collective-permute-start.13
  185.1 1.9 collective-permute-start.14
  187.1 1.2 collective-permute-start.15
  188.3 2.3 %collective-permute-done.13.refs_1_ = f32[128,128]{1,0:T(8,128)S(1)} collective-permute-done((f32[128,128]{1,0:T(8,128)S(1)}, f32[128,128]{1,0:T(8,128)S(1)}, u32[]{:S(2)}, u32[]{:S(2)}) %collective-permute-start.13) | collective-permute-done | bytes 65568 | tf_op jit(solution)/shard_map/ppermute | solution.py:350
  190.6 1.1 collective-permute-done.14.refs_2_
  191.7 0.0 collective-permute-done.15.refs_3_
  191.7 0.1 collective-permute-start.16
  191.8 0.1 collective-permute-start.17
  191.9 0.1 collective-permute-start.3
  191.9 0.1 collective-permute-start.4
  192.0 4.2 %collective-permute-start.18 = (f32[128,128]{1,0:T(8,128)S(1)}, f32[128,128]{1,0:T(8,128)S(1)}, u32[]{:S(2)}, u32[]{:S(2)}) collective-permute-start(f32[128,128]{1,0:T(8,128)S(1)} %sum_shards.1.refs_8_.refs_0_), channel_id=1, source_target_pairs={{0,12},{4,16},{8,20},{12,24},{16,28},{20,0},{24,4},{28,8},{1,13},{... | collective-permute-start | bytes 196616 | tf_op jit(solution)/shard_map/ppermute | solution.py:350
  196.2 2.3 %collective-permute-done.3.refs_1_ = bf16[96,128]{1,0:T(8,128)(2,1)S(1)} collective-permute-done((bf16[96,128]{1,0:T(8,128)(2,1)S(1)}, bf16[96,128]{1,0:T(8,128)(2,1)S(1)}, u32[]{:S(2)}, u32[]{:S(2)}) %collective-permute-start.3) | collective-permute-done | bytes 24608 | tf_op jit(solution)/shard_map/ppermute | solution.py:350
  198.5 0.0 collective-permute-start.19
  198.5 0.0 collective-permute-done.4.refs_2_
  198.5 0.2 collective-permute-start.20
  198.8 0.0 collective-permute-done.16.refs_9_.refs_1_
  198.8 0.8 collective-permute-start.21
  199.5 0.0 collective-permute-done.17.refs_10_.refs_2_
  199.5 2.3 %collective-permute-start.22 = (f32[128,128]{1,0:T(8,128)S(1)}, f32[128,128]{1,0:T(8,128)S(1)}, u32[]{:S(2)}, u32[]{:S(2)}) collective-permute-start(f32[128,128]{1,0:T(8,128)S(1)} %sum_shards.1.refs_8_.refs_0_), channel_id=1, source_target_pairs={{0,28},{4,0},{8,4},{12,8},{16,12},{20,16},{24,20},{28,24},{1,29},{... | collective-permute-start | bytes 196616 | tf_op jit(solution)/shard_map/ppermute | solution.py:350
  201.8 0.0 collective-permute-done.18.refs_11_.refs_3_
  201.8 0.0 collective-permute-start.5
  201.8 1.0 collective-permute-done.19.refs_12_.refs_4_
  202.8 0.0 collective-permute-start.6
  202.8 0.0 collective-permute-done.20.refs_13_.refs_5_
  202.8 0.8 collective-permute-start.7
  203.6 0.0 collective-permute-done.21.refs_14_.refs_6_
  203.6 2.8 %collective-permute-start.8 = (bf16[96,128]{1,0:T(8,128)(2,1)S(1)}, bf16[96,128]{1,0:T(8,128)(2,1)S(1)}, u32[]{:S(2)}, u32[]{:S(2)}) collective-permute-start(bf16[96,128]{1,0:T(8,128)(2,1)S(1)} %get-tuple-element.16.refs_0_), channel_id=1, source_target_pairs={{0,24},{4,28},{8,0},{12,4},{16,8},{20,12},{24,16},{28,20},{1,25},{... | collective-permute-start | bytes 73736 | tf_op jit(solution)/shard_map/ppermute | solution.py:350
  206.4 0.0 collective-permute-done.22.refs_15_.refs_7_
  206.4 1.0 collective-permute-start.9
  207.4 1.4 collective-permute-start.23
  208.9 2.0 collective-permute-start.24
  210.9 0.0 collective-permute-done.7.refs_5_
  210.9 0.5 collective-permute-start.25
  211.4 0.0 collective-permute-done.8.refs_6_
  211.4 0.0 collective-permute-done.9.refs_7_
  211.4 1.5 weight_grad.1
  212.9 0.3 collective-permute-done.23.refs_1_
  213.2 0.4 collective-permute-done.24.refs_2_
  213.6 1.0 collective-permute-done.25.refs_3_
  214.6 0.6 place_local.1
  (20 shorter events, 0.1 us)
Async XLA Ops:
  0.6 46.5 %copy-start.4 = (f32[384]{0:T(512)S(1)}, f32[384]{0:T(512)}, u32[]{:S(2)}) copy-start(f32[384]{0:T(512)} %constant.25.clone.xtab_ref) | copy-start | bytes 4612
  0.6 38.6 %copy-start = (bf16[8,2,128,128]{3,2,1,0:T(8,128)(2,1)S(1)}, bf16[8,2,128,128]{3,2,1,0:T(8,128)(2,1)}, u32[]{:S(2)}) copy-start(bf16[8,2,128,128]{3,2,1,0:T(8,128)(2,1)} %refs_4_.1) | copy-start | bytes 1572868
  5.3 0.9 copy-start.1
  6.2 0.7 copy-start.3
  6.9 40.3 %copy-start.2 = (bf16[32,2304]{1,0:T(8,128)(2,1)S(1)}, bf16[32,2304]{1,0:T(8,128)(2,1)}, u32[]{:S(2)}) copy-start(bf16[32,2304]{1,0:T(8,128)(2,1)} %constant.26.clone.basis_ref.rest_7_) | copy-start | bytes 442372
  6.9 40.3 %copy-start.5 = (bf16[1,6,12,2304]{3,2,1,0:T(8,128)(2,1)S(1)}, bf16[1,6,12,2304]{3,2,1,0:T(8,128)(2,1)}, u32[]{:S(2)}) copy-start(bf16[1,6,12,2304]{3,2,1,0:T(8,128)(2,1)} %t_ref.1) | copy-start | bytes 995332
  6.9 40.3 %copy-start.6 = (bf16[128,128]{1,0:T(8,128)(2,1)S(1)}, bf16[128,128]{1,0:T(8,128)(2,1)}, u32[]{:S(2)}) copy-start(bf16[128,128]{1,0:T(8,128)(2,1)} %rest_4_.1) | copy-start | bytes 98308
  6.9 40.3 %copy-start.7 = (f32[128]{0:T(128)S(1)}, f32[128]{0:T(128)}, u32[]{:S(2)}) copy-start(f32[128]{0:T(128)} %param.18) | copy-start | bytes 1540
  6.9 40.3 %copy-start.8 = (bf16[2304,128]{1,0:T(8,128)(2,1)S(1)}, bf16[2304,128]{1,0:T(8,128)(2,1)}, u32[]{:S(2)}) copy-start(bf16[2304,128]{1,0:T(8,128)(2,1)} %constant.27.clone.rest_6_) | copy-start | bytes 1769476
  6.9 40.3 %copy-start.9 = (bf16[256,128]{1,0:T(8,128)(2,1)S(1)}, bf16[256,128]{1,0:T(8,128)(2,1)}, u32[]{:S(2)}) copy-start(bf16[256,128]{1,0:T(8,128)(2,1)} %constant.29.clone.rest_9_) | copy-start | bytes 196612
  6.9 40.3 %copy-start.10 = (bf16[128,128]{1,0:T(8,128)(2,1)S(1)}, bf16[128,128]{1,0:T(8,128)(2,1)}, u32[]{:S(2)}) copy-start(bf16[128,128]{1,0:T(8,128)(2,1)} %constant.28.clone.rest_8_) | copy-start | bytes 98308
  29.5 7.2 %collective-permute-start = (f32[96,128]{1,0:T(8,128)S(1)}, f32[96,128]{1,0:T(8,128)S(1)}, u32[]{:S(2)}, u32[]{:S(2)}) collective-permute-start(f32[96,128]{1,0:T(8,128)S(1)} %get-tuple-element.13), channel_id=1, source_target_pairs={{0,1},{1,2},{2,3},{3,0},{4,5},{5,6},{6,7},{7,4},{8,9},{9,10},{10,1... | collective-permute-start | bytes 147464 | tf_op jit(solution)/shard_map/ppermute | solution.py:350
  32.6 5.0 %collective-permute-start.1 = (f32[96,128]{1,0:T(8,128)S(1)}, f32[96,128]{1,0:T(8,128)S(1)}, u32[]{:S(2)}, u32[]{:S(2)}) collective-permute-start(f32[96,128]{1,0:T(8,128)S(1)} %get-tuple-element.14), channel_id=1, source_target_pairs={{0,2},{1,3},{2,0},{3,1},{4,6},{5,7},{6,4},{7,5},{8,10},{9,11},{10,... | collective-permute-start | bytes 147464 | tf_op jit(solution)/shard_map/ppermute | solution.py:350
  35.2 4.1 %collective-permute-start.2 = (f32[96,128]{1,0:T(8,128)S(1)}, f32[96,128]{1,0:T(8,128)S(1)}, u32[]{:S(2)}, u32[]{:S(2)}) collective-permute-start(f32[96,128]{1,0:T(8,128)S(1)} %get-tuple-element.15), channel_id=1, source_target_pairs={{0,3},{1,0},{2,1},{3,2},{4,7},{5,4},{6,5},{7,6},{8,11},{9,8},{10,9... | collective-permute-start | bytes 147464 | tf_op jit(solution)/shard_map/ppermute | solution.py:350
  39.5 5.8 %collective-permute-start.10 = (bf16[96,128]{1,0:T(8,128)(2,1)S(1)}, bf16[96,128]{1,0:T(8,128)(2,1)S(1)}, u32[]{:S(2)}, u32[]{:S(2)}) collective-permute-start(bf16[96,128]{1,0:T(8,128)(2,1)S(1)} %get-tuple-element.17.rest_0_), channel_id=1, source_target_pairs={{0,1},{1,2},{2,3},{3,0},{4,5},{5,6},{6,7},{7,4},{8,9},{9,10},{10,1... | collective-permute-start | bytes 73736 | tf_op jit(solution)/shard_map/ppermute | solution.py:350
  40.0 5.6 %collective-permute-start.11 = (bf16[96,128]{1,0:T(8,128)(2,1)S(1)}, bf16[96,128]{1,0:T(8,128)(2,1)S(1)}, u32[]{:S(2)}, u32[]{:S(2)}) collective-permute-start(bf16[96,128]{1,0:T(8,128)(2,1)S(1)} %get-tuple-element.17.rest_0_), channel_id=1, source_target_pairs={{0,2},{1,3},{2,0},{3,1},{4,6},{5,7},{6,4},{7,5},{8,10},{9,11},{10,... | collective-permute-start | bytes 73736 | tf_op jit(solution)/shard_map/ppermute | solution.py:350
  43.3 3.8 %collective-permute-start.12 = (bf16[96,128]{1,0:T(8,128)(2,1)S(1)}, bf16[96,128]{1,0:T(8,128)(2,1)S(1)}, u32[]{:S(2)}, u32[]{:S(2)}) collective-permute-start(bf16[96,128]{1,0:T(8,128)(2,1)S(1)} %get-tuple-element.17.rest_0_), channel_id=1, source_target_pairs={{0,3},{1,0},{2,1},{3,2},{4,7},{5,4},{6,5},{7,6},{8,11},{9,8},{10,9... | collective-permute-start | bytes 73736 | tf_op jit(solution)/shard_map/ppermute | solution.py:350
  184.4 6.2 %collective-permute-start.13 = (f32[128,128]{1,0:T(8,128)S(1)}, f32[128,128]{1,0:T(8,128)S(1)}, u32[]{:S(2)}, u32[]{:S(2)}) collective-permute-start(f32[128,128]{1,0:T(8,128)S(1)} %get-tuple-element.19), channel_id=1, source_target_pairs={{0,1},{1,2},{2,3},{3,0},{4,5},{5,6},{6,7},{7,4},{8,9},{9,10},{10,1... | collective-permute-start | bytes 196616 | tf_op jit(solution)/shard_map/ppermute | solution.py:350
  185.1 6.6 %collective-permute-start.14 = (f32[128,128]{1,0:T(8,128)S(1)}, f32[128,128]{1,0:T(8,128)S(1)}, u32[]{:S(2)}, u32[]{:S(2)}) collective-permute-start(f32[128,128]{1,0:T(8,128)S(1)} %get-tuple-element.20), channel_id=1, source_target_pairs={{0,2},{1,3},{2,0},{3,1},{4,6},{5,7},{6,4},{7,5},{8,10},{9,11},{10,... | collective-permute-start | bytes 196616 | tf_op jit(solution)/shard_map/ppermute | solution.py:350
  187.1 4.6 %collective-permute-start.15 = (f32[128,128]{1,0:T(8,128)S(1)}, f32[128,128]{1,0:T(8,128)S(1)}, u32[]{:S(2)}, u32[]{:S(2)}) collective-permute-start(f32[128,128]{1,0:T(8,128)S(1)} %get-tuple-element.21), channel_id=1, source_target_pairs={{0,3},{1,0},{2,1},{3,2},{4,7},{5,4},{6,5},{7,6},{8,11},{9,8},{10,9... | collective-permute-start | bytes 196616 | tf_op jit(solution)/shard_map/ppermute | solution.py:350
  191.7 7.0 %collective-permute-start.16 = (f32[128,128]{1,0:T(8,128)S(1)}, f32[128,128]{1,0:T(8,128)S(1)}, u32[]{:S(2)}, u32[]{:S(2)}) collective-permute-start(f32[128,128]{1,0:T(8,128)S(1)} %sum_shards.1.refs_8_.refs_0_), channel_id=1, source_target_pairs={{0,4},{4,8},{8,12},{12,16},{16,20},{20,24},{24,28},{28,0},{1,5},{5... | collective-permute-start | bytes 196616 | tf_op jit(solution)/shard_map/ppermute | solution.py:350
  191.8 7.7 %collective-permute-start.17 = (f32[128,128]{1,0:T(8,128)S(1)}, f32[128,128]{1,0:T(8,128)S(1)}, u32[]{:S(2)}, u32[]{:S(2)}) collective-permute-start(f32[128,128]{1,0:T(8,128)S(1)} %sum_shards.1.refs_8_.refs_0_), channel_id=1, source_target_pairs={{0,8},{4,12},{8,16},{12,20},{16,24},{20,28},{24,0},{28,4},{1,9},{5... | collective-permute-start | bytes 196616 | tf_op jit(solution)/shard_map/ppermute | solution.py:350
  191.9 6.7 %collective-permute-start.3 = (bf16[96,128]{1,0:T(8,128)(2,1)S(1)}, bf16[96,128]{1,0:T(8,128)(2,1)S(1)}, u32[]{:S(2)}, u32[]{:S(2)}) collective-permute-start(bf16[96,128]{1,0:T(8,128)(2,1)S(1)} %get-tuple-element.16.refs_0_), channel_id=1, source_target_pairs={{0,4},{4,8},{8,12},{12,16},{16,20},{20,24},{24,28},{28,0},{1,5},{5... | collective-permute-start | bytes 73736 | tf_op jit(solution)/shard_map/ppermute | solution.py:350
  191.9 6.6 %collective-permute-start.4 = (bf16[96,128]{1,0:T(8,128)(2,1)S(1)}, bf16[96,128]{1,0:T(8,128)(2,1)S(1)}, u32[]{:S(2)}, u32[]{:S(2)}) collective-permute-start(bf16[96,128]{1,0:T(8,128)(2,1)S(1)} %get-tuple-element.16.refs_0_), channel_id=1, source_target_pairs={{0,8},{4,12},{8,16},{12,20},{16,24},{20,28},{24,0},{28,4},{1,9},{5... | collective-permute-start | bytes 73736 | tf_op jit(solution)/shard_map/ppermute | solution.py:350
  192.0 9.8 %collective-permute-start.18 = (f32[128,128]{1,0:T(8,128)S(1)}, f32[128,128]{1,0:T(8,128)S(1)}, u32[]{:S(2)}, u32[]{:S(2)}) collective-permute-start(f32[128,128]{1,0:T(8,128)S(1)} %sum_shards.1.refs_8_.refs_0_), channel_id=1, source_target_pairs={{0,12},{4,16},{8,20},{12,24},{16,28},{20,0},{24,4},{28,8},{1,13},{... | collective-permute-start | bytes 196616 | tf_op jit(solution)/shard_map/ppermute | solution.py:350
  198.5 4.3 %collective-permute-start.19 = (f32[128,128]{1,0:T(8,128)S(1)}, f32[128,128]{1,0:T(8,128)S(1)}, u32[]{:S(2)}, u32[]{:S(2)}) collective-permute-start(f32[128,128]{1,0:T(8,128)S(1)} %sum_shards.1.refs_8_.refs_0_), channel_id=1, source_target_pairs={{0,16},{4,20},{8,24},{12,28},{16,0},{20,4},{24,8},{28,12},{1,17},{... | collective-permute-start | bytes 196616 | tf_op jit(solution)/shard_map/ppermute | solution.py:350
  198.5 4.3 %collective-permute-start.20 = (f32[128,128]{1,0:T(8,128)S(1)}, f32[128,128]{1,0:T(8,128)S(1)}, u32[]{:S(2)}, u32[]{:S(2)}) collective-permute-start(f32[128,128]{1,0:T(8,128)S(1)} %sum_shards.1.refs_8_.refs_0_), channel_id=1, source_target_pairs={{0,20},{4,24},{8,28},{12,0},{16,4},{20,8},{24,12},{28,16},{1,21},{... | collective-permute-start | bytes 196616 | tf_op jit(solution)/shard_map/ppermute | solution.py:350
  198.8 4.9 %collective-permute-start.21 = (f32[128,128]{1,0:T(8,128)S(1)}, f32[128,128]{1,0:T(8,128)S(1)}, u32[]{:S(2)}, u32[]{:S(2)}) collective-permute-start(f32[128,128]{1,0:T(8,128)S(1)} %sum_shards.1.refs_8_.refs_0_), channel_id=1, source_target_pairs={{0,24},{4,28},{8,0},{12,4},{16,8},{20,12},{24,16},{28,20},{1,25},{... | collective-permute-start | bytes 196616 | tf_op jit(solution)/shard_map/ppermute | solution.py:350
  199.5 6.9 %collective-permute-start.22 = (f32[128,128]{1,0:T(8,128)S(1)}, f32[128,128]{1,0:T(8,128)S(1)}, u32[]{:S(2)}, u32[]{:S(2)}) collective-permute-start(f32[128,128]{1,0:T(8,128)S(1)} %sum_shards.1.refs_8_.refs_0_), channel_id=1, source_target_pairs={{0,28},{4,0},{8,4},{12,8},{16,12},{20,16},{24,20},{28,24},{1,29},{... | collective-permute-start | bytes 196616 | tf_op jit(solution)/shard_map/ppermute | solution.py:350
  201.8 5.6 %collective-permute-start.5 = (bf16[96,128]{1,0:T(8,128)(2,1)S(1)}, bf16[96,128]{1,0:T(8,128)(2,1)S(1)}, u32[]{:S(2)}, u32[]{:S(2)}) collective-permute-start(bf16[96,128]{1,0:T(8,128)(2,1)S(1)} %get-tuple-element.16.refs_0_), channel_id=1, source_target_pairs={{0,12},{4,16},{8,20},{12,24},{16,28},{20,0},{24,4},{28,8},{1,13},{... | collective-permute-start | bytes 73736 | tf_op jit(solution)/shard_map/ppermute | solution.py:350
  202.8 6.1 %collective-permute-start.6 = (bf16[96,128]{1,0:T(8,128)(2,1)S(1)}, bf16[96,128]{1,0:T(8,128)(2,1)S(1)}, u32[]{:S(2)}, u32[]{:S(2)}) collective-permute-start(bf16[96,128]{1,0:T(8,128)(2,1)S(1)} %get-tuple-element.16.refs_0_), channel_id=1, source_target_pairs={{0,16},{4,20},{8,24},{12,28},{16,0},{20,4},{24,8},{28,12},{1,17},{... | collective-permute-start | bytes 73736 | tf_op jit(solution)/shard_map/ppermute | solution.py:350
  202.8 8.1 %collective-permute-start.7 = (bf16[96,128]{1,0:T(8,128)(2,1)S(1)}, bf16[96,128]{1,0:T(8,128)(2,1)S(1)}, u32[]{:S(2)}, u32[]{:S(2)}) collective-permute-start(bf16[96,128]{1,0:T(8,128)(2,1)S(1)} %get-tuple-element.16.refs_0_), channel_id=1, source_target_pairs={{0,20},{4,24},{8,28},{12,0},{16,4},{20,8},{24,12},{28,16},{1,21},{... | collective-permute-start | bytes 73736 | tf_op jit(solution)/shard_map/ppermute | solution.py:350
  203.6 7.7 %collective-permute-start.8 = (bf16[96,128]{1,0:T(8,128)(2,1)S(1)}, bf16[96,128]{1,0:T(8,128)(2,1)S(1)}, u32[]{:S(2)}, u32[]{:S(2)}) collective-permute-start(bf16[96,128]{1,0:T(8,128)(2,1)S(1)} %get-tuple-element.16.refs_0_), channel_id=1, source_target_pairs={{0,24},{4,28},{8,0},{12,4},{16,8},{20,12},{24,16},{28,20},{1,25},{... | collective-permute-start | bytes 73736 | tf_op jit(solution)/shard_map/ppermute | solution.py:350
  206.4 4.9 %collective-permute-start.9 = (bf16[96,128]{1,0:T(8,128)(2,1)S(1)}, bf16[96,128]{1,0:T(8,128)(2,1)S(1)}, u32[]{:S(2)}, u32[]{:S(2)}) collective-permute-start(bf16[96,128]{1,0:T(8,128)(2,1)S(1)} %get-tuple-element.16.refs_0_), channel_id=1, source_target_pairs={{0,28},{4,0},{8,4},{12,8},{16,12},{20,16},{24,20},{28,24},{1,29},{... | collective-permute-start | bytes 73736 | tf_op jit(solution)/shard_map/ppermute | solution.py:350
  207.4 5.8 %collective-permute-start.23 = (f32[32,128]{1,0:T(8,128)S(1)}, f32[32,128]{1,0:T(8,128)S(1)}, u32[]{:S(2)}, u32[]{:S(2)}) collective-permute-start(f32[32,128]{1,0:T(8,128)S(1)} %sum_local.1.refs_0_), channel_id=1, source_target_pairs={{0,1},{1,2},{2,3},{3,0},{4,5},{5,6},{6,7},{7,4},{8,9},{9,10},{10,1... | collective-permute-start | bytes 49160 | tf_op jit(solution)/shard_map/ppermute | solution.py:350
  208.9 4.7 %collective-permute-start.24 = (f32[32,128]{1,0:T(8,128)S(1)}, f32[32,128]{1,0:T(8,128)S(1)}, u32[]{:S(2)}, u32[]{:S(2)}) collective-permute-start(f32[32,128]{1,0:T(8,128)S(1)} %sum_local.1.refs_0_), channel_id=1, source_target_pairs={{0,2},{1,3},{2,0},{3,1},{4,6},{5,7},{6,4},{7,5},{8,10},{9,11},{10,... | collective-permute-start | bytes 49160 | tf_op jit(solution)/shard_map/ppermute | solution.py:350
  210.9 3.7 %collective-permute-start.25 = (f32[32,128]{1,0:T(8,128)S(1)}, f32[32,128]{1,0:T(8,128)S(1)}, u32[]{:S(2)}, u32[]{:S(2)}) collective-permute-start(f32[32,128]{1,0:T(8,128)S(1)} %sum_local.1.refs_0_), channel_id=1, source_target_pairs={{0,3},{1,0},{2,1},{3,2},{4,7},{5,4},{6,5},{7,6},{8,11},{9,8},{10,9... | collective-permute-start | bytes 49160 | tf_op jit(solution)/shard_map/ppermute | solution.py:350

commit v3 on v2

--- a/solution.py
+++ b/solution.py
@@ -19,8 +19,7 @@
 bf16 = jnp.bfloat16
 inv_root_two_pi = 0.3989422804014327
 half_log2e = 0.7213475204444817
-erf_p = 0.3275911 * 0.7071067811865476
-erf_a = tuple(0.5 * a for a in (0.254829592, -0.284496736, 1.421413741, -1.453152027, 1.061405429))
+root_half = 0.7071067811865476
 
 
 def split_bf16(values):
@@ -109,12 +108,7 @@
 
 def gelu_parts(pre):
     bell = jnp.exp2(pre * pre * (-half_log2e))
-    t = pl.reciprocal(1.0 + erf_p * jnp.abs(pre), approx=True)
-    poly = erf_a[4]
-    for a in (erf_a[3], erf_a[2], erf_a[1], erf_a[0]):
-        poly = poly * t + a
-    tail = poly * t * bell
-    cdf = jnp.where(pre >= 0.0, 1.0 - tail, tail)
+    cdf = 0.5 + 0.5 * lax.erf(pre * root_half)
     return cdf, bell
 
 

time: 213 us -> 181 us (0.85)
  Pallas kernels: 162 us -> 130 us
    pallas_call x1, Pallas kernels: 137 us -> 105 us  [body(): pl.pallas_call(functools.partial(backward_kernel, slots, planes, step_pla...]
where the time goes in v3:
time: 181 us; the launch traced here: 183 us
  Pallas kernels  130 us (72%)
  starting transfers between devices  31 us (17%)
  waiting for transfers between devices  14.9 us (8%)
  local copies, waits for them, and re-layouts  4.9 us (3%)
    pallas_call x1, Pallas kernels, body(): pl.pallas_call(functools.partial(backward_kernel, slots, planes, step_pla...  105 us
    ppermute x26, starting transfers between devices, rotations(): got.append(lax.ppermute(value_of(d), axis, perm))  31 us
    pallas_call x1, Pallas kernels, body(): pl.pallas_call(functools.partial(forward_kernel, slots, planes, step_plan...  22.6 us
    ppermute x26, waiting for transfers between devices, rotations(): got.append(lax.ppermute(value_of(d), axis, perm))  14.9 us
  transfers between devices with their start and end apart: 26, of which 13 were waited for; matrix products, arithmetic and copies ran while one was open for 0% of the time, Pallas kernels for 1%

profile of v3, /device:TPU:0, one launch (start us, length us, event | category | flops | bytes accessed | tf_op | source)
XLA Modules:
  0.0 183.2 jit_solution(12550640863734566662)
XLA Ops:
  0.6 0.0 copy-start.4
  0.7 1.4 reduce_sum.9
  2.0 1.2 dynamic_slice.3
  3.2 2.0 %concatenate.3.meta_ref = s32[10]{0:T(128)S(1)} concatenate(s32[6]{0:T(128)} %bitcast.6, s32[1]{0:T(128)} %dynamic_slice.3, s32[1]{0:T(128)} %bitcast.1, s32[1]{0:T(128)} %bitcast.2.meta_ref, s32[1]{0:T(128)} %bitcast.3), dimensions={0} | concatenate | bytes 80 | tf_op jit(solution)/shard_map/concatenate | solution.py:359
  5.3 0.9 copy-done.1
  6.2 0.7 copy-done.3
  6.9 0.0 copy-start.8
  6.9 0.0 copy-start.9
  6.9 0.0 copy-start.10
  6.9 22.6 %forward_modes.1 = (f32[96,128]{1,0:T(8,128)S(1)}, f32[96,128]{1,0:T(8,128)S(1)}, f32[96,128]{1,0:T(8,128)S(1)}, f32[96,128]{1,0:T(8,128)S(1)}) custom-call(s32[10]{0:T(128)S(1)} %concatenate.3.meta_ref, f32[384]{0:T(512)S(1)} %copy-done.3, bf16[1,6,12,48,48,128]{5,4,3,2,1,0:T(8,128)(2,1)} %f_ref.3, bf16[32,2304]{1,0:T(8,128)(2,1)S(1)} %copy-done.1), custom_call_target="tpu_custom_call" | custom-call | tf_op jit(solution)/shard_map/forward_modes/pallas_call | solution.py:384
  29.5 3.1 %collective-permute-start = (f32[96,128]{1,0:T(8,128)S(1)}, f32[96,128]{1,0:T(8,128)S(1)}, u32[]{:S(2)}, u32[]{:S(2)}) collective-permute-start(f32[96,128]{1,0:T(8,128)S(1)} %get-tuple-element.13), channel_id=1, source_target_pairs={{0,1},{1,2},{2,3},{3,0},{4,5},{5,6},{6,7},{7,4},{8,9},{9,10},{10,1... | collective-permute-start | bytes 147464 | tf_op jit(solution)/shard_map/ppermute | solution.py:344
  32.6 2.6 %collective-permute-start.1 = (f32[96,128]{1,0:T(8,128)S(1)}, f32[96,128]{1,0:T(8,128)S(1)}, u32[]{:S(2)}, u32[]{:S(2)}) collective-permute-start(f32[96,128]{1,0:T(8,128)S(1)} %get-tuple-element.14), channel_id=1, source_target_pairs={{0,2},{1,3},{2,0},{3,1},{4,6},{5,7},{6,4},{7,5},{8,10},{9,11},{10,... | collective-permute-start | bytes 147464 | tf_op jit(solution)/shard_map/ppermute | solution.py:344
  35.2 1.3 collective-permute-start.2
  36.5 0.2 collective-permute-done.refs_1_
  36.7 0.9 collective-permute-done.1.refs_2_
  37.6 1.7 collective-permute-done.2.refs_3_
  39.3 0.3 mix_modes.1
  39.5 0.5 collective-permute-start.10
  40.0 3.3 %collective-permute-start.11 = (bf16[96,128]{1,0:T(8,128)(2,1)S(1)}, bf16[96,128]{1,0:T(8,128)(2,1)S(1)}, u32[]{:S(2)}, u32[]{:S(2)}) collective-permute-start(bf16[96,128]{1,0:T(8,128)(2,1)S(1)} %get-tuple-element.17.rest_0_), channel_id=1, source_target_pairs={{0,2},{1,3},{2,0},{3,1},{4,6},{5,7},{6,4},{7,5},{8,10},{9,11},{10,... | collective-permute-start | bytes 73736 | tf_op jit(solution)/shard_map/ppermute | solution.py:344
  43.3 0.1 collective-permute-start.12
  43.4 1.9 %collective-permute-done.10.rest_1_ = bf16[96,128]{1,0:T(8,128)(2,1)S(1)} collective-permute-done((bf16[96,128]{1,0:T(8,128)(2,1)S(1)}, bf16[96,128]{1,0:T(8,128)(2,1)S(1)}, u32[]{:S(2)}, u32[]{:S(2)}) %collective-permute-start.10) | collective-permute-done | bytes 24608 | tf_op jit(solution)/shard_map/ppermute | solution.py:344
  45.3 0.3 collective-permute-done.11.rest_2_
  45.6 1.5 collective-permute-done.12.rest_3_
  47.2 105.1 %backward_modes.1 = (f32[128,128]{1,0:T(8,128)S(1)}, f32[128,128]{1,0:T(8,128)S(1)}, f32[128,128]{1,0:T(8,128)S(1)}, f32[128,128]{1,0:T(8,128)S(1)}) custom-call(s32[10]{0:T(128)S(1)} %concatenate.3.meta_ref, f32[384]{0:T(512)S(1)} %copy-done.4, bf16[1,6,12,48,48,128]{5,4,3,2,1,0:T(8,128)(2,1)} %f_ref.3, bf16[1,6,12,2304]{3,2,1,0:T(8,128)(2,1)S(1)} %copy-done.5, ...), custom_call_target="tpu_custom_call" | custom-call | flops 43486543872 | bytes 42467328 | tf_op jit(solution)/shard_map/backward_modes/pallas_call | solution.py:431
  152.3 0.7 collective-permute-start.13
  153.1 1.9 %collective-permute-start.14 = (f32[128,128]{1,0:T(8,128)S(1)}, f32[128,128]{1,0:T(8,128)S(1)}, u32[]{:S(2)}, u32[]{:S(2)}) collective-permute-start(f32[128,128]{1,0:T(8,128)S(1)} %get-tuple-element.20), channel_id=1, source_target_pairs={{0,2},{1,3},{2,0},{3,1},{4,6},{5,7},{6,4},{7,5},{8,10},{9,11},{10,... | collective-permute-start | bytes 196616 | tf_op jit(solution)/shard_map/ppermute | solution.py:344
  155.0 1.2 collective-permute-start.15
  156.2 2.3 %collective-permute-done.13.refs_1_ = f32[128,128]{1,0:T(8,128)S(1)} collective-permute-done((f32[128,128]{1,0:T(8,128)S(1)}, f32[128,128]{1,0:T(8,128)S(1)}, u32[]{:S(2)}, u32[]{:S(2)}) %collective-permute-start.13) | collective-permute-done | bytes 65568 | tf_op jit(solution)/shard_map/ppermute | solution.py:344
  158.5 1.1 collective-permute-done.14.refs_2_
  159.6 0.0 collective-permute-done.15.refs_3_
  159.7 0.1 collective-permute-start.16
  159.7 0.1 collective-permute-start.17
  159.8 0.1 collective-permute-start.3
  159.9 0.1 collective-permute-start.4
  159.9 4.2 %collective-permute-start.18 = (f32[128,128]{1,0:T(8,128)S(1)}, f32[128,128]{1,0:T(8,128)S(1)}, u32[]{:S(2)}, u32[]{:S(2)}) collective-permute-start(f32[128,128]{1,0:T(8,128)S(1)} %sum_shards.1.refs_8_.refs_0_), channel_id=1, source_target_pairs={{0,12},{4,16},{8,20},{12,24},{16,28},{20,0},{24,4},{28,8},{1,13},{... | collective-permute-start | bytes 196616 | tf_op jit(solution)/shard_map/ppermute | solution.py:344
  164.2 2.3 %collective-permute-done.3.refs_1_ = bf16[96,128]{1,0:T(8,128)(2,1)S(1)} collective-permute-done((bf16[96,128]{1,0:T(8,128)(2,1)S(1)}, bf16[96,128]{1,0:T(8,128)(2,1)S(1)}, u32[]{:S(2)}, u32[]{:S(2)}) %collective-permute-start.3) | collective-permute-done | bytes 24608 | tf_op jit(solution)/shard_map/ppermute | solution.py:344
  166.4 0.0 collective-permute-start.19
  166.4 0.0 collective-permute-done.4.refs_2_
  166.4 0.2 collective-permute-start.20
  166.7 0.0 collective-permute-done.16.refs_9_.refs_1_
  166.7 0.8 collective-permute-start.21
  167.5 0.0 collective-permute-done.17.refs_10_.refs_2_
  167.5 2.3 %collective-permute-start.22 = (f32[128,128]{1,0:T(8,128)S(1)}, f32[128,128]{1,0:T(8,128)S(1)}, u32[]{:S(2)}, u32[]{:S(2)}) collective-permute-start(f32[128,128]{1,0:T(8,128)S(1)} %sum_shards.1.refs_8_.refs_0_), channel_id=1, source_target_pairs={{0,28},{4,0},{8,4},{12,8},{16,12},{20,16},{24,20},{28,24},{1,29},{... | collective-permute-start | bytes 196616 | tf_op jit(solution)/shard_map/ppermute | solution.py:344
  169.7 0.0 collective-permute-done.18.refs_11_.refs_3_
  169.7 0.0 collective-permute-start.5
  169.7 1.0 collective-permute-done.19.refs_12_.refs_4_
  170.7 0.0 collective-permute-start.6
  170.7 0.0 collective-permute-done.20.refs_13_.refs_5_
  170.7 0.8 collective-permute-start.7
  171.5 0.0 collective-permute-done.21.refs_14_.refs_6_
  171.5 2.8 %collective-permute-start.8 = (bf16[96,128]{1,0:T(8,128)(2,1)S(1)}, bf16[96,128]{1,0:T(8,128)(2,1)S(1)}, u32[]{:S(2)}, u32[]{:S(2)}) collective-permute-start(bf16[96,128]{1,0:T(8,128)(2,1)S(1)} %get-tuple-element.16.refs_0_), channel_id=1, source_target_pairs={{0,24},{4,28},{8,0},{12,4},{16,8},{20,12},{24,16},{28,20},{1,25},{... | collective-permute-start | bytes 73736 | tf_op jit(solution)/shard_map/ppermute | solution.py:344
  174.4 0.0 collective-permute-done.22.refs_15_.refs_7_
  174.4 1.0 collective-permute-start.9
  175.3 1.4 collective-permute-start.23
  176.8 2.0 %collective-permute-start.24 = (f32[32,128]{1,0:T(8,128)S(1)}, f32[32,128]{1,0:T(8,128)S(1)}, u32[]{:S(2)}, u32[]{:S(2)}) collective-permute-start(f32[32,128]{1,0:T(8,128)S(1)} %sum_local.1.refs_0_), channel_id=1, source_target_pairs={{0,2},{1,3},{2,0},{3,1},{4,6},{5,7},{6,4},{7,5},{8,10},{9,11},{10,... | collective-permute-start | bytes 49160 | tf_op jit(solution)/shard_map/ppermute | solution.py:344
  178.8 0.0 collective-permute-done.7.refs_5_
  178.8 0.5 collective-permute-start.25
  179.3 0.0 collective-permute-done.8.refs_6_
  179.3 0.0 collective-permute-done.9.refs_7_
  179.3 1.5 weight_grad.1
  180.8 0.3 collective-permute-done.23.refs_1_
  181.1 0.4 collective-permute-done.24.refs_2_
  181.5 1.0 collective-permute-done.25.refs_3_
  182.5 0.6 place_local.1
  (20 shorter events, 0.1 us)
Async XLA Ops:
  0.6 46.5 %copy-start.4 = (f32[384]{0:T(512)S(1)}, f32[384]{0:T(512)}, u32[]{:S(2)}) copy-start(f32[384]{0:T(512)} %constant.25.clone.xtab_ref) | copy-start | bytes 4612
  0.6 38.6 %copy-start = (bf16[8,2,128,128]{3,2,1,0:T(8,128)(2,1)S(1)}, bf16[8,2,128,128]{3,2,1,0:T(8,128)(2,1)}, u32[]{:S(2)}) copy-start(bf16[8,2,128,128]{3,2,1,0:T(8,128)(2,1)} %refs_4_.1) | copy-start | bytes 1572868
  5.3 0.9 copy-start.1
  6.2 0.7 copy-start.3
  6.9 40.3 %copy-start.2 = (bf16[32,2304]{1,0:T(8,128)(2,1)S(1)}, bf16[32,2304]{1,0:T(8,128)(2,1)}, u32[]{:S(2)}) copy-start(bf16[32,2304]{1,0:T(8,128)(2,1)} %constant.26.clone.basis_ref.rest_7_) | copy-start | bytes 442372
  6.9 40.3 %copy-start.5 = (bf16[1,6,12,2304]{3,2,1,0:T(8,128)(2,1)S(1)}, bf16[1,6,12,2304]{3,2,1,0:T(8,128)(2,1)}, u32[]{:S(2)}) copy-start(bf16[1,6,12,2304]{3,2,1,0:T(8,128)(2,1)} %t_ref.1) | copy-start | bytes 995332
  6.9 40.3 %copy-start.6 = (bf16[128,128]{1,0:T(8,128)(2,1)S(1)}, bf16[128,128]{1,0:T(8,128)(2,1)}, u32[]{:S(2)}) copy-start(bf16[128,128]{1,0:T(8,128)(2,1)} %rest_4_.1) | copy-start | bytes 98308
  6.9 40.3 %copy-start.7 = (f32[128]{0:T(128)S(1)}, f32[128]{0:T(128)}, u32[]{:S(2)}) copy-start(f32[128]{0:T(128)} %param.18) | copy-start | bytes 1540
  6.9 40.3 %copy-start.8 = (bf16[2304,128]{1,0:T(8,128)(2,1)S(1)}, bf16[2304,128]{1,0:T(8,128)(2,1)}, u32[]{:S(2)}) copy-start(bf16[2304,128]{1,0:T(8,128)(2,1)} %constant.27.clone.rest_6_) | copy-start | bytes 1769476
  6.9 40.3 %copy-start.9 = (bf16[256,128]{1,0:T(8,128)(2,1)S(1)}, bf16[256,128]{1,0:T(8,128)(2,1)}, u32[]{:S(2)}) copy-start(bf16[256,128]{1,0:T(8,128)(2,1)} %constant.29.clone.rest_9_) | copy-start | bytes 196612
  6.9 40.3 %copy-start.10 = (bf16[128,128]{1,0:T(8,128)(2,1)S(1)}, bf16[128,128]{1,0:T(8,128)(2,1)}, u32[]{:S(2)}) copy-start(bf16[128,128]{1,0:T(8,128)(2,1)} %constant.28.clone.rest_8_) | copy-start | bytes 98308
  29.5 7.2 %collective-permute-start = (f32[96,128]{1,0:T(8,128)S(1)}, f32[96,128]{1,0:T(8,128)S(1)}, u32[]{:S(2)}, u32[]{:S(2)}) collective-permute-start(f32[96,128]{1,0:T(8,128)S(1)} %get-tuple-element.13), channel_id=1, source_target_pairs={{0,1},{1,2},{2,3},{3,0},{4,5},{5,6},{6,7},{7,4},{8,9},{9,10},{10,1... | collective-permute-start | bytes 147464 | tf_op jit(solution)/shard_map/ppermute | solution.py:344
  32.6 5.0 %collective-permute-start.1 = (f32[96,128]{1,0:T(8,128)S(1)}, f32[96,128]{1,0:T(8,128)S(1)}, u32[]{:S(2)}, u32[]{:S(2)}) collective-permute-start(f32[96,128]{1,0:T(8,128)S(1)} %get-tuple-element.14), channel_id=1, source_target_pairs={{0,2},{1,3},{2,0},{3,1},{4,6},{5,7},{6,4},{7,5},{8,10},{9,11},{10,... | collective-permute-start | bytes 147464 | tf_op jit(solution)/shard_map/ppermute | solution.py:344
  35.2 4.1 %collective-permute-start.2 = (f32[96,128]{1,0:T(8,128)S(1)}, f32[96,128]{1,0:T(8,128)S(1)}, u32[]{:S(2)}, u32[]{:S(2)}) collective-permute-start(f32[96,128]{1,0:T(8,128)S(1)} %get-tuple-element.15), channel_id=1, source_target_pairs={{0,3},{1,0},{2,1},{3,2},{4,7},{5,4},{6,5},{7,6},{8,11},{9,8},{10,9... | collective-permute-start | bytes 147464 | tf_op jit(solution)/shard_map/ppermute | solution.py:344
  39.5 5.8 %collective-permute-start.10 = (bf16[96,128]{1,0:T(8,128)(2,1)S(1)}, bf16[96,128]{1,0:T(8,128)(2,1)S(1)}, u32[]{:S(2)}, u32[]{:S(2)}) collective-permute-start(bf16[96,128]{1,0:T(8,128)(2,1)S(1)} %get-tuple-element.17.rest_0_), channel_id=1, source_target_pairs={{0,1},{1,2},{2,3},{3,0},{4,5},{5,6},{6,7},{7,4},{8,9},{9,10},{10,1... | collective-permute-start | bytes 73736 | tf_op jit(solution)/shard_map/ppermute | solution.py:344
  40.0 5.6 %collective-permute-start.11 = (bf16[96,128]{1,0:T(8,128)(2,1)S(1)}, bf16[96,128]{1,0:T(8,128)(2,1)S(1)}, u32[]{:S(2)}, u32[]{:S(2)}) collective-permute-start(bf16[96,128]{1,0:T(8,128)(2,1)S(1)} %get-tuple-element.17.rest_0_), channel_id=1, source_target_pairs={{0,2},{1,3},{2,0},{3,1},{4,6},{5,7},{6,4},{7,5},{8,10},{9,11},{10,... | collective-permute-start | bytes 73736 | tf_op jit(solution)/shard_map/ppermute | solution.py:344
  43.3 3.8 %collective-permute-start.12 = (bf16[96,128]{1,0:T(8,128)(2,1)S(1)}, bf16[96,128]{1,0:T(8,128)(2,1)S(1)}, u32[]{:S(2)}, u32[]{:S(2)}) collective-permute-start(bf16[96,128]{1,0:T(8,128)(2,1)S(1)} %get-tuple-element.17.rest_0_), channel_id=1, source_target_pairs={{0,3},{1,0},{2,1},{3,2},{4,7},{5,4},{6,5},{7,6},{8,11},{9,8},{10,9... | collective-permute-start | bytes 73736 | tf_op jit(solution)/shard_map/ppermute | solution.py:344
  152.3 6.2 %collective-permute-start.13 = (f32[128,128]{1,0:T(8,128)S(1)}, f32[128,128]{1,0:T(8,128)S(1)}, u32[]{:S(2)}, u32[]{:S(2)}) collective-permute-start(f32[128,128]{1,0:T(8,128)S(1)} %get-tuple-element.19), channel_id=1, source_target_pairs={{0,1},{1,2},{2,3},{3,0},{4,5},{5,6},{6,7},{7,4},{8,9},{9,10},{10,1... | collective-permute-start | bytes 196616 | tf_op jit(solution)/shard_map/ppermute | solution.py:344
  153.1 6.6 %collective-permute-start.14 = (f32[128,128]{1,0:T(8,128)S(1)}, f32[128,128]{1,0:T(8,128)S(1)}, u32[]{:S(2)}, u32[]{:S(2)}) collective-permute-start(f32[128,128]{1,0:T(8,128)S(1)} %get-tuple-element.20), channel_id=1, source_target_pairs={{0,2},{1,3},{2,0},{3,1},{4,6},{5,7},{6,4},{7,5},{8,10},{9,11},{10,... | collective-permute-start | bytes 196616 | tf_op jit(solution)/shard_map/ppermute | solution.py:344
  155.0 4.6 %collective-permute-start.15 = (f32[128,128]{1,0:T(8,128)S(1)}, f32[128,128]{1,0:T(8,128)S(1)}, u32[]{:S(2)}, u32[]{:S(2)}) collective-permute-start(f32[128,128]{1,0:T(8,128)S(1)} %get-tuple-element.21), channel_id=1, source_target_pairs={{0,3},{1,0},{2,1},{3,2},{4,7},{5,4},{6,5},{7,6},{8,11},{9,8},{10,9... | collective-permute-start | bytes 196616 | tf_op jit(solution)/shard_map/ppermute | solution.py:344
  159.7 7.0 %collective-permute-start.16 = (f32[128,128]{1,0:T(8,128)S(1)}, f32[128,128]{1,0:T(8,128)S(1)}, u32[]{:S(2)}, u32[]{:S(2)}) collective-permute-start(f32[128,128]{1,0:T(8,128)S(1)} %sum_shards.1.refs_8_.refs_0_), channel_id=1, source_target_pairs={{0,4},{4,8},{8,12},{12,16},{16,20},{20,24},{24,28},{28,0},{1,5},{5... | collective-permute-start | bytes 196616 | tf_op jit(solution)/shard_map/ppermute | solution.py:344
  159.7 7.7 %collective-permute-start.17 = (f32[128,128]{1,0:T(8,128)S(1)}, f32[128,128]{1,0:T(8,128)S(1)}, u32[]{:S(2)}, u32[]{:S(2)}) collective-permute-start(f32[128,128]{1,0:T(8,128)S(1)} %sum_shards.1.refs_8_.refs_0_), channel_id=1, source_target_pairs={{0,8},{4,12},{8,16},{12,20},{16,24},{20,28},{24,0},{28,4},{1,9},{5... | collective-permute-start | bytes 196616 | tf_op jit(solution)/shard_map/ppermute | solution.py:344
  159.8 6.7 %collective-permute-start.3 = (bf16[96,128]{1,0:T(8,128)(2,1)S(1)}, bf16[96,128]{1,0:T(8,128)(2,1)S(1)}, u32[]{:S(2)}, u32[]{:S(2)}) collective-permute-start(bf16[96,128]{1,0:T(8,128)(2,1)S(1)} %get-tuple-element.16.refs_0_), channel_id=1, source_target_pairs={{0,4},{4,8},{8,12},{12,16},{16,20},{20,24},{24,28},{28,0},{1,5},{5... | collective-permute-start | bytes 73736 | tf_op jit(solution)/shard_map/ppermute | solution.py:344
  159.9 6.6 %collective-permute-start.4 = (bf16[96,128]{1,0:T(8,128)(2,1)S(1)}, bf16[96,128]{1,0:T(8,128)(2,1)S(1)}, u32[]{:S(2)}, u32[]{:S(2)}) collective-permute-start(bf16[96,128]{1,0:T(8,128)(2,1)S(1)} %get-tuple-element.16.refs_0_), channel_id=1, source_target_pairs={{0,8},{4,12},{8,16},{12,20},{16,24},{20,28},{24,0},{28,4},{1,9},{5... | collective-permute-start | bytes 73736 | tf_op jit(solution)/shard_map/ppermute | solution.py:344
  159.9 9.8 %collective-permute-start.18 = (f32[128,128]{1,0:T(8,128)S(1)}, f32[128,128]{1,0:T(8,128)S(1)}, u32[]{:S(2)}, u32[]{:S(2)}) collective-permute-start(f32[128,128]{1,0:T(8,128)S(1)} %sum_shards.1.refs_8_.refs_0_), channel_id=1, source_target_pairs={{0,12},{4,16},{8,20},{12,24},{16,28},{20,0},{24,4},{28,8},{1,13},{... | collective-permute-start | bytes 196616 | tf_op jit(solution)/shard_map/ppermute | solution.py:344
  166.4 4.3 %collective-permute-start.19 = (f32[128,128]{1,0:T(8,128)S(1)}, f32[128,128]{1,0:T(8,128)S(1)}, u32[]{:S(2)}, u32[]{:S(2)}) collective-permute-start(f32[128,128]{1,0:T(8,128)S(1)} %sum_shards.1.refs_8_.refs_0_), channel_id=1, source_target_pairs={{0,16},{4,20},{8,24},{12,28},{16,0},{20,4},{24,8},{28,12},{1,17},{... | collective-permute-start | bytes 196616 | tf_op jit(solution)/shard_map/ppermute | solution.py:344
  166.4 4.3 %collective-permute-start.20 = (f32[128,128]{1,0:T(8,128)S(1)}, f32[128,128]{1,0:T(8,128)S(1)}, u32[]{:S(2)}, u32[]{:S(2)}) collective-permute-start(f32[128,128]{1,0:T(8,128)S(1)} %sum_shards.1.refs_8_.refs_0_), channel_id=1, source_target_pairs={{0,20},{4,24},{8,28},{12,0},{16,4},{20,8},{24,12},{28,16},{1,21},{... | collective-permute-start | bytes 196616 | tf_op jit(solution)/shard_map/ppermute | solution.py:344
  166.7 4.9 %collective-permute-start.21 = (f32[128,128]{1,0:T(8,128)S(1)}, f32[128,128]{1,0:T(8,128)S(1)}, u32[]{:S(2)}, u32[]{:S(2)}) collective-permute-start(f32[128,128]{1,0:T(8,128)S(1)} %sum_shards.1.refs_8_.refs_0_), channel_id=1, source_target_pairs={{0,24},{4,28},{8,0},{12,4},{16,8},{20,12},{24,16},{28,20},{1,25},{... | collective-permute-start | bytes 196616 | tf_op jit(solution)/shard_map/ppermute | solution.py:344
  167.5 6.9 %collective-permute-start.22 = (f32[128,128]{1,0:T(8,128)S(1)}, f32[128,128]{1,0:T(8,128)S(1)}, u32[]{:S(2)}, u32[]{:S(2)}) collective-permute-start(f32[128,128]{1,0:T(8,128)S(1)} %sum_shards.1.refs_8_.refs_0_), channel_id=1, source_target_pairs={{0,28},{4,0},{8,4},{12,8},{16,12},{20,16},{24,20},{28,24},{1,29},{... | collective-permute-start | bytes 196616 | tf_op jit(solution)/shard_map/ppermute | solution.py:344
  169.7 5.6 %collective-permute-start.5 = (bf16[96,128]{1,0:T(8,128)(2,1)S(1)}, bf16[96,128]{1,0:T(8,128)(2,1)S(1)}, u32[]{:S(2)}, u32[]{:S(2)}) collective-permute-start(bf16[96,128]{1,0:T(8,128)(2,1)S(1)} %get-tuple-element.16.refs_0_), channel_id=1, source_target_pairs={{0,12},{4,16},{8,20},{12,24},{16,28},{20,0},{24,4},{28,8},{1,13},{... | collective-permute-start | bytes 73736 | tf_op jit(solution)/shard_map/ppermute | solution.py:344
  170.7 6.1 %collective-permute-start.6 = (bf16[96,128]{1,0:T(8,128)(2,1)S(1)}, bf16[96,128]{1,0:T(8,128)(2,1)S(1)}, u32[]{:S(2)}, u32[]{:S(2)}) collective-permute-start(bf16[96,128]{1,0:T(8,128)(2,1)S(1)} %get-tuple-element.16.refs_0_), channel_id=1, source_target_pairs={{0,16},{4,20},{8,24},{12,28},{16,0},{20,4},{24,8},{28,12},{1,17},{... | collective-permute-start | bytes 73736 | tf_op jit(solution)/shard_map/ppermute | solution.py:344
  170.7 8.1 %collective-permute-start.7 = (bf16[96,128]{1,0:T(8,128)(2,1)S(1)}, bf16[96,128]{1,0:T(8,128)(2,1)S(1)}, u32[]{:S(2)}, u32[]{:S(2)}) collective-permute-start(bf16[96,128]{1,0:T(8,128)(2,1)S(1)} %get-tuple-element.16.refs_0_), channel_id=1, source_target_pairs={{0,20},{4,24},{8,28},{12,0},{16,4},{20,8},{24,12},{28,16},{1,21},{... | collective-permute-start | bytes 73736 | tf_op jit(solution)/shard_map/ppermute | solution.py:344
  171.5 7.7 %collective-permute-start.8 = (bf16[96,128]{1,0:T(8,128)(2,1)S(1)}, bf16[96,128]{1,0:T(8,128)(2,1)S(1)}, u32[]{:S(2)}, u32[]{:S(2)}) collective-permute-start(bf16[96,128]{1,0:T(8,128)(2,1)S(1)} %get-tuple-element.16.refs_0_), channel_id=1, source_target_pairs={{0,24},{4,28},{8,0},{12,4},{16,8},{20,12},{24,16},{28,20},{1,25},{... | collective-permute-start | bytes 73736 | tf_op jit(solution)/shard_map/ppermute | solution.py:344
  174.4 4.9 %collective-permute-start.9 = (bf16[96,128]{1,0:T(8,128)(2,1)S(1)}, bf16[96,128]{1,0:T(8,128)(2,1)S(1)}, u32[]{:S(2)}, u32[]{:S(2)}) collective-permute-start(bf16[96,128]{1,0:T(8,128)(2,1)S(1)} %get-tuple-element.16.refs_0_), channel_id=1, source_target_pairs={{0,28},{4,0},{8,4},{12,8},{16,12},{20,16},{24,20},{28,24},{1,29},{... | collective-permute-start | bytes 73736 | tf_op jit(solution)/shard_map/ppermute | solution.py:344
  175.3 5.8 %collective-permute-start.23 = (f32[32,128]{1,0:T(8,128)S(1)}, f32[32,128]{1,0:T(8,128)S(1)}, u32[]{:S(2)}, u32[]{:S(2)}) collective-permute-start(f32[32,128]{1,0:T(8,128)S(1)} %sum_local.1.refs_0_), channel_id=1, source_target_pairs={{0,1},{1,2},{2,3},{3,0},{4,5},{5,6},{6,7},{7,4},{8,9},{9,10},{10,1... | collective-permute-start | bytes 49160 | tf_op jit(solution)/shard_map/ppermute | solution.py:344
  176.8 4.7 %collective-permute-start.24 = (f32[32,128]{1,0:T(8,128)S(1)}, f32[32,128]{1,0:T(8,128)S(1)}, u32[]{:S(2)}, u32[]{:S(2)}) collective-permute-start(f32[32,128]{1,0:T(8,128)S(1)} %sum_local.1.refs_0_), channel_id=1, source_target_pairs={{0,2},{1,3},{2,0},{3,1},{4,6},{5,7},{6,4},{7,5},{8,10},{9,11},{10,... | collective-permute-start | bytes 49160 | tf_op jit(solution)/shard_map/ppermute | solution.py:344
  178.8 3.7 %collective-permute-start.25 = (f32[32,128]{1,0:T(8,128)S(1)}, f32[32,128]{1,0:T(8,128)S(1)}, u32[]{:S(2)}, u32[]{:S(2)}) collective-permute-start(f32[32,128]{1,0:T(8,128)S(1)} %sum_local.1.refs_0_), channel_id=1, source_target_pairs={{0,3},{1,0},{2,1},{3,2},{4,7},{5,4},{6,5},{7,6},{8,11},{9,8},{10,9... | collective-permute-start | bytes 49160 | tf_op jit(solution)/shard_map/ppermute | solution.py:344

commit v4 on v3

--- a/solution.py
+++ b/solution.py
@@ -54,7 +54,7 @@
 
 
 def scalar_places(slots):
-    return dict(count=slots, total=slots + 1, shard=slots + 2, first=slots + 3)
+    return dict(count=slots, total=slots + 1, shard=slots + 2, first=slots + 3, partner=slots + 4)
 
 
 def combine_planes(q_ref, xtab_ref, cell0, shard, planes, scale, store):
@@ -74,13 +74,24 @@
 
 
 def forward_kernel(
-    slots, planes, step_planes, scale, meta_ref, xtab_ref, f_ref, basis_ref, *rest
+    slots, base, sends, planes, step_planes, scale, meta_ref, xtab_ref, f_ref, basis_ref, *rest
 ):
-    outs, q_ref = rest[:MX], rest[MX]
+    if sends:
+        t_ref, outs, send_ref, t_out_ref, q_ref = rest[0], rest[1 : MX + 1], *rest[MX + 1 :]
+    else:
+        given, outs, q_ref = rest[:MX], rest[MX : 2 * MX], rest[2 * MX]
     place = scalar_places(slots)
     g, blk = pl.program_id(0), pl.program_id(1)
-    live = g < meta_ref[place["count"]]
+    live = base + g < meta_ref[place["count"]]
     row = pl.multiple_of(g * 16, 16)
+
+    if not sends:
+
+        @pl.when((g == 0) & (blk == 0))
+        def _():
+            rows = given[0].shape[0]
+            for d in range(MX):
+                outs[d][rows : 2 * rows, :] = given[d][...]
 
     @pl.when(live)
     def _():
@@ -89,6 +100,13 @@
             field = f_ref[0, 0, p].reshape(cells, 128)
             part = jnp.dot(basis_ref[...], field, preferred_element_type=f32)
             q_ref[blk * step_planes + p] = part[0:16] + part[16:32]
+            if sends:
+                send_ref[0, p] = f_ref[0, 0, p]
+        if sends:
+
+            @pl.when(blk == 0)
+            def _():
+                t_out_ref[0] = t_ref[0, 0]
 
         @pl.when(blk == planes // step_planes - 1)
         def _():
@@ -112,22 +130,44 @@
     return cdf, bell
 
 
+def shared_live(slots, kept, blocks, count, partner, g, blk):
+    return (kept + g < count) & ((g > 0) | ((blk == blocks - 1) & (partner <= 1)))
+
+
 def backward_kernel(
-    slots, planes, step_planes, rows_step, scale, meta_ref, xtab_ref, f_ref, t_ref, *rest
+    slots, own, planes, step_planes, rows_step, scale, meta_ref, xtab_ref, f_ref, t_ref, *rest
 ):
     specs = rest[:MX]
     w_ref, proj_ref, inv_ref, basis_ref, eye_ref, ones_ref = rest[MX : MX + 6]
-    outs = rest[MX + 6 : 2 * MX + 6]
-    rhs_ref, pre_ref, slope_ref, both_ref, d_ref, total_ref, q_ref, t16_ref, spec_ref = rest[2 * MX + 6 :]
+    rest = rest[MX + 6 :]
+    if not own:
+        given, rest = rest[:MX], rest[MX:]
+    outs = rest[:MX]
+    rhs_ref, pre_ref, slope_ref, both_ref, d_ref, total_ref, q_ref, t16_ref, spec_ref = rest[MX:]
     place = scalar_places(slots)
+    kept = slots - 3
     g, blk = pl.program_id(0), pl.program_id(1)
     blocks = planes // step_planes
-    live = g < meta_ref[place["count"]]
-    row = pl.multiple_of(g * 16, 16)
+    count, partner = meta_ref[place["count"]], meta_ref[place["partner"]]
+    if own:
+        some = g < count
+        away = (g >= kept) & shared_live(slots, kept, blocks, count, partner, g - kept, blk)
+        live = some & jnp.logical_not(away)
+        positions, spec_row, out_row = kept + 1, g * 16, g * 16
+        field_at = lambda p: f_ref[0, 0, p].reshape(cells, 128)
+        lines_of = lambda: t_ref[0, 0].astype(f32)
+    else:
+        some = kept + g < partner
+        live = shared_live(slots, kept, blocks, partner, count, g, blk)
+        positions, spec_row, out_row = 3, (kept + g) * 16, (kept + 1 + g) * 16
+        field_at = lambda p: f_ref[0, p].reshape(cells, 128)
+        lines_of = lambda: t_ref[0].astype(f32)
+    row = pl.multiple_of(out_row, 16)
     shard = meta_ref[place["shard"]]
     cell0 = meta_ref[place["first"]]
-    cells = f_ref.shape[3] * f_ref.shape[4]
+    cells = inv_ref.shape[0]
     third = cells // 3
+    half = third // 2
     unroll = 2 if step_planes % 2 == 0 else 1
 
     @pl.when((g == 0) & (blk == 0))
@@ -136,21 +176,26 @@
         for n in range(2):
             rhs_ref[n, 0:128, :] = w_ref[...]
             rhs_ref[n, 128:256, :] = jnp.zeros((128, 128), bf16)
+        if not own:
+            rows = (kept + 1) * 16
+            for d in range(MX):
+                outs[d][0:rows, :] = given[d][0:rows, :]
+
+    @pl.when(some & (blk == 0))
+    def _():
+        q_ref[...] = jnp.zeros_like(q_ref)
+        lines = lines_of()
+        for a in range(planes):
+            line = jnp.broadcast_to(lines[a : a + 1, :], (16, cells))
+            t16_ref[a] = line.astype(bf16)
+        for d in range(MX):
+            spec_ref[d] = specs[d][pl.ds(pl.multiple_of(spec_row, 16), 16), :].astype(f32)
 
     @pl.when(live)
     def _():
-        @pl.when(blk == 0)
-        def _():
-            lines = t_ref[0, 0].astype(f32)
-            for a in range(planes):
-                line = jnp.broadcast_to(lines[a : a + 1, :], (16, cells))
-                t16_ref[a] = line.astype(bf16)
-            for d in range(MX):
-                spec_ref[d] = specs[d][pl.ds(row, 16), :].astype(f32)
-
-        count = meta_ref[place["total"]].astype(f32)
+        grids = meta_ref[place["total"]].astype(f32)
         proj = proj_ref[...]
-        proj_scaled = proj / jnp.full((1, 128), count, f32)
+        proj_scaled = proj / jnp.full((1, 128), grids, f32)
 
         def first_rows(a, rhs):
             re = jnp.zeros((8, 128), f32)
@@ -181,10 +226,13 @@
                 rhs = rhs_ref.at[u % 2]
                 if k == 0:
                     first_rows(blk * step_planes + n * unroll + u, rhs)
-                field = f_ref[0, 0, n * unroll + u].reshape(cells, 128)
-                part = slice(k * third, (k + 1) * third)
-                lhs = jnp.concatenate([field[part], inv_ref[part, :]], axis=1)
-                pre_ref[s % 2] = jnp.dot(lhs, rhs[...], preferred_element_type=f32)
+                field = field_at(n * unroll + u)
+                for r0 in (0, half):
+                    part = slice(k * third + r0, k * third + r0 + half)
+                    lhs = jnp.concatenate([field[part], inv_ref[part, :]], axis=1)
+                    pre_ref[s % 2, r0 : r0 + half, :] = jnp.dot(
+                        lhs, rhs[...], preferred_element_type=f32
+                    )
 
             def elementwise(s):
                 u, k = units[s]
@@ -202,14 +250,14 @@
                         both_ref[s % 2, r1 : r1 + 16, 128:256] = line * eye_ref[n1 : n1 + 16, :]
 
             def after(s):
-                resid = jnp.dot(both_ref[s % 2], ones_ref[...], preferred_element_type=f32)
-                for r0 in range(0, third, rows_step):
-                    rows = slice(r0, r0 + rows_step)
-                    d_ref[s % 2, rows, :] = (resid[rows] * slope_ref[s % 2, rows, :]).astype(bf16)
+                for r0 in (0, half):
+                    rows = slice(r0, r0 + half)
+                    resid = jnp.dot(both_ref[s % 2, rows, :], ones_ref[...], preferred_element_type=f32)
+                    d_ref[s % 2, rows, :] = (resid * slope_ref[s % 2, rows, :]).astype(bf16)
 
             def last(s):
                 u, k = units[s]
-                field = f_ref[0, 0, n * unroll + u].reshape(cells, 128)
+                field = field_at(n * unroll + u)
                 part = slice(k * third, (k + 1) * third)
                 lhs = jnp.concatenate([field[part].T, basis_ref[:, part]], axis=0)
                 sums = jnp.dot(lhs, d_ref[s % 2], preferred_element_type=f32)
@@ -231,26 +279,30 @@
 
         lax.fori_loop(0, step_planes // unroll, planes_together, 0)
 
-        @pl.when(blk == blocks - 1)
-        def _():
-            def store(d, re, im):
-                outs[d][pl.ds(row, 8), :] = re
-                outs[d][pl.ds(row + 8, 8), :] = im
-
-            combine_planes(q_ref, xtab_ref, cell0, shard, planes, scale, store)
-
-    @pl.when(jnp.logical_not(live) & (blk == 0))
+    @pl.when(some & (blk == blocks - 1))
+    def _():
+        def store(d, re, im):
+            outs[d][pl.ds(row, 8), :] = re
+            outs[d][pl.ds(row + 8, 8), :] = im
+
+        combine_planes(q_ref, xtab_ref, cell0, shard, planes, scale, store)
+
+    @pl.when(jnp.logical_not(some) & (blk == 0))
     def _():
         for out in outs:
             out[pl.ds(row, 16), :] = jnp.zeros((16, 128), f32)
 
-    @pl.when((g == slots - 1) & (blk == blocks - 1))
-    def _():
-        part = 128 // MX
+    @pl.when((g == positions - 1) & (blk == blocks - 1))
+    def _():
+        size = 128 // MX
         for d in range(MX):
             i = lax.rem(shard + d, MX)
-            at = pl.multiple_of(i * part, part)
-            outs[d][slots * 16 : slots * 16 + part, :] = total_ref[pl.ds(at, part), :]
+            at = pl.multiple_of(i * size, size)
+            part = total_ref[pl.ds(at, size), :]
+            if not own:
+                part = part + given[d][(kept + 1) * 16 : (kept + 1) * 16 + size, :]
+            rows = outs[d].shape[0]
+            outs[d][rows - size : rows, :] = part
 
 
 def mix_kernel(slots, per, shards, *refs):
@@ -292,13 +344,22 @@
     refs[count][...] = total
 
 
-def weight_kernel(lanes, slots, per, *refs):
+def weight_kernel(lanes, slots, per, lane_ref, *refs):
     coeffs, backs = refs[:lanes], refs[lanes : 2 * lanes]
-    out_ref, c_ref, b_ref = refs[2 * lanes :]
-    rows = slots * 2 * per
+    out_ref, all_ref, c_ref, b_ref = refs[2 * lanes :]
+    each = 2 * per
+    kept = slots - 3
+    rows = (slots + 1) * each
     for n in range(lanes):
-        c_ref[n * rows : (n + 1) * rows, :] = coeffs[n][...].astype(f32)
+        coeff = coeffs[n][...].astype(f32)
+        c_ref[n * rows : n * rows + (kept + 1) * each, :] = coeff[0 : (kept + 1) * each]
+        all_ref[n] = coeff[kept * each :]
         b_ref[n * rows : (n + 1) * rows, :] = backs[n][0:rows, :]
+    for n in range(lanes):
+        source = lax.rem(lane_ref[0] - n + lanes, lanes)
+        other = lax.rem(n - 1 + 2 * lax.rem(source, 2) + lanes, lanes)
+        c_ref[n * rows + (kept + 1) * each : (n + 1) * rows, :] = all_ref[other]
+    slots = slots + 1
     for m in range(per):
         re_rows = pl.ds(m, lanes * slots, stride=2 * per)
         im_rows = pl.ds(per + m, lanes * slots, stride=2 * per)
@@ -353,7 +414,7 @@
     step_planes = max(n for n in (1, 2, 3, 4) if planes % n == 0)
     blocks = planes // step_planes
     basis, inverse, xtab = phase_constants(grid_len)
-    lane = lax.axis_index("dp")
+    lane = lax.axis_index("dp").astype(jnp.int32)
     shard = lax.axis_index("fsdp").astype(jnp.int32)
     turn = shard if split == 1 else jnp.int32(0)
     meta = jnp.concatenate(
@@ -363,37 +424,80 @@
             jnp.sum(counts)[None],
             turn[None],
             (shard * planes)[None],
+            counts[lane ^ 1][None],
         ]
     ).astype(jnp.int32)
     place = scalar_places(slots)
 
-    def field_block(g, blk, meta_ref, xtab_ref):
-        count = meta_ref[place["count"]]
-        slot = meta_ref[jnp.minimum(g, count - 1)]
-        return (0, slot, jnp.where(g < count, blk, blocks - 1), 0, 0, 0)
-
-    def target_block(g, blk, meta_ref, xtab_ref):
-        count = meta_ref[place["count"]]
-        return (0, meta_ref[jnp.minimum(g, count - 1)], 0, 0)
+    kept = slots - 3
+
+    def field_block(base):
+        def block(g, blk, meta_ref, xtab_ref):
+            count = meta_ref[place["count"]]
+            slot = meta_ref[jnp.minimum(base + g, count - 1)]
+            return (0, slot, jnp.where(base + g < count, blk, blocks - 1), 0, 0, 0)
+
+        return pl.BlockSpec((1, 1, step_planes, grid_len, grid_len, width), block)
+
+    def target_block(base):
+        def block(g, blk, meta_ref, xtab_ref):
+            count = meta_ref[place["count"]]
+            return (0, meta_ref[jnp.minimum(base + g, count - 1)], 0, 0)
+
+        return pl.BlockSpec((1, 1, planes, cells), block)
+
+    def shared_item(g, blk):
+        return jnp.maximum(g * blocks + blk - (blocks - 1), 0)
 
     def fixed(*shape):
         return pl.BlockSpec(shape, lambda g, blk, meta_ref, xtab_ref: (0,) * len(shape))
 
-    field_spec = pl.BlockSpec((1, 1, step_planes, grid_len, grid_len, width), field_block)
+    items = 2 * blocks + 1
+    shared_fields = pl.BlockSpec(
+        (1, step_planes, grid_len, grid_len, width),
+        lambda g, blk, meta_ref, xtab_ref: (shared_item(g, blk), 0, 0, 0, 0),
+    )
+    shared_targets = pl.BlockSpec((1, planes, cells), lambda g, blk, meta_ref, xtab_ref: (g, 0, 0))
     part_rows = slots * 16
-    parts = pl.pallas_call(
-        functools.partial(forward_kernel, slots, planes, step_planes, float(grid_len) ** (-1.5)),
+    forward_scale = float(grid_len) ** (-1.5)
+    *late_parts, sent_fields, sent_targets = pl.pallas_call(
+        functools.partial(forward_kernel, slots, kept, True, planes, step_planes, forward_scale),
         grid_spec=pltpu.PrefetchScalarGridSpec(
             num_scalar_prefetch=2,
-            grid=(slots, blocks),
-            in_specs=[field_spec, fixed(*basis.shape)],
+            grid=(3, blocks),
+            in_specs=[field_block(kept), fixed(*basis.shape), target_block(kept)],
+            out_specs=[fixed(3 * 16, width)] * MX + [shared_fields, shared_targets],
+            scratch_shapes=[pltpu.VMEM((planes, 16, width), f32)],
+        ),
+        out_shape=[jax.ShapeDtypeStruct((3 * 16, width), f32)] * MX
+        + [
+            jax.ShapeDtypeStruct((items, step_planes, grid_len, grid_len, width), bf16),
+            jax.ShapeDtypeStruct((3, planes, cells), bf16),
+        ],
+        compiler_params=params(),
+        name="forward_shared",
+    )(meta, xtab, fields, basis, targets)
+    swap = lambda x: lax.ppermute(x, "dp", [(s, s ^ 1) for s in range(lanes)])
+    came_fields = swap(sent_fields)
+    came_targets = swap(sent_targets)
+    parts = pl.pallas_call(
+        functools.partial(forward_kernel, slots, 0, False, planes, step_planes, forward_scale),
+        grid_spec=pltpu.PrefetchScalarGridSpec(
+            num_scalar_prefetch=2,
+            grid=(3, blocks),
+            in_specs=[field_block(0), fixed(*basis.shape)] + [fixed(3 * 16, width)] * MX,
             out_specs=[fixed(part_rows, width)] * MX,
             scratch_shapes=[pltpu.VMEM((planes, 16, width), f32)],
         ),
         out_shape=[jax.ShapeDtypeStruct((part_rows, width), f32)] * MX,
         compiler_params=params(),
+        cost_estimate=pl.CostEstimate(
+            flops=3 * planes * cells * 256 * 256,
+            bytes_accessed=3 * planes * cells * width * 2,
+            transcendentals=0,
+        ),
         name="forward_modes",
-    )(meta, xtab, fields, basis)
+    )(meta, xtab, fields, basis, *late_parts)
 
     def shard_parts(pieces, count):
         if split == 1:
@@ -428,50 +532,73 @@
     eye = np.eye(128, dtype=ml_dtypes.bfloat16)
     ones = np.ones((128, 128), ml_dtypes.bfloat16)
     ones = np.concatenate([ones, -ones], axis=0)
-    results = pl.pallas_call(
-        functools.partial(backward_kernel, slots, planes, step_planes, 64, float(MODES) ** (-0.5)),
-        grid_spec=pltpu.PrefetchScalarGridSpec(
-            num_scalar_prefetch=2,
-            grid=(slots, blocks),
-            in_specs=[field_spec, pl.BlockSpec((1, 1, planes, cells), target_block)]
-            + [fixed(part_rows, width)] * MX
-            + [
-                fixed(width, width),
-                fixed(1, width),
-                fixed(*inverse.shape),
-                fixed(*basis.shape),
-                fixed(*eye.shape),
-                fixed(*ones.shape),
-            ],
-            out_specs=[fixed(part_rows + local_rows, width)] * MX,
-            scratch_shapes=[
-                pltpu.VMEM((2, 256, width), bf16),
-                pltpu.VMEM((2, cells // 3, width), f32),
-                pltpu.VMEM((2, cells // 3, width), f32),
-                pltpu.VMEM((2, cells // 3, 2 * width), bf16),
-                pltpu.VMEM((2, cells // 3, width), bf16),
-                pltpu.VMEM((width, width), f32),
-                pltpu.VMEM((planes, 16, width), f32),
-                pltpu.VMEM((planes, 16, cells), bf16),
-                pltpu.VMEM((MX, 16, width), f32),
-            ],
-        ),
-        out_shape=[jax.ShapeDtypeStruct((part_rows + local_rows, width), f32)] * MX,
-        compiler_params=params(),
-        cost_estimate=pl.CostEstimate(
-            flops=4 * slots * planes * cells * 256 * 256,
-            bytes_accessed=slots * planes * cells * width * 2,
-            transcendentals=0,
-        ),
-        name="backward_modes",
-    )(
-        meta, xtab, fields, targets, *spectrum, local_w, proj.reshape(1, width), inverse, basis, eye, ones
-    )
+
+    def own_block(g, blk, meta_ref, xtab_ref):
+        count, partner = meta_ref[place["count"]], meta_ref[place["partner"]]
+        slot = meta_ref[jnp.minimum(g, count - 1)]
+        away = (g >= kept) & shared_live(slots, kept, blocks, count, partner, g - kept, blk)
+        blk = jnp.where(away, max(blocks - 2, 0), blk)
+        return (0, slot, jnp.where(g < count, blk, blocks - 1), 0, 0, 0)
+
+    def backward(own, fields_, targets_, spectrum_, given):
+        positions = kept + 1 if own else 3
+        rows = (kept + 1 if own else slots + 1) * 16 + local_rows
+        own_fields = pl.BlockSpec((1, 1, step_planes, grid_len, grid_len, width), own_block)
+        return pl.pallas_call(
+            functools.partial(
+                backward_kernel, slots, own, planes, step_planes, 64, float(MODES) ** (-0.5)
+            ),
+            grid_spec=pltpu.PrefetchScalarGridSpec(
+                num_scalar_prefetch=2,
+                grid=(positions, blocks),
+                in_specs=([own_fields, target_block(0)] if own else [shared_fields, shared_targets])
+                + [fixed(part_rows, width)] * MX
+                + [
+                    fixed(width, width),
+                    fixed(1, width),
+                    fixed(*inverse.shape),
+                    fixed(*basis.shape),
+                    fixed(*eye.shape),
+                    fixed(*ones.shape),
+                ]
+                + [fixed(*g.shape) for g in given],
+                out_specs=[fixed(rows, width)] * MX,
+                scratch_shapes=[
+                    pltpu.VMEM((2, 256, width), bf16),
+                    pltpu.VMEM((2, cells // 3, width), f32),
+                    pltpu.VMEM((2, cells // 3, width), f32),
+                    pltpu.VMEM((2, cells // 3, 2 * width), bf16),
+                    pltpu.VMEM((2, cells // 3, width), bf16),
+                    pltpu.VMEM((width, width), f32),
+                    pltpu.VMEM((planes, 16, width), f32),
+                    pltpu.VMEM((planes, 16, cells), bf16),
+                    pltpu.VMEM((MX, 16, width), f32),
+                ],
+            ),
+            out_shape=[jax.ShapeDtypeStruct((rows, width), f32)] * MX,
+            compiler_params=params(),
+            cost_estimate=pl.CostEstimate(
+                flops=4 * positions * planes * cells * 256 * 256,
+                bytes_accessed=positions * planes * cells * width * 2,
+                transcendentals=0,
+            ),
+            name="backward_own" if own else "backward_shared",
+        )(
+            meta, xtab, fields_, targets_, *spectrum_, local_w, proj.reshape(1, width),
+            inverse, basis, eye, ones, *given,
+        )
+
+    came_spectrum = [swap(piece) for piece in spectrum]
+    own_results = backward(True, fields, targets, spectrum, [])
+    results = backward(False, came_fields, came_targets, came_spectrum, own_results)
+    places = slots + 1
+    part_rows = places * 16
+    place_rows = places * 2 * per
 
     if split == 1:
         chunk = lambda d: results[d]
     else:
-        backs = shard_parts([r[:part_rows] for r in results], slots)
+        backs = shard_parts([r[:part_rows] for r in results], places)
         local = jnp.concatenate([r[part_rows:] for r in results], axis=0)
         rows = width // shards
         chunk = lambda d: jnp.concatenate(
@@ -488,7 +615,7 @@
     )(*came)
     sums = rotations(lambda d: own_sum, "dp", lanes)
     own_local = pl.pallas_call(
-        functools.partial(local_sum_kernel, lanes, own_rows),
+        functools.partial(local_sum_kernel, lanes, place_rows),
         in_specs=whole_vmem(lanes),
         out_specs=pl.BlockSpec(memory_space=pltpu.VMEM),
         out_shape=jax.ShapeDtypeStruct((width // shards, width), f32),
@@ -498,16 +625,17 @@
     locals_ = rotations(lambda d: own_local, "fsdp", shards)
     grad_spectral = pl.pallas_call(
         functools.partial(weight_kernel, lanes, slots, per),
-        in_specs=whole_vmem(2 * lanes),
+        in_specs=[pl.BlockSpec(memory_space=pltpu.SMEM)] + whole_vmem(2 * lanes),
         out_specs=pl.BlockSpec(memory_space=pltpu.VMEM),
         out_shape=jax.ShapeDtypeStruct((per, 2, width, width), f32),
-        scratch_shapes=[pltpu.VMEM((lanes * own_rows, width), f32)] * 2,
+        scratch_shapes=[pltpu.VMEM((lanes, 3 * 2 * per, width), f32)]
+        + [pltpu.VMEM((lanes * place_rows, width), f32)] * 2,
         compiler_params=params(),
         cost_estimate=pl.CostEstimate(
-            flops=2 * per * 192 * 128 * 256, bytes_accessed=2 * per * 2 * width * width * 4, transcendentals=0
+            flops=2 * per * 256 * 128 * 256, bytes_accessed=2 * per * 2 * width * width * 4, transcendentals=0
         ),
         name="weight_grad",
-    )(*coeffs, *sums)
+    )(lane[None], *coeffs, *sums)
     grad_local = pl.pallas_call(
         functools.partial(place_kernel, shards),
         in_specs=[pl.BlockSpec(memory_space=pltpu.SMEM)] + whole_vmem(shards),

time: 181 us -> 168 us (0.928)
  Pallas kernels: 130 us -> 108 us
  local copies, waits for them, and re-layouts: 4.9 us -> 12.2 us
    pallas_call x3 -> x5, Pallas kernels: 128 us -> 105 us  [the longest x2 75 us: backward(): pl.pallas_call(functools.partial(backward_kernel, slots, own, planes, ste...]
    unnamed x22 -> x26, local copies, waits for them, and re-layouts: 1.64 us -> 8.31 us
  transfers between devices with their start and end apart: 26 -> 32, of which waited for: 13 -> 14; matrix products, arithmetic and copies ran while one was open for 0% -> 0% of each run, Pallas kernels for 1% -> 48%
where the time goes in v4:
time: 168 us; the launch traced here: 169 us
  Pallas kernels  108 us (64%)
  starting transfers between devices  31.4 us (19%)
  waiting for transfers between devices  15.2 us (9%)
  local copies, waits for them, and re-layouts  12.2 us (7%)
    pallas_call x2, Pallas kernels, backward(): pl.pallas_call(functools.partial(backward_kernel, slots, own, planes, ste...  75 us
    ppermute x26, starting transfers between devices, rotations(): got.append(lax.ppermute(value_of(d), axis, perm))  31.4 us
    pallas_call x1, Pallas kernels, body(): pl.pallas_call(functools.partial(forward_kernel, slots, kept, True, plane...  18.5 us
    ppermute x26, waiting for transfers between devices, rotations(): got.append(lax.ppermute(value_of(d), axis, perm))  15.2 us
    pallas_call x1, Pallas kernels, body(): pl.pallas_call(functools.partial(forward_kernel, slots, 0, False, planes,...  11.9 us
    unnamed x26, local copies, waits for them, and re-layouts  8.31 us
  transfers between devices with their start and end apart: 32, of which 14 were waited for; matrix products, arithmetic and copies ran while one was open for 0% of the time, Pallas kernels for 48%

profile of v4, /device:TPU:0, one launch (start us, length us, event | category | flops | bytes accessed | tf_op | source)
XLA Modules:
  0.0 169.0 jit_solution(6637380221840977905)
XLA Ops:
  0.6 1.3 reduce_sum.9
  1.9 1.3 fusion
  3.2 2.6 %concatenate.3.meta_ref = s32[11]{0:T(128)S(1)} concatenate(s32[6]{0:T(128)} %bitcast.8, s32[1]{0:T(128)} %get-tuple-element.43, s32[1]{0:T(128)} %bitcast.2, s32[1]{0:T(128)} %bitcast.3.meta_ref, s32[1]{0:T(128)} %bitcast.4, s32[1]{0:T(128)} %get-tuple-element.42), dimensions={0} | concatenate | bytes 88 | tf_op jit(solution)/shard_map/concatenate | solution.py:420
  5.8 0.9 copy-done
  6.7 1.0 copy-done.3
  7.7 0.7 copy-done.5
  8.4 18.5 %forward_shared.1 = (f32[48,128]{1,0:T(8,128)S(1)}, f32[48,128]{1,0:T(8,128)S(1)}, f32[48,128]{1,0:T(8,128)S(1)}, f32[48,128]{1,0:T(8,128)S(1)}, bf16[7,4,48,48,...) custom-call(s32[11]{0:T(128)S(1)} %concatenate.3.meta_ref, f32[384]{0:T(512)S(1)} %copy-done.5, ...), custom_call_target="tpu_custom_call" | custom-call | tf_op jit(solution)/shard_map/forward_shared/pallas_call | solution.py:463
  26.9 0.0 collective-permute-start.10
  27.0 0.0 copy-start.4
  27.0 0.0 copy-start.6
  27.0 0.0 copy-start.7
  27.0 0.0 copy-start.8
  27.0 0.0 copy-start.9
  27.0 0.0 copy-start.10
  27.0 0.0 copy-start.11
  27.0 11.9 %forward_modes.1 = (f32[96,128]{1,0:T(8,128)S(1)}, f32[96,128]{1,0:T(8,128)S(1)}, f32[96,128]{1,0:T(8,128)S(1)}, f32[96,128]{1,0:T(8,128)S(1)}) custom-call(s32[11]{0:T(128)S(1)} %concatenate.3.meta_ref, f32[384]{0:T(512)S(1)} %copy-done.5, bf16[1,6,12,48,48,128]{5,4,3,2,1,0:T(8,128)(2,1)} %f_ref.5, bf16[32,2304]{1,0:T(8,128)(2,1)S(1)} %copy-done, ...), custom_call_target="tpu_custom_call" | custom-call | flops 5435817984 | bytes 21233664 | tf_op jit(solution)/shard_map/forward_modes/pallas_call | solution.py:483
  39.0 3.1 %collective-permute-start = (f32[96,128]{1,0:T(8,128)S(1)}, f32[96,128]{1,0:T(8,128)S(1)}, u32[]{:S(2)}, u32[]{:S(2)}) collective-permute-start(f32[96,128]{1,0:T(8,128)S(1)} %get-tuple-element.27), channel_id=1, source_target_pairs={{0,1},{1,2},{2,3},{3,0},{4,5},{5,6},{6,7},{7,4},{8,9},{9,10},{10,1... | collective-permute-start | bytes 147464 | tf_op jit(solution)/shard_map/ppermute | solution.py:405
  42.0 2.6 %collective-permute-start.1 = (f32[96,128]{1,0:T(8,128)S(1)}, f32[96,128]{1,0:T(8,128)S(1)}, u32[]{:S(2)}, u32[]{:S(2)}) collective-permute-start(f32[96,128]{1,0:T(8,128)S(1)} %get-tuple-element.28), channel_id=1, source_target_pairs={{0,2},{1,3},{2,0},{3,1},{4,6},{5,7},{6,4},{7,5},{8,10},{9,11},{10,... | collective-permute-start | bytes 147464 | tf_op jit(solution)/shard_map/ppermute | solution.py:405
  44.6 1.3 collective-permute-start.2
  46.0 0.2 collective-permute-done.refs_1_
  46.1 0.9 collective-permute-done.1.refs_2_
  47.0 1.7 %collective-permute-done.2.refs_3_ = f32[96,128]{1,0:T(8,128)S(1)} collective-permute-done((f32[96,128]{1,0:T(8,128)S(1)}, f32[96,128]{1,0:T(8,128)S(1)}, u32[]{:S(2)}, u32[]{:S(2)}) %collective-permute-start.2) | collective-permute-done | bytes 49184 | tf_op jit(solution)/shard_map/ppermute | solution.py:405
  48.7 0.3 mix_modes.1
  49.0 0.1 collective-permute-start.12
  49.1 0.5 collective-permute-start.13
  49.5 3.3 %collective-permute-start.15 = (bf16[96,128]{1,0:T(8,128)(2,1)S(1)}, bf16[96,128]{1,0:T(8,128)(2,1)S(1)}, u32[]{:S(2)}, u32[]{:S(2)}) collective-permute-start(bf16[96,128]{1,0:T(8,128)(2,1)S(1)} %get-tuple-element.33.rest_0_), channel_id=1, source_target_pairs={{0,2},{1,3},{2,0},{3,1},{4,6},{5,7},{6,4},{7,5},{8,10},{9,11},{10,... | collective-permute-start | bytes 73736 | tf_op jit(solution)/shard_map/ppermute | solution.py:405
  52.8 0.1 collective-permute-start.17
  52.9 0.0 collective-permute-done.12.rest_0_
  52.9 0.0 collective-permute-start.11
  53.0 1.9 %collective-permute-done.13.rest_1_ = bf16[96,128]{1,0:T(8,128)(2,1)S(1)} collective-permute-done((bf16[96,128]{1,0:T(8,128)(2,1)S(1)}, bf16[96,128]{1,0:T(8,128)(2,1)S(1)}, u32[]{:S(2)}, u32[]{:S(2)}) %collective-permute-start.13) | collective-permute-done | bytes 24608 | tf_op jit(solution)/shard_map/ppermute | solution.py:405
  54.8 0.6 collective-permute-done.15.rest_2_
  55.4 0.0 collective-permute-start.16
  55.4 1.2 collective-permute-done.17.rest_3_
  56.7 0.0 collective-permute-start.18
  56.7 66.6 %backward_own.1 = (f32[96,128]{1,0:T(8,128)S(1)}, f32[96,128]{1,0:T(8,128)S(1)}, f32[96,128]{1,0:T(8,128)S(1)}, f32[96,128]{1,0:T(8,128)S(1)}) custom-call(s32[11]{0:T(128)S(1)} %concatenate.3.meta_ref, f32[384]{0:T(512)S(1)} %copy-done.6, bf16[1,6,12,48,48,128]{5,4,3,2,1,0:T(8,128)(2,1)} %f_ref.5, bf16[1,6,12,2304]{3,2,1,0:T(8,128)(2,1)S(1)} %copy-done.4, ...), custom_call_target="tpu_custom_call" | custom-call | flops 28991029248 | bytes 28311552 | tf_op jit(solution)/shard_map/backward_own/pallas_call | solution.py:547
  123.4 5.7 %copy-done.12 = bf16[7,4,48,48,128]{4,3,2,1,0:T(8,128)(2,1)} copy-done((bf16[7,4,48,48,128]{4,3,2,1,0:T(8,128)(2,1)}, bf16[7,4,48,48,128]{4,3,2,1,0:T(8,128)(2,1)S(1)}, u32[]{:S(2)}) %copy-start.12) | copy-done | bytes 16515096
  129.0 8.4 %backward_shared.1 = (f32[144,128]{1,0:T(8,128)S(1)}, f32[144,128]{1,0:T(8,128)S(1)}, f32[144,128]{1,0:T(8,128)S(1)}, f32[144,128]{1,0:T(8,128)S(1)}) custom-call(s32[11]{0:T(128)S(1)} %concatenate.3.meta_ref, f32[384]{0:T(512)S(1)} %copy-done.6, bf16[7,4,48,48,128]{4,3,2,1,0:T(8,128)(2,1)} %copy-done.12, ...), custom_call_target="tpu_custom_call" | custom-call | flops 21743271936 | bytes 21233664 | tf_op jit(solution)/shard_map/backward_shared/pallas_call | solution.py:547
  137.4 0.7 collective-permute-start.19
  138.2 1.9 %collective-permute-start.20 = (f32[144,128]{1,0:T(8,128)S(1)}, f32[144,128]{1,0:T(8,128)S(1)}, u32[]{:S(2)}, u32[]{:S(2)}) collective-permute-start(f32[144,128]{1,0:T(8,128)S(1)} %get-tuple-element.40), channel_id=1, source_target_pairs={{0,2},{1,3},{2,0},{3,1},{4,6},{5,7},{6,4},{7,5},{8,10},{9,11},{10,... | collective-permute-start | bytes 221192 | tf_op jit(solution)/shard_map/ppermute | solution.py:405
  140.1 1.7 %collective-permute-start.21 = (f32[144,128]{1,0:T(8,128)S(1)}, f32[144,128]{1,0:T(8,128)S(1)}, u32[]{:S(2)}, u32[]{:S(2)}) collective-permute-start(f32[144,128]{1,0:T(8,128)S(1)} %get-tuple-element.41), channel_id=1, source_target_pairs={{0,3},{1,0},{2,1},{3,2},{4,7},{5,4},{6,5},{7,6},{8,11},{9,8},{10,9... | collective-permute-start | bytes 221192 | tf_op jit(solution)/shard_map/ppermute | solution.py:405
  141.8 1.9 %collective-permute-done.19.refs_1_ = f32[144,128]{1,0:T(8,128)S(1)} collective-permute-done((f32[144,128]{1,0:T(8,128)S(1)}, f32[144,128]{1,0:T(8,128)S(1)}, u32[]{:S(2)}, u32[]{:S(2)}) %collective-permute-start.19) | collective-permute-done | bytes 73760 | tf_op jit(solution)/shard_map/ppermute | solution.py:405
  143.8 1.2 collective-permute-done.20.refs_2_
  145.0 0.1 collective-permute-start.22
  145.1 0.1 collective-permute-start.23
  145.2 0.1 collective-permute-start.3
  145.2 0.1 collective-permute-start.4
  145.3 4.2 %collective-permute-start.24 = (f32[144,128]{1,0:T(8,128)S(1)}, f32[144,128]{1,0:T(8,128)S(1)}, u32[]{:S(2)}, u32[]{:S(2)}) collective-permute-start(f32[144,128]{1,0:T(8,128)S(1)} %sum_shards.1.refs_8_.refs_0_), channel_id=1, source_target_pairs={{0,12},{4,16},{8,20},{12,24},{16,28},{20,0},{24,4},{28,8},{1,13},{... | collective-permute-start | bytes 221192 | tf_op jit(solution)/shard_map/ppermute | solution.py:405
  149.5 2.6 %collective-permute-done.3.refs_1_ = bf16[96,128]{1,0:T(8,128)(2,1)S(1)} collective-permute-done((bf16[96,128]{1,0:T(8,128)(2,1)S(1)}, bf16[96,128]{1,0:T(8,128)(2,1)S(1)}, u32[]{:S(2)}, u32[]{:S(2)}) %collective-permute-start.3) | collective-permute-done | bytes 24608 | tf_op jit(solution)/shard_map/ppermute | solution.py:405
  152.2 0.9 collective-permute-start.27
  153.1 2.3 %collective-permute-start.28 = (f32[144,128]{1,0:T(8,128)S(1)}, f32[144,128]{1,0:T(8,128)S(1)}, u32[]{:S(2)}, u32[]{:S(2)}) collective-permute-start(f32[144,128]{1,0:T(8,128)S(1)} %sum_shards.1.refs_8_.refs_0_), channel_id=1, source_target_pairs={{0,28},{4,0},{8,4},{12,8},{16,12},{20,16},{24,20},{28,24},{1,29},{... | collective-permute-start | bytes 221192 | tf_op jit(solution)/shard_map/ppermute | solution.py:405
  155.5 1.1 collective-permute-done.25.refs_12_.refs_4_
  156.5 0.0 collective-permute-start.6
  156.5 0.7 collective-permute-start.7
  157.3 0.1 collective-permute-done.27.refs_14_.refs_6_
  157.3 2.7 %collective-permute-start.8 = (bf16[96,128]{1,0:T(8,128)(2,1)S(1)}, bf16[96,128]{1,0:T(8,128)(2,1)S(1)}, u32[]{:S(2)}, u32[]{:S(2)}) collective-permute-start(bf16[96,128]{1,0:T(8,128)(2,1)S(1)} %get-tuple-element.30.refs_0_), channel_id=1, source_target_pairs={{0,24},{4,28},{8,0},{12,4},{16,8},{20,12},{24,16},{28,20},{1,25},{... | collective-permute-start | bytes 73736 | tf_op jit(solution)/shard_map/ppermute | solution.py:405
  160.1 1.0 collective-permute-start.9
  161.1 1.4 collective-permute-start.29
  162.5 2.2 %collective-permute-start.30 = (f32[32,128]{1,0:T(8,128)S(1)}, f32[32,128]{1,0:T(8,128)S(1)}, u32[]{:S(2)}, u32[]{:S(2)}) collective-permute-start(f32[32,128]{1,0:T(8,128)S(1)} %sum_local.1.refs_0_), channel_id=1, source_target_pairs={{0,2},{1,3},{2,0},{3,1},{4,6},{5,7},{6,4},{7,5},{8,10},{9,11},{10,... | collective-permute-start | bytes 49160 | tf_op jit(solution)/shard_map/ppermute | solution.py:405
  164.7 0.4 collective-permute-start.31
  165.0 1.6 weight_grad.1
  166.6 0.3 collective-permute-done.29.refs_1_
  166.9 0.4 collective-permute-done.30.refs_2_
  167.2 1.2 collective-permute-done.31.refs_3_
  168.4 0.6 place_local.1
  (38 shorter events, 0.1 us)
Async XLA Ops:
  5.8 0.9 copy-start
  6.7 1.0 copy-start.3
  7.7 0.7 copy-start.5
  26.9 96.4 %collective-permute-start.10 = (bf16[7,4,48,48,128]{4,3,2,1,0:T(8,128)(2,1)}, bf16[7,4,48,48,128]{4,3,2,1,0:T(8,128)(2,1)S(1)}, u32[]{:S(2)}, u32[]{:S(2)}) collective-permute-start(bf16[7,4,48,48,128]{4,3,2,1,0:T(8,128)(2,1)} %get-tuple-element.31), channel_id=1, source_target_pairs={{0,4},{4,0},{8,12},{12,8},{16,20},{20,16},{24,28},{28,24},{1,5},{5... | collective-permute-start | bytes 49545224 | tf_op jit(solution)/shard_map/ppermute | solution.py:480
  26.9 21.8 %copy-start.2 = (bf16[8,2,128,128]{3,2,1,0:T(8,128)(2,1)S(1)}, bf16[8,2,128,128]{3,2,1,0:T(8,128)(2,1)}, u32[]{:S(2)}) copy-start(bf16[8,2,128,128]{3,2,1,0:T(8,128)(2,1)} %refs_4_.1) | copy-start | bytes 1572868
  26.9 29.7 %copy-start.1 = (bf16[32,2304]{1,0:T(8,128)(2,1)S(1)}, bf16[32,2304]{1,0:T(8,128)(2,1)}, u32[]{:S(2)}) copy-start(bf16[32,2304]{1,0:T(8,128)(2,1)} %constant.28.clone.basis_ref.rest_7_) | copy-start | bytes 442372
  27.0 29.7 %copy-start.4 = (bf16[1,6,12,2304]{3,2,1,0:T(8,128)(2,1)S(1)}, bf16[1,6,12,2304]{3,2,1,0:T(8,128)(2,1)}, u32[]{:S(2)}) copy-start(bf16[1,6,12,2304]{3,2,1,0:T(8,128)(2,1)} %t_ref.1) | copy-start | bytes 995332
  27.0 29.7 %copy-start.6 = (f32[384]{0:T(512)S(1)}, f32[384]{0:T(512)}, u32[]{:S(2)}) copy-start(f32[384]{0:T(512)} %constant.27.clone.xtab_ref) | copy-start | bytes 4612
  27.0 29.7 %copy-start.7 = (bf16[128,128]{1,0:T(8,128)(2,1)S(1)}, bf16[128,128]{1,0:T(8,128)(2,1)}, u32[]{:S(2)}) copy-start(bf16[128,128]{1,0:T(8,128)(2,1)} %rest_4_.3) | copy-start | bytes 98308
  27.0 29.7 %copy-start.8 = (f32[128]{0:T(128)S(1)}, f32[128]{0:T(128)}, u32[]{:S(2)}) copy-start(f32[128]{0:T(128)} %param.18) | copy-start | bytes 1540
  27.0 29.7 %copy-start.9 = (bf16[2304,128]{1,0:T(8,128)(2,1)S(1)}, bf16[2304,128]{1,0:T(8,128)(2,1)}, u32[]{:S(2)}) copy-start(bf16[2304,128]{1,0:T(8,128)(2,1)} %constant.29.clone.rest_6_) | copy-start | bytes 1769476
  27.0 29.7 %copy-start.10 = (bf16[256,128]{1,0:T(8,128)(2,1)S(1)}, bf16[256,128]{1,0:T(8,128)(2,1)}, u32[]{:S(2)}) copy-start(bf16[256,128]{1,0:T(8,128)(2,1)} %constant.31.clone.rest_9_) | copy-start | bytes 196612
  27.0 29.7 %copy-start.11 = (bf16[128,128]{1,0:T(8,128)(2,1)S(1)}, bf16[128,128]{1,0:T(8,128)(2,1)}, u32[]{:S(2)}) copy-start(bf16[128,128]{1,0:T(8,128)(2,1)} %constant.30.clone.rest_8_) | copy-start | bytes 98308
  39.0 7.2 %collective-permute-start = (f32[96,128]{1,0:T(8,128)S(1)}, f32[96,128]{1,0:T(8,128)S(1)}, u32[]{:S(2)}, u32[]{:S(2)}) collective-permute-start(f32[96,128]{1,0:T(8,128)S(1)} %get-tuple-element.27), channel_id=1, source_target_pairs={{0,1},{1,2},{2,3},{3,0},{4,5},{5,6},{6,7},{7,4},{8,9},{9,10},{10,1... | collective-permute-start | bytes 147464 | tf_op jit(solution)/shard_map/ppermute | solution.py:405
  42.0 5.0 %collective-permute-start.1 = (f32[96,128]{1,0:T(8,128)S(1)}, f32[96,128]{1,0:T(8,128)S(1)}, u32[]{:S(2)}, u32[]{:S(2)}) collective-permute-start(f32[96,128]{1,0:T(8,128)S(1)} %get-tuple-element.28), channel_id=1, source_target_pairs={{0,2},{1,3},{2,0},{3,1},{4,6},{5,7},{6,4},{7,5},{8,10},{9,11},{10,... | collective-permute-start | bytes 147464 | tf_op jit(solution)/shard_map/ppermute | solution.py:405
  44.6 4.1 %collective-permute-start.2 = (f32[96,128]{1,0:T(8,128)S(1)}, f32[96,128]{1,0:T(8,128)S(1)}, u32[]{:S(2)}, u32[]{:S(2)}) collective-permute-start(f32[96,128]{1,0:T(8,128)S(1)} %get-tuple-element.29), channel_id=1, source_target_pairs={{0,3},{1,0},{2,1},{3,2},{4,7},{5,4},{6,5},{7,6},{8,11},{9,8},{10,9... | collective-permute-start | bytes 147464 | tf_op jit(solution)/shard_map/ppermute | solution.py:405
  49.0 4.0 %collective-permute-start.12 = (bf16[96,128]{1,0:T(8,128)(2,1)S(1)}, bf16[96,128]{1,0:T(8,128)(2,1)S(1)}, u32[]{:S(2)}, u32[]{:S(2)}) collective-permute-start(bf16[96,128]{1,0:T(8,128)(2,1)S(1)} %get-tuple-element.33.rest_0_), channel_id=1, source_target_pairs={{0,4},{4,0},{8,12},{12,8},{16,20},{20,16},{24,28},{28,24},{1,5},{5... | collective-permute-start | bytes 73736 | tf_op jit(solution)/shard_map/ppermute | solution.py:480
  49.1 5.8 %collective-permute-start.13 = (bf16[96,128]{1,0:T(8,128)(2,1)S(1)}, bf16[96,128]{1,0:T(8,128)(2,1)S(1)}, u32[]{:S(2)}, u32[]{:S(2)}) collective-permute-start(bf16[96,128]{1,0:T(8,128)(2,1)S(1)} %get-tuple-element.33.rest_0_), channel_id=1, source_target_pairs={{0,1},{1,2},{2,3},{3,0},{4,5},{5,6},{6,7},{7,4},{8,9},{9,10},{10,1... | collective-permute-start | bytes 73736 | tf_op jit(solution)/shard_map/ppermute | solution.py:405
  49.5 5.9 %collective-permute-start.15 = (bf16[96,128]{1,0:T(8,128)(2,1)S(1)}, bf16[96,128]{1,0:T(8,128)(2,1)S(1)}, u32[]{:S(2)}, u32[]{:S(2)}) collective-permute-start(bf16[96,128]{1,0:T(8,128)(2,1)S(1)} %get-tuple-element.33.rest_0_), channel_id=1, source_target_pairs={{0,2},{1,3},{2,0},{3,1},{4,6},{5,7},{6,4},{7,5},{8,10},{9,11},{10,... | collective-permute-start | bytes 73736 | tf_op jit(solution)/shard_map/ppermute | solution.py:405
  52.8 3.8 %collective-permute-start.17 = (bf16[96,128]{1,0:T(8,128)(2,1)S(1)}, bf16[96,128]{1,0:T(8,128)(2,1)S(1)}, u32[]{:S(2)}, u32[]{:S(2)}) collective-permute-start(bf16[96,128]{1,0:T(8,128)(2,1)S(1)} %get-tuple-element.33.rest_0_), channel_id=1, source_target_pairs={{0,3},{1,0},{2,1},{3,2},{4,7},{5,4},{6,5},{7,6},{8,11},{9,8},{10,9... | collective-permute-start | bytes 73736 | tf_op jit(solution)/shard_map/ppermute | solution.py:405
  52.9 70.4 %collective-permute-start.11 = (bf16[3,12,2304]{2,1,0:T(8,128)(2,1)S(1)}, bf16[3,12,2304]{2,1,0:T(8,128)(2,1)S(1)}, u32[]{:S(2)}, u32[]{:S(2)}) collective-permute-start(bf16[3,12,2304]{2,1,0:T(8,128)(2,1)S(1)} %get-tuple-element.32), channel_id=1, source_target_pairs={{0,4},{4,0},{8,12},{12,8},{16,20},{20,16},{24,28},{28,24},{1,5},{5... | collective-permute-start | bytes 497672 | tf_op jit(solution)/shard_map/ppermute | solution.py:480
  54.8 68.5 %collective-permute-start.14 = (bf16[96,128]{1,0:T(8,128)(2,1)S(1)}, bf16[96,128]{1,0:T(8,128)(2,1)S(1)}, u32[]{:S(2)}, u32[]{:S(2)}) collective-permute-start(bf16[96,128]{1,0:T(8,128)(2,1)S(1)} %collective-permute-done.13.rest_1_), channel_id=1, source_target_pairs={{0,4},{4,0},{8,12},{12,8},{16,20},{20,16},{24,28},{28,24},{1,5},{5... | collective-permute-start | bytes 73736 | tf_op jit(solution)/shard_map/ppermute | solution.py:480
  55.4 67.9 %collective-permute-start.16 = (bf16[96,128]{1,0:T(8,128)(2,1)S(1)}, bf16[96,128]{1,0:T(8,128)(2,1)S(1)}, u32[]{:S(2)}, u32[]{:S(2)}) collective-permute-start(bf16[96,128]{1,0:T(8,128)(2,1)S(1)} %collective-permute-done.15.rest_2_), channel_id=1, source_target_pairs={{0,4},{4,0},{8,12},{12,8},{16,20},{20,16},{24,28},{28,24},{1,5},{5... | collective-permute-start | bytes 73736 | tf_op jit(solution)/shard_map/ppermute | solution.py:480
  56.7 66.7 %collective-permute-start.18 = (bf16[96,128]{1,0:T(8,128)(2,1)S(1)}, bf16[96,128]{1,0:T(8,128)(2,1)S(1)}, u32[]{:S(2)}, u32[]{:S(2)}) collective-permute-start(bf16[96,128]{1,0:T(8,128)(2,1)S(1)} %collective-permute-done.17.rest_3_), channel_id=1, source_target_pairs={{0,4},{4,0},{8,12},{12,8},{16,20},{20,16},{24,28},{28,24},{1,5},{5... | collective-permute-start | bytes 73736 | tf_op jit(solution)/shard_map/ppermute | solution.py:480
  123.4 5.7 %copy-start.12 = (bf16[7,4,48,48,128]{4,3,2,1,0:T(8,128)(2,1)}, bf16[7,4,48,48,128]{4,3,2,1,0:T(8,128)(2,1)S(1)}, u32[]{:S(2)}) copy-start(bf16[7,4,48,48,128]{4,3,2,1,0:T(8,128)(2,1)S(1)} %collective-permute-done.10.f_ref) | copy-start | bytes 49545220
  137.4 6.3 %collective-permute-start.19 = (f32[144,128]{1,0:T(8,128)S(1)}, f32[144,128]{1,0:T(8,128)S(1)}, u32[]{:S(2)}, u32[]{:S(2)}) collective-permute-start(f32[144,128]{1,0:T(8,128)S(1)} %get-tuple-element.39), channel_id=1, source_target_pairs={{0,1},{1,2},{2,3},{3,0},{4,5},{5,6},{6,7},{7,4},{8,9},{9,10},{10,1... | collective-permute-start | bytes 221192 | tf_op jit(solution)/shard_map/ppermute | solution.py:405
  138.2 6.8 %collective-permute-start.20 = (f32[144,128]{1,0:T(8,128)S(1)}, f32[144,128]{1,0:T(8,128)S(1)}, u32[]{:S(2)}, u32[]{:S(2)}) collective-permute-start(f32[144,128]{1,0:T(8,128)S(1)} %get-tuple-element.40), channel_id=1, source_target_pairs={{0,2},{1,3},{2,0},{3,1},{4,6},{5,7},{6,4},{7,5},{8,10},{9,11},{10,... | collective-permute-start | bytes 221192 | tf_op jit(solution)/shard_map/ppermute | solution.py:405
  140.1 4.9 %collective-permute-start.21 = (f32[144,128]{1,0:T(8,128)S(1)}, f32[144,128]{1,0:T(8,128)S(1)}, u32[]{:S(2)}, u32[]{:S(2)}) collective-permute-start(f32[144,128]{1,0:T(8,128)S(1)} %get-tuple-element.41), channel_id=1, source_target_pairs={{0,3},{1,0},{2,1},{3,2},{4,7},{5,4},{6,5},{7,6},{8,11},{9,8},{10,9... | collective-permute-start | bytes 221192 | tf_op jit(solution)/shard_map/ppermute | solution.py:405
  145.0 7.2 %collective-permute-start.22 = (f32[144,128]{1,0:T(8,128)S(1)}, f32[144,128]{1,0:T(8,128)S(1)}, u32[]{:S(2)}, u32[]{:S(2)}) collective-permute-start(f32[144,128]{1,0:T(8,128)S(1)} %sum_shards.1.refs_8_.refs_0_), channel_id=1, source_target_pairs={{0,4},{4,8},{8,12},{12,16},{16,20},{20,24},{24,28},{28,0},{1,5},{5... | collective-permute-start | bytes 221192 | tf_op jit(solution)/shard_map/ppermute | solution.py:405
  145.1 8.0 %collective-permute-start.23 = (f32[144,128]{1,0:T(8,128)S(1)}, f32[144,128]{1,0:T(8,128)S(1)}, u32[]{:S(2)}, u32[]{:S(2)}) collective-permute-start(f32[144,128]{1,0:T(8,128)S(1)} %sum_shards.1.refs_8_.refs_0_), channel_id=1, source_target_pairs={{0,8},{4,12},{8,16},{12,20},{16,24},{20,28},{24,0},{28,4},{1,9},{5... | collective-permute-start | bytes 221192 | tf_op jit(solution)/shard_map/ppermute | solution.py:405
  145.2 7.0 %collective-permute-start.3 = (bf16[96,128]{1,0:T(8,128)(2,1)S(1)}, bf16[96,128]{1,0:T(8,128)(2,1)S(1)}, u32[]{:S(2)}, u32[]{:S(2)}) collective-permute-start(bf16[96,128]{1,0:T(8,128)(2,1)S(1)} %get-tuple-element.30.refs_0_), channel_id=1, source_target_pairs={{0,4},{4,8},{8,12},{12,16},{16,20},{20,24},{24,28},{28,0},{1,5},{5... | collective-permute-start | bytes 73736 | tf_op jit(solution)/shard_map/ppermute | solution.py:405
  145.2 6.9 %collective-permute-start.4 = (bf16[96,128]{1,0:T(8,128)(2,1)S(1)}, bf16[96,128]{1,0:T(8,128)(2,1)S(1)}, u32[]{:S(2)}, u32[]{:S(2)}) collective-permute-start(bf16[96,128]{1,0:T(8,128)(2,1)S(1)} %get-tuple-element.30.refs_0_), channel_id=1, source_target_pairs={{0,8},{4,12},{8,16},{12,20},{16,24},{20,28},{24,0},{28,4},{1,9},{5... | collective-permute-start | bytes 73736 | tf_op jit(solution)/shard_map/ppermute | solution.py:405
  145.3 10.2 %collective-permute-start.24 = (f32[144,128]{1,0:T(8,128)S(1)}, f32[144,128]{1,0:T(8,128)S(1)}, u32[]{:S(2)}, u32[]{:S(2)}) collective-permute-start(f32[144,128]{1,0:T(8,128)S(1)} %sum_shards.1.refs_8_.refs_0_), channel_id=1, source_target_pairs={{0,12},{4,16},{8,20},{12,24},{16,28},{20,0},{24,4},{28,8},{1,13},{... | collective-permute-start | bytes 221192 | tf_op jit(solution)/shard_map/ppermute | solution.py:405
  152.2 4.4 %collective-permute-start.25 = (f32[144,128]{1,0:T(8,128)S(1)}, f32[144,128]{1,0:T(8,128)S(1)}, u32[]{:S(2)}, u32[]{:S(2)}) collective-permute-start(f32[144,128]{1,0:T(8,128)S(1)} %sum_shards.1.refs_8_.refs_0_), channel_id=1, source_target_pairs={{0,16},{4,20},{8,24},{12,28},{16,0},{20,4},{24,8},{28,12},{1,17},{... | collective-permute-start | bytes 221192 | tf_op jit(solution)/shard_map/ppermute | solution.py:405
  152.2 4.4 %collective-permute-start.26 = (f32[144,128]{1,0:T(8,128)S(1)}, f32[144,128]{1,0:T(8,128)S(1)}, u32[]{:S(2)}, u32[]{:S(2)}) collective-permute-start(f32[144,128]{1,0:T(8,128)S(1)} %sum_shards.1.refs_8_.refs_0_), channel_id=1, source_target_pairs={{0,20},{4,24},{8,28},{12,0},{16,4},{20,8},{24,12},{28,16},{1,21},{... | collective-permute-start | bytes 221192 | tf_op jit(solution)/shard_map/ppermute | solution.py:405
  152.2 5.1 %collective-permute-start.27 = (f32[144,128]{1,0:T(8,128)S(1)}, f32[144,128]{1,0:T(8,128)S(1)}, u32[]{:S(2)}, u32[]{:S(2)}) collective-permute-start(f32[144,128]{1,0:T(8,128)S(1)} %sum_shards.1.refs_8_.refs_0_), channel_id=1, source_target_pairs={{0,24},{4,28},{8,0},{12,4},{16,8},{20,12},{24,16},{28,20},{1,25},{... | collective-permute-start | bytes 221192 | tf_op jit(solution)/shard_map/ppermute | solution.py:405
  153.1 6.9 %collective-permute-start.28 = (f32[144,128]{1,0:T(8,128)S(1)}, f32[144,128]{1,0:T(8,128)S(1)}, u32[]{:S(2)}, u32[]{:S(2)}) collective-permute-start(f32[144,128]{1,0:T(8,128)S(1)} %sum_shards.1.refs_8_.refs_0_), channel_id=1, source_target_pairs={{0,28},{4,0},{8,4},{12,8},{16,12},{20,16},{24,20},{28,24},{1,29},{... | collective-permute-start | bytes 221192 | tf_op jit(solution)/shard_map/ppermute | solution.py:405
  155.5 5.6 %collective-permute-start.5 = (bf16[96,128]{1,0:T(8,128)(2,1)S(1)}, bf16[96,128]{1,0:T(8,128)(2,1)S(1)}, u32[]{:S(2)}, u32[]{:S(2)}) collective-permute-start(bf16[96,128]{1,0:T(8,128)(2,1)S(1)} %get-tuple-element.30.refs_0_), channel_id=1, source_target_pairs={{0,12},{4,16},{8,20},{12,24},{16,28},{20,0},{24,4},{28,8},{1,13},{... | collective-permute-start | bytes 73736 | tf_op jit(solution)/shard_map/ppermute | solution.py:405
  156.5 5.9 %collective-permute-start.6 = (bf16[96,128]{1,0:T(8,128)(2,1)S(1)}, bf16[96,128]{1,0:T(8,128)(2,1)S(1)}, u32[]{:S(2)}, u32[]{:S(2)}) collective-permute-start(bf16[96,128]{1,0:T(8,128)(2,1)S(1)} %get-tuple-element.30.refs_0_), channel_id=1, source_target_pairs={{0,16},{4,20},{8,24},{12,28},{16,0},{20,4},{24,8},{28,12},{1,17},{... | collective-permute-start | bytes 73736 | tf_op jit(solution)/shard_map/ppermute | solution.py:405
  156.5 8.1 %collective-permute-start.7 = (bf16[96,128]{1,0:T(8,128)(2,1)S(1)}, bf16[96,128]{1,0:T(8,128)(2,1)S(1)}, u32[]{:S(2)}, u32[]{:S(2)}) collective-permute-start(bf16[96,128]{1,0:T(8,128)(2,1)S(1)} %get-tuple-element.30.refs_0_), channel_id=1, source_target_pairs={{0,20},{4,24},{8,28},{12,0},{16,4},{20,8},{24,12},{28,16},{1,21},{... | collective-permute-start | bytes 73736 | tf_op jit(solution)/shard_map/ppermute | solution.py:405
  157.3 7.7 %collective-permute-start.8 = (bf16[96,128]{1,0:T(8,128)(2,1)S(1)}, bf16[96,128]{1,0:T(8,128)(2,1)S(1)}, u32[]{:S(2)}, u32[]{:S(2)}) collective-permute-start(bf16[96,128]{1,0:T(8,128)(2,1)S(1)} %get-tuple-element.30.refs_0_), channel_id=1, source_target_pairs={{0,24},{4,28},{8,0},{12,4},{16,8},{20,12},{24,16},{28,20},{1,25},{... | collective-permute-start | bytes 73736 | tf_op jit(solution)/shard_map/ppermute | solution.py:405
  160.1 4.9 %collective-permute-start.9 = (bf16[96,128]{1,0:T(8,128)(2,1)S(1)}, bf16[96,128]{1,0:T(8,128)(2,1)S(1)}, u32[]{:S(2)}, u32[]{:S(2)}) collective-permute-start(bf16[96,128]{1,0:T(8,128)(2,1)S(1)} %get-tuple-element.30.refs_0_), channel_id=1, source_target_pairs={{0,28},{4,0},{8,4},{12,8},{16,12},{20,16},{24,20},{28,24},{1,29},{... | collective-permute-start | bytes 73736 | tf_op jit(solution)/shard_map/ppermute | solution.py:405
  161.1 5.8 %collective-permute-start.29 = (f32[32,128]{1,0:T(8,128)S(1)}, f32[32,128]{1,0:T(8,128)S(1)}, u32[]{:S(2)}, u32[]{:S(2)}) collective-permute-start(f32[32,128]{1,0:T(8,128)S(1)} %sum_local.1.refs_0_), channel_id=1, source_target_pairs={{0,1},{1,2},{2,3},{3,0},{4,5},{5,6},{6,7},{7,4},{8,9},{9,10},{10,1... | collective-permute-start | bytes 49160 | tf_op jit(solution)/shard_map/ppermute | solution.py:405
  162.5 4.7 %collective-permute-start.30 = (f32[32,128]{1,0:T(8,128)S(1)}, f32[32,128]{1,0:T(8,128)S(1)}, u32[]{:S(2)}, u32[]{:S(2)}) collective-permute-start(f32[32,128]{1,0:T(8,128)S(1)} %sum_local.1.refs_0_), channel_id=1, source_target_pairs={{0,2},{1,3},{2,0},{3,1},{4,6},{5,7},{6,4},{7,5},{8,10},{9,11},{10,... | collective-permute-start | bytes 49160 | tf_op jit(solution)/shard_map/ppermute | solution.py:405
  164.7 3.7 %collective-permute-start.31 = (f32[32,128]{1,0:T(8,128)S(1)}, f32[32,128]{1,0:T(8,128)S(1)}, u32[]{:S(2)}, u32[]{:S(2)}) collective-permute-start(f32[32,128]{1,0:T(8,128)S(1)} %sum_local.1.refs_0_), channel_id=1, source_target_pairs={{0,3},{1,0},{2,1},{3,2},{4,7},{5,4},{6,5},{7,6},{8,11},{9,8},{10,9... | collective-permute-start | bytes 49160 | tf_op jit(solution)/shard_map/ppermute | solution.py:405
